TPU v7x, 512 devices: a whole 4x8x8 slice. The times are simulated.
512 devices in a mesh: prow: 32 (over y, x), pcol: 16 (over z, core).
Axes of the slice: x: 4, y: 8, z: 8, core: 2. Of those that a mesh axis runs over, the one named last changes fastest.
Arguments:
- trailing: float32 [40960, 8192], P('prow', 'pcol'), may hold values from -6 to 6
- l_panel: float32 [40960, 512], P('prow', 'pcol'), as said below
- pivots: int32 [512], replicated, may hold values from 512 to 40959, as said below
Outputs:
- updated: float32 [40960, 8192], P('prow', 'pcol')
Inputs may be any that keep to these rules, and one draw needn't show every extreme that they name: `pivots`: all pivot rows are different and lie below the first 512 rows; at most 32 of them lie among the 1280 rows of one prow index, and exactly 32 among those of one prow index in every draw. `l_panel`: rows below the first 512 are dense; the first 512 rows are zero on and above the diagonal.
All inputs are finite; a program needn't handle non-finite values.
Results may differ from a plain program's by a relative error of at most 0.000059.
Values sent between devices are 32-bit elements; how exact they have to be, the bound alone decides.
No kernel may reach another device: no remote copies, remote signals or barrier semaphores. Data moves between devices by JAX's collectives and lax.ppermute only.
A program may use at most 64 MiB of HBM per device.

v0:
```python
import jax
import jax.numpy as jnp
from jax import lax
from jax.sharding import PartitionSpec as P


def from_root(shard, axis, root):
    mine = lax.axis_index(axis) == root
    return lax.psum(jnp.where(mine, shard, jnp.zeros_like(shard)), axis)


def solve_block(diag_rows, rhs):
    return jax.scipy.linalg.solve_triangular(diag_rows, rhs, lower=True, unit_diagonal=True)


def on_device(trailing, l_panel, pivots):
    rows_here, cols_here = trailing.shape
    block = pivots.shape[0]
    prow_index = lax.axis_index("prow")
    owner = pivots // rows_here
    local = pivots % rows_here
    mine = owner == prow_index
    l_full = lax.all_gather(l_panel, "pcol", axis=1, tiled=True)
    top_orig, diag_rows = (
        from_root(trailing[:block], "prow", 0),
        from_root(l_full[:block], "prow", 0),
    )
    swapped = trailing.at[jnp.where(mine, local, rows_here)].set(top_orig, mode="drop")
    picked = jnp.where(mine[:, None], trailing[jnp.where(mine, local, 0)], 0.0)
    chosen = lax.psum(picked, "prow")
    upper = solve_block(diag_rows, chosen)
    lowered = swapped - jnp.dot(l_full, upper, precision=lax.Precision.HIGHEST)
    global_rows = prow_index * rows_here + jnp.arange(rows_here)
    upper_padded = jnp.concatenate(
        [upper, jnp.zeros((rows_here - block, cols_here), jnp.float32)], axis=0
    )
    return jnp.where(global_rows[:, None] < block, upper_padded, lowered)


def solution(mesh):
    placed = (P("prow", "pcol"), P("prow", "pcol"), P())
    return jax.shard_map(
        on_device, mesh=mesh, in_specs=placed, out_specs=P("prow", "pcol"), check_vma=False
    )
```

profile of v0, /device:TPU:1, one launch (start us, length us, event | category | flops | bytes accessed | tf_op | source)
XLA Modules:
  0.0 324.9 jit_solution(11304377484049614199)
XLA Ops:
  6.5 1.8 copy.36
  8.4 2.3 gather_fusion
  10.8 2.3 broadcast_select_fusion
  13.1 46.1 %all-gather.2.cloned.1.call-done = f32[1280,512]{0,1:T(8,128)} async-done(((f32[1280,32]{0,1:T(8,128)}), f32[1280,512]{0,1:T(8,128)}) %all-gather.2.cloned.1.call-update) | async-done | bytes 2621456 | tf_op jit(solution)/shard_map/all_gather | solution.py:23
  59.2 2.3 slice.54
  61.5 2.5 copy.18
  64.1 2.8 slice_select_fusion
  66.9 161.8 %all-reduce.3.cloned.1.call-done = (f32[512,512]{1,0:T(8,128)}, f32[512,512]{1,0:T(8,128)}, f32[512,512]{1,0:T(8,128)}) async-done(((f32[512,512]{1,0:T(8,128)}, f32[512,512]{1,0:T(8,128)}, f32[512,512]{1,0:T(8,128)}), (f32[512,512]{1,0:T(8,128)}, f32[512,512]{1,0:T(8,128)}, f32[512,512]{1,0:T(8,128)})) %all-reduce.3.cloned.1.call-update) | async-done | bytes 3145744 | tf_op jit(solution)/shard_map/psum | solution.py:30
  228.7 2.4 convert_add_fusion
  231.1 11.6 %while.1 = (s32[]{:T(128)}, f32[512,512]{1,0:T(8,128)}, s32[4,2]{0,1:T(2,128)S(1)}, f32[4,128,128]{2,1,0:T(8,128)S(1)}, s32[]{:T(128)}) while((s32[]{:T(128)}, f32[512,512]{1,0:T(8,128)}, s32[4,2]{0,1:T(2,128)S(1)}, f32[4,128,128]{2,1,0:T(8,128)S(1)}, s32[]{:T(128)}) %tuple.21), condition=%wide.while_cond, body=%wide.while_body.sunk | while | flops 2 | bytes 131189 | solution.py:13
  231.7 2.2 bitcast_dynamic-update-slice_fusion.2
  234.7 2.2 bitcast_dynamic-update-slice_fusion.2
  237.6 2.2 bitcast_dynamic-update-slice_fusion.2
  240.5 2.2 bitcast_dynamic-update-slice_fusion.2
  242.7 39.3 %custom-call.4 = f32[4,128,128]{1,2,0:T(8,128)S(1)} custom-call(f32[4,128,128]{2,1,0:T(8,128)S(1)} %get-tuple-element.12), custom_call_target="InvertDiagBlocksLowerTriangular" | custom-call | tf_op jit(solution)/shard_map/jit(_solve_triangular)/triangular_solve | solution.py:13
  282.0 1.5 fusion.17
  283.5 0.8 copy.12
  284.3 1.4 convolution_subtract_fusion.1
  287.0 1.4 convolution_subtract_fusion
  288.4 1.3 fusion.22
  289.7 2.4 convolution_subtract_fusion.2
  292.1 0.8 copy.14
  292.9 4.0 %scatter_fusion = f32[1280,512]{1,0:T(8,128)S(1)} fusion(f32[1280,512]{1,0:T(8,128)S(1)} %copy.36, s32[512]{0:T(512)S(1)} %get-tuple-element.24, f32[512,512]{1,0:T(8,128)} %get-tuple-element.23), kind=kCustom, calls=%fused_computation.1 | custom fusion | bytes 3147776 | tf_op jit(solution)/shard_map/scatter | solution.py:28
  297.0 2.1 copy.16
  299.1 2.2 fusion.21
  301.3 1.8 copy.15
  303.1 1.0 constant_dynamic-update-slice_fusion.3
  304.1 1.0 constant_dynamic-update-slice_fusion.2
  305.1 1.0 constant_dynamic-update-slice_fusion.1
  306.1 1.0 constant_dynamic-update-slice_fusion
  307.2 7.7 %fusion.1 = f32[1280,512]{0,1:T(8,128)} fusion(f32[1280,512]{0,1:T(8,128)S(1)} %broadcast_dynamic-update-slice_fusion, f32[1280,512]{0,1:T(8,128)S(1)} %copy-done, f32[1280,512]{0,1:T(8,128)} %all-gather.2.cloned.1.call-done, pred[1280]{0:T(1024)(128)(4,1)S(1)} %add_compare_fusion, f32[128,512]{1,0:T(8,128)S(1)} %copy-done.1, f32[128,512]{1,0:T(8,128)S(1)} %fusion.22, ...), kind=kOutput, calls=%fused_computation.6 | convolution fusion | flops 4028628992 | bytes 11535616 | tf_op jit(solution)/shard_map/dot_general | solution.py:32
  314.8 3.2 copy.17
  (31 shorter events, 4.2 us)
Async XLA Ops:
  6.5 1.8 copy-start.3
  6.5 52.7 %all-gather.2.cloned.1.call-start = ((), (), s32[]{:S(2)}) async-start(), calls=%async_computation | async-start | bytes 2785280 | tf_op jit(solution)/shard_map/all_gather | solution.py:23
  8.3 220.4 %all-reduce.3.cloned.1.call-start = ((), (), s32[]{:S(2)}) async-start(), calls=%async_computation.1 | async-start | bytes 6291456 | tf_op jit(solution)/shard_map/psum | solution.py:30
  282.0 4.9 %copy-start.2 = (f32[4,128,128]{1,2,0:T(8,128)}, f32[4,128,128]{1,2,0:T(8,128)S(1)}, u32[]{:S(2)}) copy-start(f32[4,128,128]{1,2,0:T(8,128)S(1)} %custom-call.4) | copy-start | bytes 786436
  299.1 8.1 %copy-start = (f32[1280,512]{0,1:T(8,128)S(1)}, f32[1280,512]{0,1:T(8,128)}, u32[]{:S(2)}) copy-start(f32[1280,512]{0,1:T(8,128)} %copy.16) | copy-start | bytes 7864324
  303.1 4.1 %copy-start.1 = (f32[128,512]{1,0:T(8,128)S(1)}, f32[128,512]{1,0:T(8,128)}, u32[]{:S(2)}) copy-start(f32[128,512]{1,0:T(8,128)} %fusion.21) | copy-start | bytes 786436
Sparse Core Ops, SparseCore 0:
  9.5 49.7 all-gather.1
  67.0 161.6 all-reduce.2
where the time goes:
time: 328 us; the launch traced here: 325 us
  waiting for transfers between devices  208 us (63%)
  other arithmetic  46.9 us (14%)
  local copies, waits for them, and re-layouts  38.1 us (12%)
  matrix products  18.3 us (6%)
  between operations  13.6 us (4%)
    psum x1, waiting for transfers between devices, on_device(): chosen = lax.psum(picked, 'prow')  162 us
    all_gather x1, waiting for transfers between devices, on_device(): l_full = lax.all_gather(l_panel, 'pcol', axis=1, tiled=True)  46.1 us
    another operation x4, other arithmetic, solve_block(): jax.scipy.linalg.solve_triangular(diag_rows, rhs, lower=True, unit_diagon...  41.7 us
    another operation x12, local copies, waits for them, and re-layouts  11.5 us
    another operation x7, matrix products, solve_block(): jax.scipy.linalg.solve_triangular(diag_rows, rhs, lower=True, unit_diagon...  10.6 us
    unnamed x14, local copies, waits for them, and re-layouts  8.23 us
    dot_general x1, matrix products, on_device(): lowered = swapped - jnp.dot(l_full, upper, precision=lax.Precision.HIGHEST)  7.69 us
  transfers between devices with their start and end apart: 2, of which 2 were waited for; matrix products, arithmetic and copies ran while one was open for 1% of the time, Pallas kernels for 0%

commit v1 on v0

v1 whole, which is shorter than its diff:
```python
import jax
import jax.numpy as jnp
from jax import lax
from jax.experimental import pallas as pl
from jax.experimental.pallas import tpu as pltpu
from jax.sharding import PartitionSpec as P

NX, NY = 4, 8
NPROW = NX * NY
CAP = 32
HI = lax.Precision.HIGHEST


def dot(a, b, dims=((1,), (0,)), precision=HI):
    return lax.dot_general(a, b, (dims, ((), ())), precision=precision, preferred_element_type=jnp.float32)


def split(a):
    hi = a.astype(jnp.bfloat16)
    lo = (a - hi.astype(jnp.float32)).astype(jnp.bfloat16)
    return hi, lo


def prep_kernel(lt_ref, hi_ref, lo_ref):
    hi, lo = split(lt_ref[...].T)
    hi_ref[...] = hi
    lo_ref[...] = lo


def prep(lt):
    k, rows = lt.shape
    tile = 256
    return pl.pallas_call(
        prep_kernel,
        grid=(rows // tile,),
        in_specs=[pl.BlockSpec((k, tile), lambda i: (0, i))],
        out_specs=[pl.BlockSpec((tile, k), lambda i: (i, 0))] * 2,
        out_shape=[jax.ShapeDtypeStruct((rows, k), jnp.bfloat16)] * 2,
        name="prep_l",
    )(lt)


def invert_upper(u_ref, m_ref):
    n = u_ref.shape[0]
    base = 128
    row = lax.broadcasted_iota(jnp.int32, (base, base), 0)
    col = lax.broadcasted_iota(jnp.int32, (base, base), 1)
    eye = jnp.where(row == col, 1.0, 0.0)
    blocks = [u_ref[pl.ds(b * base, base), pl.ds(b * base, base)] for b in range(n // base)]
    invs = [eye] * len(blocks)
    s = 1
    while s < base:
        mask = (row // (2 * s) == col // (2 * s)) & (row % (2 * s) < s) & (col % (2 * s) >= s)
        parts = [jnp.where(mask, u, 0.0) for u in blocks]
        if s == 1:
            invs = [m - q for m, q in zip(invs, parts)]
        else:
            half = [dot(m, q) for m, q in zip(invs, parts)]
            invs = [m - dot(h, m) for m, h in zip(invs, half)]
        s *= 2
    m_ref[...] = jnp.zeros_like(m_ref)
    for b, m in enumerate(invs):
        m_ref[pl.ds(b * base, base), pl.ds(b * base, base)] = m
    s = base
    while s < n:
        for b in range(0, n, 2 * s):
            up, dn = pl.ds(b, s), pl.ds(b + s, s)
            t = dot(m_ref[up, up], u_ref[up, dn])
            m_ref[up, dn] = -dot(t, m_ref[dn, dn])
        s *= 2


def update_kernel(rows_ref, first_ref, u_ref, chosen_ref, top_ref, hi_ref, lo_ref, trail_ref, out_ref, m_ref, x_ref):
    n = u_ref.shape[0]
    out_ref[...] = trail_ref[...]
    for r in range(CAP):
        row = rows_ref[r]

        @pl.when(row >= 0)
        def _(r=r, row=row):
            out_ref[pl.ds(row, 1), :] = top_ref[pl.ds(r, 1), :]

    invert_upper(u_ref, m_ref)
    x_ref[...] = dot(m_ref[...].T, chosen_ref[...])
    xhi, xlo = split(x_ref[...])
    tile = 256
    for i in range(out_ref.shape[0] // tile):
        here = pl.ds(i * tile, tile)
        hi, lo = hi_ref[here, :], lo_ref[here, :]
        acc = dot(hi, xhi, precision=None) + (dot(lo, xhi, precision=None) + dot(hi, xlo, precision=None))
        out_ref[here, :] = out_ref[here, :] - acc

    @pl.when(first_ref[0] == 1)
    def _():
        out_ref[pl.ds(0, n), :] = x_ref[...]


def update(rows, first, u, chosen, top, hi, lo, trailing):
    n = u.shape[0]
    smem = pl.BlockSpec(memory_space=pltpu.SMEM)
    vmem = pl.BlockSpec(memory_space=pltpu.VMEM)
    return pl.pallas_call(
        update_kernel,
        in_specs=[smem, smem] + [vmem] * 6,
        out_specs=vmem,
        out_shape=jax.ShapeDtypeStruct(trailing.shape, jnp.float32),
        scratch_shapes=[pltpu.VMEM((n, n), jnp.float32), pltpu.VMEM((n, trailing.shape[1]), jnp.float32)],
        compiler_params=pltpu.CompilerParams(vmem_limit_bytes=40 * 1024 * 1024),
        name="solve_update",
    )(rows, first, u, chosen, top, hi, lo, trailing)


def to_x(k):
    return [(0, k)]


def to_y(k):
    return [(x, NX * k + x) for x in range(NX)]


def on_device(trailing, l_panel, pivots):
    rows_here, cols_here = trailing.shape
    block = pivots.shape[0]
    p = lax.axis_index("prow")

    lt = l_panel.T
    lt_full = lax.all_gather(lt, "pcol", axis=0, tiled=True)

    slab = lt[:, :block]
    got = [lax.ppermute(slab, "prow", to_x(k)) for k in range(1, NX)]
    slab = jnp.where(p == 0, slab, sum(got))
    got = [lax.ppermute(slab, "prow", to_y(k)) for k in range(1, NY)]
    slab = jnp.where(p < NX, slab, sum(got))
    u = lax.all_gather(slab, "pcol", axis=0, tiled=True)

    owner = pivots // rows_here
    local = pivots % rows_here
    ks = jnp.arange(block, dtype=jnp.int32)
    before = (owner[None, :] == owner[:, None]) & (ks[None, :] < ks[:, None])
    slot = owner * CAP + jnp.sum(before.astype(jnp.int32), axis=1)
    mine = slot[None, :] == (p * CAP + jnp.arange(CAP, dtype=jnp.int32))[:, None]
    rows = jnp.sum(jnp.where(mine, local[None, :] + 1, 0), axis=1) - 1
    slots = jnp.arange(NPROW * CAP, dtype=jnp.int32)
    k_of = jnp.sum(jnp.where(slot[None, :] == slots[:, None], ks[None, :], 0), axis=1)

    picked = trailing.at[jnp.maximum(rows, 0)].get(mode="promise_in_bounds")
    sent = jnp.broadcast_to(picked[None], (NPROW, CAP, cols_here))
    every = lax.all_to_all(sent, "prow", 0, 0, tiled=True).reshape(NPROW * CAP, cols_here)
    chosen = every.at[slot].get(mode="promise_in_bounds")

    tops = trailing[:block].at[k_of].get(mode="promise_in_bounds")
    tops = tops.reshape(NY, NX, CAP, cols_here)
    got = [lax.ppermute(tops[:, k], "prow", to_x(k)) for k in range(1, NX)]
    tops = jnp.where(p == 0, tops[:, 0], sum(got))
    got = [lax.ppermute(tops[k], "prow", to_y(k)) for k in range(1, NY)]
    top = jnp.where(p < NX, tops[0], sum(got))

    hi, lo = prep(lt_full)
    first = (p == 0).astype(jnp.int32)[None]
    return update(rows, first, u, chosen, top, hi, lo, trailing)


def solution(mesh):
    placed = (P("prow", "pcol"), P("prow", "pcol"), P())
    return jax.shard_map(
        on_device, mesh=mesh, in_specs=placed, out_specs=P("prow", "pcol"), check_vma=False
    )
```

time: 328 us -> 152 us (0.46)
  the two profiles are of different devices: /device:TPU:1 before, /device:TPU:60 now
where the time goes in v1:
time: 152 us; the launch traced here: 151 us
  waiting for transfers between devices  72.9 us (48%)
  starting transfers between devices  24.6 us (16%)
  local copies, waits for them, and re-layouts  19.9 us (13%)
  Pallas kernels  15.9 us (10%)
  between operations  13.9 us (9%)
  other arithmetic  3.45 us (2%)
    ppermute x7, waiting for transfers between devices, on_device(): got = [lax.ppermute(slab, 'prow', to_y(k)) for k in range(1, NY)]  44.9 us
    ppermute x7, waiting for transfers between devices, on_device(): got = [lax.ppermute(tops[k], 'prow', to_y(k)) for k in range(1, NY)]  27.3 us
    pallas_call x1, Pallas kernels, update(): pl.pallas_call(update_kernel, in_specs=[smem, smem] + [vmem] * 6, out_spe...  10.6 us
    all_to_all x1, starting transfers between devices, on_device(): lax.all_to_all(sent, 'prow', 0, 0, tiled=True)  9.76 us
    pallas_call x1, Pallas kernels, prep(): pl.pallas_call(prep_kernel, grid=(rows // tile,), in_specs=[pl.BlockSpec(...  5.3 us
    ppermute x7, starting transfers between devices, on_device(): got = [lax.ppermute(slab, 'prow', to_y(k)) for k in range(1, NY)]  5.28 us
    ppermute x7, starting transfers between devices, on_device(): got = [lax.ppermute(tops[k], 'prow', to_y(k)) for k in range(1, NY)]  5.28 us
    unnamed x12, local copies, waits for them, and re-layouts  5.09 us
  transfers between devices with their start and end apart: 23, of which 2 were waited for; matrix products, arithmetic and copies ran while one was open for 12% of the time, Pallas kernels for 4%

profile of v1, /device:TPU:60, one launch (start us, length us, event | category | flops | bytes accessed | tf_op | source)
XLA Modules:
  0.0 150.6 jit_solution(11504942960303783909)
XLA Ops:
  6.5 0.7 all-gather.5.cloned.1.call-update
  7.3 0.7 add_select_fusion.3
  8.4 2.4 %gather_fusion = f32[32,512]{1,0:T(8,128)S(1)} fusion(f32[1280,512]{1,0:T(8,128)} %trail_ref.1, s32[1024]{0:T(1024)S(1)} %pad_clamp_fusion.1), kind=kCustom, calls=%fused_computation | custom fusion | bytes 131200 | tf_op jit(solution)/shard_map/gather | solution.py:146
  10.8 1.6 %broadcast_in_dim.54 = f32[32,32,512]{2,1,0:T(8,128)} broadcast(f32[32,512]{1,0:T(8,128)S(1)} %gather_fusion), dimensions={1,2} | broadcast | bytes 2162688 | tf_op jit(solution)/shard_map/broadcast_in_dim | solution.py:147
  12.4 9.8 %all-to-all-start = ((f32[32,32,512]{2,1,0:T(8,128)}), f32[32,32,512]{2,1,0:T(8,128)}, u32[]{:S(2)}, u32[]{:S(2)}) async-start(f32[32,32,512]{2,1,0:T(8,128)} %broadcast_in_dim.54), calls=%async_computation | async-start | bytes 4194304 | tf_op jit(solution)/shard_map/all_to_all | solution.py:148
  22.3 0.8 collective-permute-start
  23.1 0.7 collective-permute-start.1
  23.7 0.7 collective-permute-start.2
  24.5 0.7 collective-permute-start.3
  26.1 0.7 collective-permute-start.5
  26.8 0.7 collective-permute-start.6
  27.5 0.7 collective-permute-start.7
  28.1 0.7 collective-permute-start.8
  28.8 1.3 collective-permute-start.9
  30.2 44.8 %collective-permute-done.9 = f32[32,512]{1,0:T(8,128)S(1)} collective-permute-done((f32[32,512]{1,0:T(8,128)S(1)}, f32[32,512]{1,0:T(8,128)S(1)}, u32[]{:S(2)}, u32[]{:S(2)}) %collective-permute-start.9) | collective-permute-done | bytes 65568 | tf_op jit(solution)/shard_map/ppermute | solution.py:132
  75.0 0.7 add_select_fusion
  75.7 4.9 %gather_fusion.2 = f32[1024,512]{1,0:T(8,128)} fusion(f32[512,512]{1,0:T(8,128)S(1)} %slice-done, s32[1024]{0:T(1024)S(1)} %broadcast_clamp_fusion), kind=kCustom, calls=%fused_computation.2 | custom fusion | bytes 4198400 | tf_op jit(solution)/shard_map/gather | solution.py:151
  80.7 1.5 %slice_bitcast_fusion.1 = (f32[8,32,512]{2,1,0:T(8,128)S(1)}, f32[8,32,512]{2,1,0:T(8,128)S(1)}, f32[8,32,512]{2,1,0:T(8,128)S(1)}) fusion(f32[8,4,32,512]{3,2,1,0:T(8,128)} %bitcast.42), kind=kLoop, calls=%fused_computation.9 | loop fusion | bytes 3145728 | tf_op jit(solution)/shard_map/squeeze | solution.py:153
  82.2 0.7 collective-permute-start.10
  82.9 0.7 collective-permute-start.11
  83.6 0.7 collective-permute-start.12
  84.3 1.3 fusion.1
  85.6 0.7 collective-permute-start.13
  89.7 1.3 collective-permute-start.19
  91.1 27.3 %collective-permute-done.19 = f32[32,512]{1,0:T(8,128)S(1)} collective-permute-done((f32[32,512]{1,0:T(8,128)S(1)}, f32[32,512]{1,0:T(8,128)S(1)}, u32[]{:S(2)}, u32[]{:S(2)}) %collective-permute-start.19) | collective-permute-done | bytes 65568 | tf_op jit(solution)/shard_map/ppermute | solution.py:155
  118.4 4.3 %gather_fusion.1 = f32[512,512]{1,0:T(8,128)} fusion(f32[1024,512]{1,0:T(8,128)} %bitcast.2, s32[1024]{0:T(1024)S(1)} %pad_clamp_fusion), kind=kCustom, calls=%fused_computation.1 | custom fusion | bytes 2099200 | tf_op jit(solution)/shard_map/gather | solution.py:149
  122.7 5.3 %prep_l.1 = (bf16[1280,512]{1,0:T(8,128)(2,1)}, bf16[1280,512]{1,0:T(8,128)(2,1)}) custom-call(f32[512,1280]{1,0:T(8,128)} %all-gather.5.cloned.1.call-done.lt_ref), custom_call_target="tpu_custom_call" | custom-call | tf_op jit(solution)/shard_map/prep_l/pallas_call | solution.py:33
  128.0 1.2 copy-done.1
  129.3 1.3 copy-done.2
  130.6 1.3 copy-done.3
  131.9 1.2 copy-done.4
  133.1 10.6 %solve_update.1 = f32[1280,512]{1,0:T(8,128)} custom-call(s32[32]{0:T(128)S(1)} %get-tuple-element.24.rows_ref, s32[1]{0:T(128)} %bitcast.first_ref, f32[512,512]{1,0:T(8,128)S(1)} %copy-done.4, f32[512,512]{1,0:T(8,128)S(1)} %copy-done.1, f32[32,512]{1,0:T(8,128)S(1)} %fusion.2.top_ref, bf16[1280,512]{1,0:T(8,128)(2,1)S(1)} %copy-done.2, ...), custom_call_target="tpu_custom_call" | custom-call | tf_op jit(solution)/shard_map/solve_update/pallas_call | solution.py:102
  (54 shorter events, 5.0 us)
Async XLA Ops:
  6.5 116.2 %all-gather.5.cloned.1.call-start = ((), (), s32[]{:S(2)}) async-start(), calls=%async_computation.2 | async-start | bytes 2785280 | tf_op jit(solution)/shard_map/all_gather | solution.py:127
  12.4 9.8 %copy-start.5 = (f32[1280,32]{0,1:T(8,128)S(1)}, f32[1280,32]{0,1:T(8,128)}, u32[]{:S(2)}) copy-start(f32[1280,32]{0,1:T(8,128)} %param.4) | copy-start | bytes 491524
  12.4 106.0 %all-to-all-start = ((f32[32,32,512]{2,1,0:T(8,128)}), f32[32,32,512]{2,1,0:T(8,128)}, u32[]{:S(2)}, u32[]{:S(2)}) async-start(f32[32,32,512]{2,1,0:T(8,128)} %broadcast_in_dim.54), calls=%async_computation | async-start | bytes 4194304 | tf_op jit(solution)/shard_map/all_to_all | solution.py:148
  22.2 53.6 %slice-start = ((f32[1280,512]{1,0:T(8,128)}), f32[512,512]{1,0:T(8,128)S(1)}, s32[]{:S(2)}) async-start(f32[1280,512]{1,0:T(8,128)} %trail_ref.1), calls=%async_computation.3 | async-start | bytes 2097152 | tf_op jit(solution)/shard_map/slice | solution.py:151
  22.2 105.8 %all-gather.3.cloned.1.call-start = ((), (), s32[]{:S(2)}) async-start(), calls=%async_computation.1 | async-start | bytes 1114112 | tf_op jit(solution)/shard_map/all_gather | solution.py:134
  22.3 2.2 %collective-permute-start = (f32[32,512]{1,0:T(8,128)S(1)}, f32[32,512]{1,0:T(8,128)S(1)}, u32[]{:S(2)}, u32[]{:S(2)}) collective-permute-start(f32[32,512]{1,0:T(8,128)S(1)} %slice.62), channel_id=1, source_target_pairs={{0,16},{1,17},{2,18},{3,19},{4,20},{5,21},{6,22},{7,23},{8,24},{9,... | collective-permute-start | bytes 196616 | tf_op jit(solution)/shard_map/ppermute | solution.py:130
  23.1 1.4 collective-permute-start.1
  23.7 0.7 collective-permute-start.2
  24.5 3.7 %collective-permute-start.3 = (f32[32,512]{1,0:T(8,128)S(1)}, f32[32,512]{1,0:T(8,128)S(1)}, u32[]{:S(2)}, u32[]{:S(2)}) collective-permute-start(f32[32,512]{1,0:T(8,128)S(1)} %add_select_fusion.1), channel_id=1, source_target_pairs={{0,64},{16,80},{32,96},{48,112},{1,65},{17,81},{33,97},{49,113},{2... | collective-permute-start | bytes 196616 | tf_op jit(solution)/shard_map/ppermute | solution.py:132
  25.1 3.7 %collective-permute-start.4 = (f32[32,512]{1,0:T(8,128)S(1)}, f32[32,512]{1,0:T(8,128)S(1)}, u32[]{:S(2)}, u32[]{:S(2)}) collective-permute-start(f32[32,512]{1,0:T(8,128)S(1)} %add_select_fusion.1), channel_id=1, source_target_pairs={{0,128},{16,144},{32,160},{48,176},{1,129},{17,145},{33,161},{49,1... | collective-permute-start | bytes 196616 | tf_op jit(solution)/shard_map/ppermute | solution.py:132
  26.1 4.0 %collective-permute-start.5 = (f32[32,512]{1,0:T(8,128)S(1)}, f32[32,512]{1,0:T(8,128)S(1)}, u32[]{:S(2)}, u32[]{:S(2)}) collective-permute-start(f32[32,512]{1,0:T(8,128)S(1)} %add_select_fusion.1), channel_id=1, source_target_pairs={{0,192},{16,208},{32,224},{48,240},{1,193},{17,209},{33,225},{49,2... | collective-permute-start | bytes 196616 | tf_op jit(solution)/shard_map/ppermute | solution.py:132
  26.8 3.4 %collective-permute-start.6 = (f32[32,512]{1,0:T(8,128)S(1)}, f32[32,512]{1,0:T(8,128)S(1)}, u32[]{:S(2)}, u32[]{:S(2)}) collective-permute-start(f32[32,512]{1,0:T(8,128)S(1)} %add_select_fusion.1), channel_id=1, source_target_pairs={{0,256},{16,272},{32,288},{48,304},{1,257},{17,273},{33,289},{49,3... | collective-permute-start | bytes 196616 | tf_op jit(solution)/shard_map/ppermute | solution.py:132
  27.5 2.7 %collective-permute-start.7 = (f32[32,512]{1,0:T(8,128)S(1)}, f32[32,512]{1,0:T(8,128)S(1)}, u32[]{:S(2)}, u32[]{:S(2)}) collective-permute-start(f32[32,512]{1,0:T(8,128)S(1)} %add_select_fusion.1), channel_id=1, source_target_pairs={{0,320},{16,336},{32,352},{48,368},{1,321},{17,337},{33,353},{49,3... | collective-permute-start | bytes 196616 | tf_op jit(solution)/shard_map/ppermute | solution.py:132
  28.1 2.0 %collective-permute-start.8 = (f32[32,512]{1,0:T(8,128)S(1)}, f32[32,512]{1,0:T(8,128)S(1)}, u32[]{:S(2)}, u32[]{:S(2)}) collective-permute-start(f32[32,512]{1,0:T(8,128)S(1)} %add_select_fusion.1), channel_id=1, source_target_pairs={{0,384},{16,400},{32,416},{48,432},{1,385},{17,401},{33,417},{49,4... | collective-permute-start | bytes 196616 | tf_op jit(solution)/shard_map/ppermute | solution.py:132
  28.8 46.2 %collective-permute-start.9 = (f32[32,512]{1,0:T(8,128)S(1)}, f32[32,512]{1,0:T(8,128)S(1)}, u32[]{:S(2)}, u32[]{:S(2)}) collective-permute-start(f32[32,512]{1,0:T(8,128)S(1)} %add_select_fusion.1), channel_id=1, source_target_pairs={{0,448},{16,464},{32,480},{48,496},{1,449},{17,465},{33,481},{49,4... | collective-permute-start | bytes 196616 | tf_op jit(solution)/shard_map/ppermute | solution.py:132
  82.2 2.1 %collective-permute-start.10 = (f32[8,32,512]{2,1,0:T(8,128)S(1)}, f32[8,32,512]{2,1,0:T(8,128)S(1)}, u32[]{:S(2)}, u32[]{:S(2)}) collective-permute-start(f32[8,32,512]{2,1,0:T(8,128)S(1)} %get-tuple-element.12), channel_id=1, source_target_pairs={{0,16},{1,17},{2,18},{3,19},{4,20},{5,21},{6,22},{7,23},{8,24},{9,... | collective-permute-start | bytes 1572872 | tf_op jit(solution)/shard_map/ppermute | solution.py:153
  82.9 1.4 collective-permute-start.11
  83.6 0.7 collective-permute-start.12
  85.6 3.4 %collective-permute-start.13 = (f32[32,512]{1,0:T(8,128)S(1)}, f32[32,512]{1,0:T(8,128)S(1)}, u32[]{:S(2)}, u32[]{:S(2)}) collective-permute-start(f32[32,512]{1,0:T(8,128)S(1)} %get-tuple-element.20), channel_id=1, source_target_pairs={{0,64},{16,80},{32,96},{48,112},{1,65},{17,81},{33,97},{49,113},{2... | collective-permute-start | bytes 196616 | tf_op jit(solution)/shard_map/ppermute | solution.py:155
  86.3 3.4 %collective-permute-start.14 = (f32[32,512]{1,0:T(8,128)S(1)}, f32[32,512]{1,0:T(8,128)S(1)}, u32[]{:S(2)}, u32[]{:S(2)}) collective-permute-start(f32[32,512]{1,0:T(8,128)S(1)} %get-tuple-element.14), channel_id=1, source_target_pairs={{0,128},{16,144},{32,160},{48,176},{1,129},{17,145},{33,161},{49,1... | collective-permute-start | bytes 196616 | tf_op jit(solution)/shard_map/ppermute | solution.py:155
  87.0 4.0 %collective-permute-start.15 = (f32[32,512]{1,0:T(8,128)S(1)}, f32[32,512]{1,0:T(8,128)S(1)}, u32[]{:S(2)}, u32[]{:S(2)}) collective-permute-start(f32[32,512]{1,0:T(8,128)S(1)} %get-tuple-element.19), channel_id=1, source_target_pairs={{0,192},{16,208},{32,224},{48,240},{1,193},{17,209},{33,225},{49,2... | collective-permute-start | bytes 196616 | tf_op jit(solution)/shard_map/ppermute | solution.py:155
  87.7 3.4 %collective-permute-start.16 = (f32[32,512]{1,0:T(8,128)S(1)}, f32[32,512]{1,0:T(8,128)S(1)}, u32[]{:S(2)}, u32[]{:S(2)}) collective-permute-start(f32[32,512]{1,0:T(8,128)S(1)} %get-tuple-element.18), channel_id=1, source_target_pairs={{0,256},{16,272},{32,288},{48,304},{1,257},{17,273},{33,289},{49,3... | collective-permute-start | bytes 196616 | tf_op jit(solution)/shard_map/ppermute | solution.py:155
  88.3 2.7 %collective-permute-start.17 = (f32[32,512]{1,0:T(8,128)S(1)}, f32[32,512]{1,0:T(8,128)S(1)}, u32[]{:S(2)}, u32[]{:S(2)}) collective-permute-start(f32[32,512]{1,0:T(8,128)S(1)} %get-tuple-element.17), channel_id=1, source_target_pairs={{0,320},{16,336},{32,352},{48,368},{1,321},{17,337},{33,353},{49,3... | collective-permute-start | bytes 196616 | tf_op jit(solution)/shard_map/ppermute | solution.py:155
  89.0 2.0 %collective-permute-start.18 = (f32[32,512]{1,0:T(8,128)S(1)}, f32[32,512]{1,0:T(8,128)S(1)}, u32[]{:S(2)}, u32[]{:S(2)}) collective-permute-start(f32[32,512]{1,0:T(8,128)S(1)} %get-tuple-element.16), channel_id=1, source_target_pairs={{0,384},{16,400},{32,416},{48,432},{1,385},{17,401},{33,417},{49,4... | collective-permute-start | bytes 196616 | tf_op jit(solution)/shard_map/ppermute | solution.py:155
  89.7 28.6 %collective-permute-start.19 = (f32[32,512]{1,0:T(8,128)S(1)}, f32[32,512]{1,0:T(8,128)S(1)}, u32[]{:S(2)}, u32[]{:S(2)}) collective-permute-start(f32[32,512]{1,0:T(8,128)S(1)} %get-tuple-element.15), channel_id=1, source_target_pairs={{0,448},{16,464},{32,480},{48,496},{1,449},{17,465},{33,481},{49,4... | collective-permute-start | bytes 196616 | tf_op jit(solution)/shard_map/ppermute | solution.py:155
  122.7 5.3 %copy-start = (f32[1280,512]{1,0:T(8,128)S(1)}, f32[1280,512]{1,0:T(8,128)}, u32[]{:S(2)}) copy-start(f32[1280,512]{1,0:T(8,128)} %trail_ref.1) | copy-start | bytes 7864324
  128.0 1.2 copy-start.1
  129.3 1.3 copy-start.2
  130.6 1.3 copy-start.3
  131.9 1.2 copy-start.4
Sparse Core Ops, SparseCore 0:
  9.5 47.7 all-gather.4
  75.8 44.6 all-gather.2

commit v2 on v1

v2 whole, which is shorter than its diff:
```python
import jax
import jax.numpy as jnp
from jax import lax
from jax.experimental import pallas as pl
from jax.experimental.pallas import tpu as pltpu
from jax.sharding import Mesh, PartitionSpec as P

NX, NY, NZ, NC = 4, 8, 8, 2
NPROW = NX * NY
CAP = 32
LANES = 128
SHARE = LANES // CAP
PROW, PCOL = ("y", "x"), ("z", "c")
HI = lax.Precision.HIGHEST
SMEM = pl.BlockSpec(memory_space=pltpu.SMEM)
VMEM = pl.BlockSpec(memory_space=pltpu.VMEM)


def dot(a, b, dims=((1,), (0,)), precision=HI):
    return lax.dot_general(a, b, (dims, ((), ())), precision=precision, preferred_element_type=jnp.float32)


def split(a):
    hi = a.astype(jnp.bfloat16)
    lo = (a - hi.astype(jnp.float32)).astype(jnp.bfloat16)
    return hi, lo


def pick_kernel(rows_ref, group_ref, trail_ref, out_ref, near, lanes, sems):
    def copy(r):
        tile = pl.multiple_of((jnp.maximum(rows_ref[r], 0) // 8) * 8, 8)
        return pltpu.make_async_copy(trail_ref.at[pl.ds(tile, 8), :], near.at[r], sems.at[r])

    for r in range(CAP):
        copy(r).start()
    lanes[...] = jnp.zeros_like(lanes)
    base = group_ref[0] * CAP
    for r in range(CAP):
        copy(r).wait()
        row = jnp.maximum(rows_ref[r], 0) % 8
        lanes[pl.ds(base + r, 1), :] = near[r, pl.ds(row, 1), :]
    out_ref[...] = lanes[...].T


def pick(rows, group, trailing):
    cols = trailing.shape[1]
    return pl.pallas_call(
        pick_kernel,
        in_specs=[SMEM, SMEM, pl.BlockSpec(memory_space=pl.ANY)],
        out_specs=VMEM,
        out_shape=jax.ShapeDtypeStruct((cols, LANES), jnp.float32),
        scratch_shapes=[
            pltpu.VMEM((CAP, 8, cols), jnp.float32),
            pltpu.VMEM((LANES, cols), jnp.float32),
            pltpu.SemaphoreType.DMA((CAP,)),
        ],
        name="pick_rows",
    )(rows, group, trailing)


def order_kernel(slots_ref, onehot_ref, out_ref):
    owners, cols, _ = slots_ref.shape
    acc = None
    for g in range(owners // SHARE):
        x, y = divmod(SHARE * g, NY)
        part = slots_ref[NX * y + x]
        for i in range(1, SHARE):
            part = part + slots_ref[NX * (y + i) + x]
        hi, rest = split(part)
        mid, lo = split(part - hi.astype(jnp.float32))
        three = jnp.concatenate([hi, mid, lo], axis=0)
        got = dot(three, onehot_ref[pl.ds(g * LANES, LANES), :], precision=None)
        acc = got if acc is None else acc + got
    rows = acc[:cols] + acc[cols : 2 * cols] + acc[2 * cols :]
    out_ref[...] = jnp.broadcast_to(rows[None], out_ref.shape)


def to_order(slots, onehot):
    owners, cols, _ = slots.shape
    return pl.pallas_call(
        order_kernel,
        in_specs=[VMEM, VMEM],
        out_specs=VMEM,
        out_shape=jax.ShapeDtypeStruct((owners, cols, onehot.shape[1]), jnp.float32),
        name="slots_to_order",
    )(slots, onehot)


def tops_kernel(first_ref, onehot_ref, trail_ref, *refs):
    outs, sems = refs[:NX], refs[NX]

    def run(pick, top, rows):
        n = top.shape[0]
        reads = [
            pltpu.make_async_copy(trail_ref.at[pl.ds(0, n), :], top, sems.at[0]),
            pltpu.make_async_copy(onehot_ref, pick, sems.at[1]),
        ]
        for copy in reads:
            copy.start()
        for copy in reads:
            copy.wait()
        hi, rest = split(top[...])
        mid, lo = split(top[...] - hi.astype(jnp.float32))
        writes = []
        for x in range(NX):
            here = pick[pl.ds(x * NY * CAP, NY * CAP), :]
            got = dot(here, hi, precision=None) + dot(here, mid, precision=None)
            rows[x] = got + dot(here, lo, precision=None)
            writes.append(pltpu.make_async_copy(rows.at[x], outs[x], sems.at[2 + x]))
            writes[-1].start()
        for copy in writes:
            copy.wait()

    @pl.when(first_ref[0] == 1)
    def _():
        slots, n = onehot_ref.shape
        cols = trail_ref.shape[1]
        pl.run_scoped(
            run,
            pltpu.VMEM((slots, n), jnp.bfloat16),
            pltpu.VMEM((n, cols), jnp.float32),
            pltpu.VMEM((NX, NY * CAP, cols), jnp.float32),
        )


def to_owners(first, onehot, trailing):
    cols = trailing.shape[1]
    hbm = pl.BlockSpec(memory_space=pl.ANY)
    return pl.pallas_call(
        tops_kernel,
        in_specs=[SMEM, hbm, hbm],
        out_specs=[hbm] * NX,
        out_shape=[jax.ShapeDtypeStruct((NY * CAP, cols), jnp.float32)] * NX,
        scratch_shapes=[pltpu.SemaphoreType.DMA((2 + NX,))],
        compiler_params=pltpu.CompilerParams(vmem_limit_bytes=24 * 1024 * 1024),
        name="tops_to_owners",
    )(first, onehot, trailing)


def invert_upper(u_ref, m_ref, between):
    n = u_ref.shape[0]
    base = 128
    row = lax.broadcasted_iota(jnp.int32, (base, base), 0)
    col = lax.broadcasted_iota(jnp.int32, (base, base), 1)
    eye = jnp.where(row == col, 1.0, 0.0)
    blocks = [u_ref[pl.ds(b * base, base), pl.ds(b * base, base)] for b in range(n // base)]
    invs = [eye] * len(blocks)
    m_ref[...] = jnp.zeros_like(m_ref)
    s = 1
    while s < base:
        mask = (row // (2 * s) == col // (2 * s)) & (row % (2 * s) < s) & (col % (2 * s) >= s)
        parts = [jnp.where(mask, u, 0.0) for u in blocks]
        if s == 1:
            invs = [m - q for m, q in zip(invs, parts)]
        else:
            half = [dot(m, q) for m, q in zip(invs, parts)]
            invs = [m - dot(h, m) for m, h in zip(invs, half)]
        between()
        s *= 2
    for b, m in enumerate(invs):
        m_ref[pl.ds(b * base, base), pl.ds(b * base, base)] = m
    s = base
    while s < n:
        for b in range(0, n, 2 * s):
            up, dn = pl.ds(b, s), pl.ds(b + s, s)
            t = dot(m_ref[up, up], u_ref[up, dn])
            m_ref[up, dn] = -dot(t, m_ref[dn, dn])
        s *= 2


TILE = 256


def factor_kernel(full_ref, m3_ref, l2_ref, u, m, lt, sems):
    n, rows = lt.shape
    get_u = pltpu.make_async_copy(full_ref.at[:, pl.ds(rows, n)], u, sems.at[0])
    get_l = pltpu.make_async_copy(full_ref.at[:, pl.ds(0, rows)], lt, sems.at[1])
    get_u.start()
    get_l.start()
    get_u.wait()

    todo = list(range(rows // TILE))

    def between():
        if not todo:
            return
        i = todo.pop(0)
        if i == 0:
            get_l.wait()
        at = pl.ds(i * TILE, TILE)
        hi, lo = split(lt[:, at].T)
        l2_ref[at, pl.ds(0, n)] = hi
        l2_ref[at, pl.ds(n, n)] = lo

    invert_upper(u, m, between)
    while todo:
        between()
    hi, lo = split(m[...])
    m3_ref[pl.ds(0, n), :] = hi
    m3_ref[pl.ds(n, n), :] = hi
    m3_ref[pl.ds(2 * n, n), :] = lo


def factor(full, rows):
    n = full.shape[0]
    f32, bf16 = jnp.float32, jnp.bfloat16
    return pl.pallas_call(
        factor_kernel,
        in_specs=[pl.BlockSpec(memory_space=pl.ANY)],
        out_specs=[VMEM, VMEM],
        out_shape=[jax.ShapeDtypeStruct((3 * n, n), bf16), jax.ShapeDtypeStruct((rows, 2 * n), bf16)],
        scratch_shapes=[
            pltpu.VMEM((n, n), f32),
            pltpu.VMEM((n, n), f32),
            pltpu.VMEM((n, rows), f32),
            pltpu.SemaphoreType.DMA((2,)),
        ],
        compiler_params=pltpu.CompilerParams(vmem_limit_bytes=56 * 1024 * 1024),
        name="factor",
    )(full)


def update_kernel(
    rows_ref, first_ref, top_ref, m3_ref, l2_ref, ct_ref, trail_ref, out_ref, m3, l2, ct, x3, here, sems
):
    rows, n = l2.shape[0], ct.shape[1]
    tiles, late = rows // TILE, n // TILE
    sources = ((ct_ref, ct), (m3_ref, m3), (trail_ref, here), (l2_ref, l2))
    gets = [pltpu.make_async_copy(a, b, sems.at[tiles + i]) for i, (a, b) in enumerate(sources)]
    for copy in gets:
        copy.start()
    gets[0].wait()
    gets[1].wait()
    hi, lo = split(ct[...])
    xt = dot(jnp.concatenate([hi, lo, hi], axis=1), m3[...], precision=None)
    hi, lo = split(xt)
    x3[:, pl.ds(0, n)] = hi
    x3[:, pl.ds(n, n)] = hi
    x3[:, pl.ds(2 * n, n)] = lo

    gets[2].wait()
    for r in range(CAP):
        row = rows_ref[r]

        @pl.when(row >= 0)
        def _(r=r, row=row):
            here[pl.ds(row, 1), :] = top_ref[pl.ds(r, 1), :]

    gets[3].wait()
    puts = []

    def put(i):
        at = pl.ds(i * TILE, TILE)
        puts.append(pltpu.make_async_copy(here.at[at, :], out_ref.at[at, :], sems.at[i]))
        puts[-1].start()

    both = ((1,), (1,))
    for i in list(range(late, tiles)) + list(range(late)):
        at = pl.ds(i * TILE, TILE)
        acc = dot(l2[at, :], x3[:, pl.ds(0, 2 * n)], both, None)
        acc = acc + dot(l2[at, pl.ds(0, n)], x3[:, pl.ds(2 * n, n)], both, None)
        here[at, :] = here[at, :] - acc
        if i >= late:
            put(i)

    @pl.when(first_ref[0] == 1)
    def _():
        here[pl.ds(0, n), :] = xt.T

    for i in range(late):
        put(i)
    for copy in puts:
        copy.wait()


def update(rows, first, top, m3, l2, ct, trailing):
    height, cols = trailing.shape
    n = ct.shape[1]
    hbm = pl.BlockSpec(memory_space=pl.ANY)
    f32, bf16 = jnp.float32, jnp.bfloat16
    return pl.pallas_call(
        update_kernel,
        in_specs=[SMEM, SMEM, VMEM, hbm, hbm, hbm, hbm],
        out_specs=hbm,
        out_shape=jax.ShapeDtypeStruct(trailing.shape, f32),
        scratch_shapes=[
            pltpu.VMEM(m3.shape, bf16),
            pltpu.VMEM(l2.shape, bf16),
            pltpu.VMEM(ct.shape, f32),
            pltpu.VMEM((cols, 3 * n), bf16),
            pltpu.VMEM((height, cols), f32),
            pltpu.SemaphoreType.DMA((height // TILE + 4,)),
        ],
        compiler_params=pltpu.CompilerParams(vmem_limit_bytes=56 * 1024 * 1024),
        name="solve_update",
    )(rows, first, top, m3, l2, ct, trailing)


def to_x(k):
    return [(0, k)]


def to_y(k):
    return [(x, NX * k + x) for x in range(NX)]


def after(value, *others):
    return lax.optimization_barrier((value, *others))[0]


def on_device(trailing, l_panel, pivots):
    rows_here, cols_here = trailing.shape
    block = pivots.shape[0]
    p = lax.axis_index(PROW)
    first = (p == 0).astype(jnp.int32)[None]

    owner = pivots // rows_here
    local = pivots % rows_here
    ks = jnp.arange(block, dtype=jnp.int32)
    before = (owner[None, :] == owner[:, None]) & (ks[None, :] < ks[:, None])
    place = (owner % NX) * NY + owner // NX
    slot = place * CAP + jnp.sum(before.astype(jnp.int32), axis=1)
    y, x = lax.axis_index("y"), lax.axis_index("x")
    mine = slot[None, :] == ((x * NY + y) * CAP + jnp.arange(CAP, dtype=jnp.int32))[:, None]
    rows = jnp.sum(jnp.where(mine, local[None, :] + 1, 0), axis=1) - 1
    slots = jnp.arange(NPROW * CAP, dtype=jnp.int32)
    onehot = (slot[None, :] == slots[:, None]).astype(jnp.bfloat16)
    lanes = pick(rows, (y % SHARE)[None], trailing)

    lt = l_panel.T
    slab = lt[:, :block]
    got = [lax.ppermute(slab, PROW, to_x(k)) for k in range(1, NX)]
    slab = jnp.where(p == 0, slab, sum(got))

    slab, lanes = lax.optimization_barrier((slab, lanes))

    got = [lax.ppermute(slab, PROW, to_y(k)) for k in range(1, NY)]
    lanes = after(lanes, got[0])
    slab = jnp.where(p < NX, slab, sum(got))

    full = lax.all_gather(jnp.concatenate([lt, slab], axis=1), PCOL, axis=0, tiled=True)

    share = lanes.reshape(NPROW, cols_here // NPROW, LANES)
    share = lax.all_to_all(share, PROW, 0, 0, tiled=True)

    tops = to_owners(first, onehot, after(trailing, slab))
    tops_x = [lax.ppermute(tops[k], PROW, to_x(k)) for k in range(1, NX)]

    ct = to_order(share, onehot)
    ct, tops_x = lax.optimization_barrier((ct, tops_x))
    ct = lax.all_to_all(ct, PROW, 0, 0, tiled=True).reshape(cols_here, block)

    tops = jnp.where(p == 0, tops[0], sum(tops_x)).reshape(NY, CAP, cols_here)
    early, late = range(1, NY - 2), range(NY - 2, NY)
    got = [lax.ppermute(tops[k], PROW, to_y(k)) for k in early]
    m3, l2 = factor(full, rows_here)
    tops, m3, got = lax.optimization_barrier((tops, m3, got))
    got += [lax.ppermute(tops[k], PROW, to_y(k)) for k in late]
    top = jnp.where(p < NX, tops[0], sum(got))
    return update(rows, first, top, m3, l2, ct, trailing)


def solution(mesh):
    grid = Mesh(mesh.devices.reshape(NY, NX, NZ, NC), ("y", "x", "z", "c"))
    placed = (P(PROW, PCOL), P(PROW, PCOL), P())
    return jax.shard_map(
        on_device, mesh=grid, in_specs=placed, out_specs=P(PROW, PCOL), check_vma=False
    )
```

time: 152 us -> 119 us (0.78)
  the two profiles are of different devices: /device:TPU:60 before, /device:TPU:256 now
where the time goes in v2:
time: 119 us
  starting transfers between devices  41.6 us (35%)
  Pallas kernels  25.1 us (21%)
  blocking collectives  21.9 us (18%)
  between operations  13.8 us (12%)
  waiting for transfers between devices  9.41 us (8%)
  other arithmetic  4.83 us (4%)
  local copies, waits for them, and re-layouts  1.96 us (2%)
    all_to_all x1, blocking collectives, on_device(): share = lax.all_to_all(share, PROW, 0, 0, tiled=True)  21.9 us
    ppermute x5, starting transfers between devices, on_device(): got = [lax.ppermute(tops[k], PROW, to_y(k)) for k in early]  12.2 us
    ppermute x7, starting transfers between devices, on_device(): got = [lax.ppermute(slab, PROW, to_y(k)) for k in range(1, NY)]  9.05 us
    pallas_call x1, Pallas kernels, factor(): pl.pallas_call(factor_kernel, in_specs=[pl.BlockSpec(memory_space=pl.ANY)...  8.08 us
    pallas_call x1, Pallas kernels, update(): pl.pallas_call(update_kernel, in_specs=[SMEM, SMEM, VMEM, hbm, hbm, hbm,...  7.77 us
    ppermute x3, starting transfers between devices, on_device(): got = [lax.ppermute(slab, PROW, to_x(k)) for k in range(1, NX)]  7.24 us
    all_to_all x1, starting transfers between devices, on_device(): ct = lax.all_to_all(ct, PROW, 0, 0, tiled=True).reshape(cols_here, block)  5.78 us
    ppermute x5, waiting for transfers between devices, on_device(): got = [lax.ppermute(tops[k], PROW, to_y(k)) for k in early]  5.45 us
  transfers between devices with their start and end apart: 22, of which 9 were waited for; matrix products, arithmetic and copies ran while one was open for 3% of the time, Pallas kernels for 15%

profile of v2, /device:TPU:256, one launch (start us, length us, event | category | flops | bytes accessed | tf_op | source)
XLA Modules:
  0.0 118.6 jit_solution(14334750867391266500)
XLA Ops:
  7.5 4.7 %collective-permute-start.2 = (f32[32,512]{1,0:T(8,128)S(1)}, f32[32,512]{1,0:T(8,128)S(1)}, u32[]{:S(2)}, u32[]{:S(2)}) collective-permute-start(f32[32,512]{1,0:T(8,128)S(1)} %slice.41), channel_id=1, source_target_pairs={{0,48},{1,49},{2,50},{3,51},{4,52},{5,53},{6,54},{7,55},{8,56},{9,... | collective-permute-start | bytes 196616 | tf_op jit(solution)/shard_map/ppermute | solution.py:332
  12.1 1.3 %collective-permute-start.1 = (f32[32,512]{1,0:T(8,128)S(1)}, f32[32,512]{1,0:T(8,128)S(1)}, u32[]{:S(2)}, u32[]{:S(2)}) collective-permute-start(f32[32,512]{1,0:T(8,128)S(1)} %slice.41), channel_id=1, source_target_pairs={{0,32},{1,33},{2,34},{3,35},{4,36},{5,37},{6,38},{7,39},{8,40},{9,... | collective-permute-start | bytes 196616 | tf_op jit(solution)/shard_map/ppermute | solution.py:332
  13.4 1.3 %collective-permute-start = (f32[32,512]{1,0:T(8,128)S(1)}, f32[32,512]{1,0:T(8,128)S(1)}, u32[]{:S(2)}, u32[]{:S(2)}) collective-permute-start(f32[32,512]{1,0:T(8,128)S(1)} %slice.41), channel_id=1, source_target_pairs={{0,16},{1,17},{2,18},{3,19},{4,20},{5,21},{6,22},{7,23},{8,24},{9,... | collective-permute-start | bytes 196616 | tf_op jit(solution)/shard_map/ppermute | solution.py:332
  16.5 3.4 %pick_rows.1 = f32[512,128]{1,0:T(8,128)} custom-call(s32[32]{0:T(128)} %broadcast_add_fusion.rows_ref, s32[1]{0:T(128)} %bitcast.2.group_ref, f32[1280,512]{1,0:T(8,128)} %trail_ref.4), custom_call_target="tpu_custom_call" | custom-call | tf_op jit(solution)/shard_map/pick_rows/pallas_call | solution.py:47
  19.9 1.3 %collective-permute-start.9 = (f32[32,512]{1,0:T(8,128)S(1)}, f32[32,512]{1,0:T(8,128)S(1)}, u32[]{:S(2)}, u32[]{:S(2)}) collective-permute-start(f32[32,512]{1,0:T(8,128)S(1)} %add_select_fusion.2), channel_id=1, source_target_pairs={{0,448},{16,464},{32,480},{48,496},{1,449},{17,465},{33,481},{49,4... | collective-permute-start | bytes 196616 | tf_op jit(solution)/shard_map/ppermute | solution.py:337
  21.2 1.3 %collective-permute-start.8 = (f32[32,512]{1,0:T(8,128)S(1)}, f32[32,512]{1,0:T(8,128)S(1)}, u32[]{:S(2)}, u32[]{:S(2)}) collective-permute-start(f32[32,512]{1,0:T(8,128)S(1)} %add_select_fusion.2), channel_id=1, source_target_pairs={{0,384},{16,400},{32,416},{48,432},{1,385},{17,401},{33,417},{49,4... | collective-permute-start | bytes 196616 | tf_op jit(solution)/shard_map/ppermute | solution.py:337
  22.5 1.3 %collective-permute-start.7 = (f32[32,512]{1,0:T(8,128)S(1)}, f32[32,512]{1,0:T(8,128)S(1)}, u32[]{:S(2)}, u32[]{:S(2)}) collective-permute-start(f32[32,512]{1,0:T(8,128)S(1)} %add_select_fusion.2), channel_id=1, source_target_pairs={{0,320},{16,336},{32,352},{48,368},{1,321},{17,337},{33,353},{49,3... | collective-permute-start | bytes 196616 | tf_op jit(solution)/shard_map/ppermute | solution.py:337
  23.8 1.3 %collective-permute-start.6 = (f32[32,512]{1,0:T(8,128)S(1)}, f32[32,512]{1,0:T(8,128)S(1)}, u32[]{:S(2)}, u32[]{:S(2)}) collective-permute-start(f32[32,512]{1,0:T(8,128)S(1)} %add_select_fusion.2), channel_id=1, source_target_pairs={{0,256},{16,272},{32,288},{48,304},{1,257},{17,273},{33,289},{49,3... | collective-permute-start | bytes 196616 | tf_op jit(solution)/shard_map/ppermute | solution.py:337
  25.1 1.3 %collective-permute-start.5 = (f32[32,512]{1,0:T(8,128)S(1)}, f32[32,512]{1,0:T(8,128)S(1)}, u32[]{:S(2)}, u32[]{:S(2)}) collective-permute-start(f32[32,512]{1,0:T(8,128)S(1)} %add_select_fusion.2), channel_id=1, source_target_pairs={{0,192},{16,208},{32,224},{48,240},{1,193},{17,209},{33,225},{49,2... | collective-permute-start | bytes 196616 | tf_op jit(solution)/shard_map/ppermute | solution.py:337
  26.4 1.3 %collective-permute-start.4 = (f32[32,512]{1,0:T(8,128)S(1)}, f32[32,512]{1,0:T(8,128)S(1)}, u32[]{:S(2)}, u32[]{:S(2)}) collective-permute-start(f32[32,512]{1,0:T(8,128)S(1)} %add_select_fusion.2), channel_id=1, source_target_pairs={{0,128},{16,144},{32,160},{48,176},{1,129},{17,145},{33,161},{49,1... | collective-permute-start | bytes 196616 | tf_op jit(solution)/shard_map/ppermute | solution.py:337
  27.8 1.3 %collective-permute-start.3 = (f32[32,512]{1,0:T(8,128)S(1)}, f32[32,512]{1,0:T(8,128)S(1)}, u32[]{:S(2)}, u32[]{:S(2)}) collective-permute-start(f32[32,512]{1,0:T(8,128)S(1)} %add_select_fusion.2), channel_id=1, source_target_pairs={{0,64},{16,80},{32,96},{48,112},{1,65},{17,81},{33,97},{49,113},{2... | collective-permute-start | bytes 196616 | tf_op jit(solution)/shard_map/ppermute | solution.py:337
  29.1 1.2 %collective-permute-done.4 = f32[32,512]{1,0:T(8,128)S(1)} collective-permute-done((f32[32,512]{1,0:T(8,128)S(1)}, f32[32,512]{1,0:T(8,128)S(1)}, u32[]{:S(2)}, u32[]{:S(2)}) %collective-permute-start.4) | collective-permute-done | bytes 65568 | tf_op jit(solution)/shard_map/ppermute | solution.py:337
  32.3 3.1 %tops_to_owners.1 = (f32[256,512]{1,0:T(8,128)S(1)}, f32[256,512]{1,0:T(8,128)}, f32[256,512]{1,0:T(8,128)}, f32[256,512]{1,0:T(8,128)}) custom-call(s32[1]{0:T(128)} %bitcast.first_ref, bf16[1024,512]{1,0:T(8,128)(2,1)S(1)} %fusion.onehot_ref, f32[1280,512]{1,0:T(8,128)S(1)} %copy-done), custom_call_target="tpu_custom_call" | custom-call | tf_op jit(solution)/shard_map/tops_to_owners/pallas_call | solution.py:129
  35.5 1.3 %collective-permute-start.10 = (f32[256,512]{1,0:T(8,128)}, f32[256,512]{1,0:T(8,128)S(1)}, u32[]{:S(2)}, u32[]{:S(2)}) collective-permute-start(f32[256,512]{1,0:T(8,128)} %get-tuple-element.31), channel_id=1, source_target_pairs={{0,16},{1,17},{2,18},{3,19},{4,20},{5,21},{6,22},{7,23},{8,24},{9,... | collective-permute-start | bytes 1572872 | tf_op jit(solution)/shard_map/ppermute | solution.py:347
  36.8 1.4 %collective-permute-start.11 = (f32[256,512]{1,0:T(8,128)}, f32[256,512]{1,0:T(8,128)S(1)}, u32[]{:S(2)}, u32[]{:S(2)}) collective-permute-start(f32[256,512]{1,0:T(8,128)} %get-tuple-element.32), channel_id=1, source_target_pairs={{0,32},{1,33},{2,34},{3,35},{4,36},{5,37},{6,38},{7,39},{8,40},{9,... | collective-permute-start | bytes 1572872 | tf_op jit(solution)/shard_map/ppermute | solution.py:347
  38.2 2.1 %collective-permute-start.12 = (f32[256,512]{1,0:T(8,128)}, f32[256,512]{1,0:T(8,128)}, u32[]{:S(2)}, u32[]{:S(2)}) collective-permute-start(f32[256,512]{1,0:T(8,128)} %get-tuple-element.33), channel_id=1, source_target_pairs={{0,48},{1,49},{2,50},{3,51},{4,52},{5,53},{6,54},{7,55},{8,56},{9,... | collective-permute-start | bytes 1572872 | tf_op jit(solution)/shard_map/ppermute | solution.py:347
  40.3 21.9 %all_to_all.10.slots_ref = f32[32,16,128]{2,1,0:T(8,128)} all-to-all(f32[32,16,128]{2,1,0:T(8,128)S(1)} %bitcast.15), channel_id=1, replica_groups=mesh['y'=8,'x'=4,'z'=8,'c'=2] {'y','x'}, dimensions={0} | all-to-all | bytes 524288 | tf_op jit(solution)/shard_map/all_to_all | solution.py:344
  62.1 2.8 %slots_to_order.1 = f32[32,16,512]{2,1,0:T(8,128)} custom-call(f32[32,16,128]{2,1,0:T(8,128)} %all_to_all.10.slots_ref, bf16[1024,512]{1,0:T(8,128)(2,1)} %copy-done.1), custom_call_target="tpu_custom_call" | custom-call | tf_op jit(solution)/shard_map/slots_to_order/pallas_call | solution.py:80
  65.0 5.8 %all-to-all-start.1 = ((f32[32,16,512]{2,1,0:T(8,128)}), f32[32,16,512]{2,1,0:T(8,128)S(1)}, u32[]{:S(2)}, u32[]{:S(2)}) async-start(f32[32,16,512]{2,1,0:T(8,128)} %slots_to_order.1), calls=%async_computation.1 | async-start | bytes 2097152 | tf_op jit(solution)/shard_map/all_to_all | solution.py:351
  70.7 1.3 %add_select_fusion = f32[256,512]{1,0:T(8,128)S(1)} fusion(f32[256,512]{1,0:T(8,128)S(1)} %get-tuple-element.28, f32[256,512]{1,0:T(8,128)} %collective-permute-done.12, f32[256,512]{1,0:T(8,128)S(1)} %collective-permute-done.10, f32[256,512]{1,0:T(8,128)S(1)} %collective-permute-done.11, pred[]{:T(512)S(6)} %eq.55), kind=kLoop, calls=%fused_computation.5 | loop fusion | flops 393216 | bytes 2621441 | tf_op jit(solution)/shard_map/jit(_where)/select_n | solution.py:353
  72.0 6.7 %collective-permute-start.17 = (f32[32,512]{1,0:T(8,128)S(1)}, f32[32,512]{1,0:T(8,128)S(1)}, u32[]{:S(2)}, u32[]{:S(2)}) collective-permute-start(f32[32,512]{1,0:T(8,128)S(1)} %get-tuple-element.49), channel_id=1, source_target_pairs={{0,320},{16,336},{32,352},{48,368},{1,321},{17,337},{33,353},{49,3... | collective-permute-start | bytes 196616 | tf_op jit(solution)/shard_map/ppermute | solution.py:355
  78.8 1.6 %collective-permute-start.16 = (f32[32,512]{1,0:T(8,128)S(1)}, f32[32,512]{1,0:T(8,128)S(1)}, u32[]{:S(2)}, u32[]{:S(2)}) collective-permute-start(f32[32,512]{1,0:T(8,128)S(1)} %get-tuple-element.50), channel_id=1, source_target_pairs={{0,256},{16,272},{32,288},{48,304},{1,257},{17,273},{33,289},{49,3... | collective-permute-start | bytes 196616 | tf_op jit(solution)/shard_map/ppermute | solution.py:355
  80.3 1.3 %collective-permute-start.15 = (f32[32,512]{1,0:T(8,128)S(1)}, f32[32,512]{1,0:T(8,128)S(1)}, u32[]{:S(2)}, u32[]{:S(2)}) collective-permute-start(f32[32,512]{1,0:T(8,128)S(1)} %get-tuple-element.51), channel_id=1, source_target_pairs={{0,192},{16,208},{32,224},{48,240},{1,193},{17,209},{33,225},{49,2... | collective-permute-start | bytes 196616 | tf_op jit(solution)/shard_map/ppermute | solution.py:355
  81.6 1.3 %collective-permute-start.14 = (f32[32,512]{1,0:T(8,128)S(1)}, f32[32,512]{1,0:T(8,128)S(1)}, u32[]{:S(2)}, u32[]{:S(2)}) collective-permute-start(f32[32,512]{1,0:T(8,128)S(1)} %get-tuple-element.52), channel_id=1, source_target_pairs={{0,128},{16,144},{32,160},{48,176},{1,129},{17,145},{33,161},{49,1... | collective-permute-start | bytes 196616 | tf_op jit(solution)/shard_map/ppermute | solution.py:355
  82.9 1.3 %collective-permute-start.13 = (f32[32,512]{1,0:T(8,128)S(1)}, f32[32,512]{1,0:T(8,128)S(1)}, u32[]{:S(2)}, u32[]{:S(2)}) collective-permute-start(f32[32,512]{1,0:T(8,128)S(1)} %get-tuple-element.53), channel_id=1, source_target_pairs={{0,64},{16,80},{32,96},{48,112},{1,65},{17,81},{33,97},{49,113},{2... | collective-permute-start | bytes 196616 | tf_op jit(solution)/shard_map/ppermute | solution.py:355
  84.3 8.1 %factor.1 = (bf16[1536,512]{1,0:T(8,128)(2,1)}, bf16[1280,1024]{1,0:T(8,128)(2,1)}) custom-call(f32[512,1792]{1,0:T(8,128)} %all-gather.2.cloned.1.call-done.full_ref), custom_call_target="tpu_custom_call" | custom-call | tf_op jit(solution)/shard_map/factor/pallas_call | solution.py:207
  92.4 1.3 %collective-permute-done.17 = f32[32,512]{1,0:T(8,128)S(1)} collective-permute-done((f32[32,512]{1,0:T(8,128)S(1)}, f32[32,512]{1,0:T(8,128)S(1)}, u32[]{:S(2)}, u32[]{:S(2)}) %collective-permute-start.17) | collective-permute-done | bytes 65568 | tf_op jit(solution)/shard_map/ppermute | solution.py:355
  93.6 2.0 %collective-permute-done.16 = f32[32,512]{1,0:T(8,128)S(1)} collective-permute-done((f32[32,512]{1,0:T(8,128)S(1)}, f32[32,512]{1,0:T(8,128)S(1)}, u32[]{:S(2)}, u32[]{:S(2)}) %collective-permute-start.16) | collective-permute-done | bytes 65568 | tf_op jit(solution)/shard_map/ppermute | solution.py:355
  97.8 1.3 %collective-permute-start.18 = (f32[32,512]{1,0:T(8,128)S(1)}, f32[32,512]{1,0:T(8,128)S(1)}, u32[]{:S(2)}, u32[]{:S(2)}) collective-permute-start(f32[32,512]{1,0:T(8,128)S(1)} %get-tuple-element.47), channel_id=1, source_target_pairs={{0,384},{16,400},{32,416},{48,432},{1,385},{17,401},{33,417},{49,4... | collective-permute-start | bytes 196616 | tf_op jit(solution)/shard_map/ppermute | solution.py:358
  99.1 1.3 %collective-permute-start.19 = (f32[32,512]{1,0:T(8,128)S(1)}, f32[32,512]{1,0:T(8,128)S(1)}, u32[]{:S(2)}, u32[]{:S(2)}) collective-permute-start(f32[32,512]{1,0:T(8,128)S(1)} %get-tuple-element.48), channel_id=1, source_target_pairs={{0,448},{16,464},{32,480},{48,496},{1,449},{17,465},{33,481},{49,4... | collective-permute-start | bytes 196616 | tf_op jit(solution)/shard_map/ppermute | solution.py:358
  101.0 1.3 %collective-permute-done.19 = f32[32,512]{1,0:T(8,128)S(1)} collective-permute-done((f32[32,512]{1,0:T(8,128)S(1)}, f32[32,512]{1,0:T(8,128)S(1)}, u32[]{:S(2)}, u32[]{:S(2)}) %collective-permute-start.19) | collective-permute-done | bytes 65568 | tf_op jit(solution)/shard_map/ppermute | solution.py:358
  104.0 7.8 %solve_update.1 = f32[1280,512]{1,0:T(8,128)} custom-call(s32[32]{0:T(128)} %broadcast_add_fusion.rows_ref, s32[1]{0:T(128)} %bitcast.first_ref, f32[32,512]{1,0:T(8,128)} %bitcast_select_fusion.top_ref, bf16[1536,512]{1,0:T(8,128)(2,1)} %get-tuple-element.44.m3_ref, bf16[1280,1024]{1,0:T(8,128)(2,1)} %get-tuple-element.45.l2_ref, f32[512,512]{1,0:T(8,128)} %bitcast.12, ...), custom_call_target="tpu_custom_call" | custom-call | tf_op jit(solution)/shard_map/solve_update/pallas_call | solution.py:281
  (44 shorter events, 9.2 us)
Async XLA Ops:
  6.5 13.4 %copy-start.4 = (f32[1280,32]{0,1:T(8,128)S(1)}, f32[1280,32]{0,1:T(8,128)}, u32[]{:S(2)}) copy-start(f32[1280,32]{0,1:T(8,128)} %param.4) | copy-start | bytes 491524
  6.5 77.7 %all-gather.2.cloned.1.call-start = ((), (), s32[]{:S(2)}) async-start(), calls=%async_computation.2 | async-start | bytes 3899392 | tf_op jit(solution)/shard_map/all_gather | solution.py:341
  7.5 12.4 %collective-permute-start.2 = (f32[32,512]{1,0:T(8,128)S(1)}, f32[32,512]{1,0:T(8,128)S(1)}, u32[]{:S(2)}, u32[]{:S(2)}) collective-permute-start(f32[32,512]{1,0:T(8,128)S(1)} %slice.41), channel_id=1, source_target_pairs={{0,48},{1,49},{2,50},{3,51},{4,52},{5,53},{6,54},{7,55},{8,56},{9,... | collective-permute-start | bytes 196616 | tf_op jit(solution)/shard_map/ppermute | solution.py:332
  12.1 7.8 %collective-permute-start.1 = (f32[32,512]{1,0:T(8,128)S(1)}, f32[32,512]{1,0:T(8,128)S(1)}, u32[]{:S(2)}, u32[]{:S(2)}) collective-permute-start(f32[32,512]{1,0:T(8,128)S(1)} %slice.41), channel_id=1, source_target_pairs={{0,32},{1,33},{2,34},{3,35},{4,36},{5,37},{6,38},{7,39},{8,40},{9,... | collective-permute-start | bytes 196616 | tf_op jit(solution)/shard_map/ppermute | solution.py:332
  13.4 6.5 %collective-permute-start = (f32[32,512]{1,0:T(8,128)S(1)}, f32[32,512]{1,0:T(8,128)S(1)}, u32[]{:S(2)}, u32[]{:S(2)}) collective-permute-start(f32[32,512]{1,0:T(8,128)S(1)} %slice.41), channel_id=1, source_target_pairs={{0,16},{1,17},{2,18},{3,19},{4,20},{5,21},{6,22},{7,23},{8,24},{9,... | collective-permute-start | bytes 196616 | tf_op jit(solution)/shard_map/ppermute | solution.py:332
  16.5 15.8 %copy-start = (f32[1280,512]{1,0:T(8,128)S(1)}, f32[1280,512]{1,0:T(8,128)}, u32[]{:S(2)}) copy-start(f32[1280,512]{1,0:T(8,128)} %trail_ref.4) | copy-start | bytes 7864324
  19.9 6.5 %collective-permute-start.9 = (f32[32,512]{1,0:T(8,128)S(1)}, f32[32,512]{1,0:T(8,128)S(1)}, u32[]{:S(2)}, u32[]{:S(2)}) collective-permute-start(f32[32,512]{1,0:T(8,128)S(1)} %add_select_fusion.2), channel_id=1, source_target_pairs={{0,448},{16,464},{32,480},{48,496},{1,449},{17,465},{33,481},{49,4... | collective-permute-start | bytes 196616 | tf_op jit(solution)/shard_map/ppermute | solution.py:337
  21.2 6.5 %collective-permute-start.8 = (f32[32,512]{1,0:T(8,128)S(1)}, f32[32,512]{1,0:T(8,128)S(1)}, u32[]{:S(2)}, u32[]{:S(2)}) collective-permute-start(f32[32,512]{1,0:T(8,128)S(1)} %add_select_fusion.2), channel_id=1, source_target_pairs={{0,384},{16,400},{32,416},{48,432},{1,385},{17,401},{33,417},{49,4... | collective-permute-start | bytes 196616 | tf_op jit(solution)/shard_map/ppermute | solution.py:337
  22.5 6.5 %collective-permute-start.7 = (f32[32,512]{1,0:T(8,128)S(1)}, f32[32,512]{1,0:T(8,128)S(1)}, u32[]{:S(2)}, u32[]{:S(2)}) collective-permute-start(f32[32,512]{1,0:T(8,128)S(1)} %add_select_fusion.2), channel_id=1, source_target_pairs={{0,320},{16,336},{32,352},{48,368},{1,321},{17,337},{33,353},{49,3... | collective-permute-start | bytes 196616 | tf_op jit(solution)/shard_map/ppermute | solution.py:337
  23.8 5.2 %collective-permute-start.6 = (f32[32,512]{1,0:T(8,128)S(1)}, f32[32,512]{1,0:T(8,128)S(1)}, u32[]{:S(2)}, u32[]{:S(2)}) collective-permute-start(f32[32,512]{1,0:T(8,128)S(1)} %add_select_fusion.2), channel_id=1, source_target_pairs={{0,256},{16,272},{32,288},{48,304},{1,257},{17,273},{33,289},{49,3... | collective-permute-start | bytes 196616 | tf_op jit(solution)/shard_map/ppermute | solution.py:337
  25.1 4.0 %collective-permute-start.5 = (f32[32,512]{1,0:T(8,128)S(1)}, f32[32,512]{1,0:T(8,128)S(1)}, u32[]{:S(2)}, u32[]{:S(2)}) collective-permute-start(f32[32,512]{1,0:T(8,128)S(1)} %add_select_fusion.2), channel_id=1, source_target_pairs={{0,192},{16,208},{32,224},{48,240},{1,193},{17,209},{33,225},{49,2... | collective-permute-start | bytes 196616 | tf_op jit(solution)/shard_map/ppermute | solution.py:337
  26.4 3.9 %collective-permute-start.4 = (f32[32,512]{1,0:T(8,128)S(1)}, f32[32,512]{1,0:T(8,128)S(1)}, u32[]{:S(2)}, u32[]{:S(2)}) collective-permute-start(f32[32,512]{1,0:T(8,128)S(1)} %add_select_fusion.2), channel_id=1, source_target_pairs={{0,128},{16,144},{32,160},{48,176},{1,129},{17,145},{33,161},{49,1... | collective-permute-start | bytes 196616 | tf_op jit(solution)/shard_map/ppermute | solution.py:337
  27.8 3.4 %collective-permute-start.3 = (f32[32,512]{1,0:T(8,128)S(1)}, f32[32,512]{1,0:T(8,128)S(1)}, u32[]{:S(2)}, u32[]{:S(2)}) collective-permute-start(f32[32,512]{1,0:T(8,128)S(1)} %add_select_fusion.2), channel_id=1, source_target_pairs={{0,64},{16,80},{32,96},{48,112},{1,65},{17,81},{33,97},{49,113},{2... | collective-permute-start | bytes 196616 | tf_op jit(solution)/shard_map/ppermute | solution.py:337
  31.1 9.1 %copy-start.3 = (f32[512,128]{1,0:T(8,128)S(1)}, f32[512,128]{1,0:T(8,128)}, u32[]{:S(2)}) copy-start(f32[512,128]{1,0:T(8,128)} %pick_rows.1) | copy-start | bytes 786436
  32.3 3.2 %copy-start.1 = (bf16[1024,512]{1,0:T(8,128)(2,1)}, bf16[1024,512]{1,0:T(8,128)(2,1)S(1)}, u32[]{:S(2)}) copy-start(bf16[1024,512]{1,0:T(8,128)(2,1)S(1)} %fusion.onehot_ref) | copy-start | bytes 3145732
  35.5 29.5 %collective-permute-start.10 = (f32[256,512]{1,0:T(8,128)}, f32[256,512]{1,0:T(8,128)S(1)}, u32[]{:S(2)}, u32[]{:S(2)}) collective-permute-start(f32[256,512]{1,0:T(8,128)} %get-tuple-element.31), channel_id=1, source_target_pairs={{0,16},{1,17},{2,18},{3,19},{4,20},{5,21},{6,22},{7,23},{8,24},{9,... | collective-permute-start | bytes 1572872 | tf_op jit(solution)/shard_map/ppermute | solution.py:347
  36.8 28.1 %collective-permute-start.11 = (f32[256,512]{1,0:T(8,128)}, f32[256,512]{1,0:T(8,128)S(1)}, u32[]{:S(2)}, u32[]{:S(2)}) collective-permute-start(f32[256,512]{1,0:T(8,128)} %get-tuple-element.32), channel_id=1, source_target_pairs={{0,32},{1,33},{2,34},{3,35},{4,36},{5,37},{6,38},{7,39},{8,40},{9,... | collective-permute-start | bytes 1572872 | tf_op jit(solution)/shard_map/ppermute | solution.py:347
  38.2 26.8 %collective-permute-start.12 = (f32[256,512]{1,0:T(8,128)}, f32[256,512]{1,0:T(8,128)}, u32[]{:S(2)}, u32[]{:S(2)}) collective-permute-start(f32[256,512]{1,0:T(8,128)} %get-tuple-element.33), channel_id=1, source_target_pairs={{0,48},{1,49},{2,50},{3,51},{4,52},{5,53},{6,54},{7,55},{8,56},{9,... | collective-permute-start | bytes 1572872 | tf_op jit(solution)/shard_map/ppermute | solution.py:347
  65.0 38.0 %all-to-all-start.1 = ((f32[32,16,512]{2,1,0:T(8,128)}), f32[32,16,512]{2,1,0:T(8,128)S(1)}, u32[]{:S(2)}, u32[]{:S(2)}) async-start(f32[32,16,512]{2,1,0:T(8,128)} %slots_to_order.1), calls=%async_computation.1 | async-start | bytes 2097152 | tf_op jit(solution)/shard_map/all_to_all | solution.py:351
  72.0 21.6 %collective-permute-start.17 = (f32[32,512]{1,0:T(8,128)S(1)}, f32[32,512]{1,0:T(8,128)S(1)}, u32[]{:S(2)}, u32[]{:S(2)}) collective-permute-start(f32[32,512]{1,0:T(8,128)S(1)} %get-tuple-element.49), channel_id=1, source_target_pairs={{0,320},{16,336},{32,352},{48,368},{1,321},{17,337},{33,353},{49,3... | collective-permute-start | bytes 196616 | tf_op jit(solution)/shard_map/ppermute | solution.py:355
  78.8 16.8 %collective-permute-start.16 = (f32[32,512]{1,0:T(8,128)S(1)}, f32[32,512]{1,0:T(8,128)S(1)}, u32[]{:S(2)}, u32[]{:S(2)}) collective-permute-start(f32[32,512]{1,0:T(8,128)S(1)} %get-tuple-element.50), channel_id=1, source_target_pairs={{0,256},{16,272},{32,288},{48,304},{1,257},{17,273},{33,289},{49,3... | collective-permute-start | bytes 196616 | tf_op jit(solution)/shard_map/ppermute | solution.py:355
  80.3 16.1 %collective-permute-start.15 = (f32[32,512]{1,0:T(8,128)S(1)}, f32[32,512]{1,0:T(8,128)S(1)}, u32[]{:S(2)}, u32[]{:S(2)}) collective-permute-start(f32[32,512]{1,0:T(8,128)S(1)} %get-tuple-element.51), channel_id=1, source_target_pairs={{0,192},{16,208},{32,224},{48,240},{1,193},{17,209},{33,225},{49,2... | collective-permute-start | bytes 196616 | tf_op jit(solution)/shard_map/ppermute | solution.py:355
  81.6 15.5 %collective-permute-start.14 = (f32[32,512]{1,0:T(8,128)S(1)}, f32[32,512]{1,0:T(8,128)S(1)}, u32[]{:S(2)}, u32[]{:S(2)}) collective-permute-start(f32[32,512]{1,0:T(8,128)S(1)} %get-tuple-element.52), channel_id=1, source_target_pairs={{0,128},{16,144},{32,160},{48,176},{1,129},{17,145},{33,161},{49,1... | collective-permute-start | bytes 196616 | tf_op jit(solution)/shard_map/ppermute | solution.py:355
  82.9 14.9 %collective-permute-start.13 = (f32[32,512]{1,0:T(8,128)S(1)}, f32[32,512]{1,0:T(8,128)S(1)}, u32[]{:S(2)}, u32[]{:S(2)}) collective-permute-start(f32[32,512]{1,0:T(8,128)S(1)} %get-tuple-element.53), channel_id=1, source_target_pairs={{0,64},{16,80},{32,96},{48,112},{1,65},{17,81},{33,97},{49,113},{2... | collective-permute-start | bytes 196616 | tf_op jit(solution)/shard_map/ppermute | solution.py:355
  97.8 3.2 %collective-permute-start.18 = (f32[32,512]{1,0:T(8,128)S(1)}, f32[32,512]{1,0:T(8,128)S(1)}, u32[]{:S(2)}, u32[]{:S(2)}) collective-permute-start(f32[32,512]{1,0:T(8,128)S(1)} %get-tuple-element.47), channel_id=1, source_target_pairs={{0,384},{16,400},{32,416},{48,432},{1,385},{17,401},{33,417},{49,4... | collective-permute-start | bytes 196616 | tf_op jit(solution)/shard_map/ppermute | solution.py:358
  99.1 3.2 %collective-permute-start.19 = (f32[32,512]{1,0:T(8,128)S(1)}, f32[32,512]{1,0:T(8,128)S(1)}, u32[]{:S(2)}, u32[]{:S(2)}) collective-permute-start(f32[32,512]{1,0:T(8,128)S(1)} %get-tuple-element.48), channel_id=1, source_target_pairs={{0,448},{16,464},{32,480},{48,496},{1,449},{17,465},{33,481},{49,4... | collective-permute-start | bytes 196616 | tf_op jit(solution)/shard_map/ppermute | solution.py:358
  103.0 1.0 copy-start.2
Sparse Core Ops, SparseCore 0:
  32.0 39.6 all-gather.1

commit v3 on v2

--- a/solution.py
+++ b/solution.py
@@ -9,6 +9,7 @@
 NPROW = NX * NY
 CAP = 32
 LANES = 128
+NEAR = 6
 SHARE = LANES // CAP
 PROW, PCOL = ("y", "x"), ("z", "c")
 HI = lax.Precision.HIGHEST
@@ -54,87 +55,92 @@
             pltpu.VMEM((LANES, cols), jnp.float32),
             pltpu.SemaphoreType.DMA((CAP,)),
         ],
+        cost_estimate=pl.CostEstimate(flops=0, bytes_accessed=0, transcendentals=0),
         name="pick_rows",
     )(rows, group, trailing)
 
 
-def order_kernel(slots_ref, onehot_ref, out_ref):
+def onehot(slot, start, count):
+    here = start + lax.broadcasted_iota(jnp.int32, (count, slot.shape[1]), 0)
+    return jnp.where(here == slot, 1.0, 0.0).astype(jnp.bfloat16)
+
+
+def pieces(a):
+    hi, rest = split(a)
+    mid, lo = split(a - hi.astype(jnp.float32))
+    return hi, mid, lo
+
+
+def owner_at(place):
+    if place < NX * NEAR:
+        x, y = divmod(place, NEAR)
+    else:
+        y, x = divmod(place, NX)
+    return NX * y + x
+
+
+def place_of(y, x):
+    return jnp.where(y < NEAR, x * NEAR + y, NX * y + x)
+
+
+def order_kernel(slot_ref, slots_ref, out_ref):
     owners, cols, _ = slots_ref.shape
     acc = None
     for g in range(owners // SHARE):
-        x, y = divmod(SHARE * g, NY)
-        part = slots_ref[NX * y + x]
+        part = slots_ref[owner_at(SHARE * g)]
         for i in range(1, SHARE):
-            part = part + slots_ref[NX * (y + i) + x]
-        hi, rest = split(part)
-        mid, lo = split(part - hi.astype(jnp.float32))
-        three = jnp.concatenate([hi, mid, lo], axis=0)
-        got = dot(three, onehot_ref[pl.ds(g * LANES, LANES), :], precision=None)
+            part = part + slots_ref[owner_at(SHARE * g + i)]
+        three = jnp.concatenate(pieces(part), axis=0)
+        got = dot(three, onehot(slot_ref[...], g * LANES, LANES), precision=None)
         acc = got if acc is None else acc + got
     rows = acc[:cols] + acc[cols : 2 * cols] + acc[2 * cols :]
     out_ref[...] = jnp.broadcast_to(rows[None], out_ref.shape)
 
 
-def to_order(slots, onehot):
+def to_order(slots, slot):
     owners, cols, _ = slots.shape
     return pl.pallas_call(
         order_kernel,
         in_specs=[VMEM, VMEM],
         out_specs=VMEM,
-        out_shape=jax.ShapeDtypeStruct((owners, cols, onehot.shape[1]), jnp.float32),
+        out_shape=jax.ShapeDtypeStruct((owners, cols, slot.shape[1]), jnp.float32),
+        cost_estimate=pl.CostEstimate(flops=0, bytes_accessed=0, transcendentals=0),
         name="slots_to_order",
-    )(slots, onehot)
-
-
-def tops_kernel(first_ref, onehot_ref, trail_ref, *refs):
-    outs, sems = refs[:NX], refs[NX]
-
-    def run(pick, top, rows):
-        n = top.shape[0]
-        reads = [
-            pltpu.make_async_copy(trail_ref.at[pl.ds(0, n), :], top, sems.at[0]),
-            pltpu.make_async_copy(onehot_ref, pick, sems.at[1]),
-        ]
-        for copy in reads:
-            copy.start()
-        for copy in reads:
-            copy.wait()
-        hi, rest = split(top[...])
-        mid, lo = split(top[...] - hi.astype(jnp.float32))
-        writes = []
-        for x in range(NX):
-            here = pick[pl.ds(x * NY * CAP, NY * CAP), :]
-            got = dot(here, hi, precision=None) + dot(here, mid, precision=None)
-            rows[x] = got + dot(here, lo, precision=None)
-            writes.append(pltpu.make_async_copy(rows.at[x], outs[x], sems.at[2 + x]))
-            writes[-1].start()
-        for copy in writes:
-            copy.wait()
+    )(slot, slots)
+
+
+def tops_kernel(first_ref, slot_ref, trail_ref, *refs):
+    outs, sem = refs[:-1], refs[-1]
+
+    def run(top):
+        read = pltpu.make_async_copy(trail_ref.at[pl.ds(0, top.shape[0]), :], top, sem)
+        read.start()
+        read.wait()
+        parts = pieces(top[...])
+        start = 0
+        for out in outs:
+            pick = onehot(slot_ref[...], start, out.shape[0])
+            hi, mid, lo = (dot(pick, part, precision=None) for part in parts)
+            out[...] = hi + mid + lo
+            start += out.shape[0]
 
     @pl.when(first_ref[0] == 1)
     def _():
-        slots, n = onehot_ref.shape
-        cols = trail_ref.shape[1]
-        pl.run_scoped(
-            run,
-            pltpu.VMEM((slots, n), jnp.bfloat16),
-            pltpu.VMEM((n, cols), jnp.float32),
-            pltpu.VMEM((NX, NY * CAP, cols), jnp.float32),
-        )
-
-
-def to_owners(first, onehot, trailing):
+        pl.run_scoped(run, pltpu.VMEM((slot_ref.shape[1], trail_ref.shape[1]), jnp.float32))
+
+
+def to_owners(first, slot, trailing):
     cols = trailing.shape[1]
-    hbm = pl.BlockSpec(memory_space=pl.ANY)
+    counts = [NEAR * CAP] * NX + [NX * CAP] * (NY - NEAR)
     return pl.pallas_call(
         tops_kernel,
-        in_specs=[SMEM, hbm, hbm],
-        out_specs=[hbm] * NX,
-        out_shape=[jax.ShapeDtypeStruct((NY * CAP, cols), jnp.float32)] * NX,
-        scratch_shapes=[pltpu.SemaphoreType.DMA((2 + NX,))],
-        compiler_params=pltpu.CompilerParams(vmem_limit_bytes=24 * 1024 * 1024),
+        in_specs=[SMEM, VMEM, pl.BlockSpec(memory_space=pl.ANY)],
+        out_specs=[VMEM] * len(counts),
+        out_shape=[jax.ShapeDtypeStruct((count, cols), jnp.float32) for count in counts],
+        scratch_shapes=[pltpu.SemaphoreType.DMA],
+        compiler_params=pltpu.CompilerParams(vmem_limit_bytes=16 * 1024 * 1024),
         name="tops_to_owners",
-    )(first, onehot, trailing)
+    )(first, slot, trailing)
 
 
 def invert_upper(u_ref, m_ref, between):
@@ -155,7 +161,7 @@
         else:
             half = [dot(m, q) for m, q in zip(invs, parts)]
             invs = [m - dot(h, m) for m, h in zip(invs, half)]
-        between()
+        between(s)
         s *= 2
     for b, m in enumerate(invs):
         m_ref[pl.ds(b * base, base), pl.ds(b * base, base)] = m
@@ -171,51 +177,62 @@
 TILE = 256
 
 
-def factor_kernel(full_ref, m3_ref, l2_ref, u, m, lt, sems):
+def factor_kernel(full_ref, m3_ref, l2_ref, u, m, lt, m3, l2, sems):
     n, rows = lt.shape
     get_u = pltpu.make_async_copy(full_ref.at[:, pl.ds(rows, n)], u, sems.at[0])
     get_l = pltpu.make_async_copy(full_ref.at[:, pl.ds(0, rows)], lt, sems.at[1])
     get_u.start()
+    get_u.wait()
     get_l.start()
-    get_u.wait()
 
     todo = list(range(rows // TILE))
-
-    def between():
-        if not todo:
+    puts = []
+
+    def between(s):
+        if s < 4 or not todo:
             return
         i = todo.pop(0)
         if i == 0:
             get_l.wait()
         at = pl.ds(i * TILE, TILE)
         hi, lo = split(lt[:, at].T)
-        l2_ref[at, pl.ds(0, n)] = hi
-        l2_ref[at, pl.ds(n, n)] = lo
+        l2[at, pl.ds(0, n)] = hi
+        l2[at, pl.ds(n, n)] = lo
+        puts.append(pltpu.make_async_copy(l2.at[at, :], l2_ref.at[at, :], sems.at[2 + i]))
+        puts[-1].start()
 
     invert_upper(u, m, between)
     while todo:
-        between()
+        between(n)
     hi, lo = split(m[...])
-    m3_ref[pl.ds(0, n), :] = hi
-    m3_ref[pl.ds(n, n), :] = hi
-    m3_ref[pl.ds(2 * n, n), :] = lo
+    m3[pl.ds(0, n), :] = hi
+    m3[pl.ds(n, n), :] = hi
+    m3[pl.ds(2 * n, n), :] = lo
+    puts.append(pltpu.make_async_copy(m3, m3_ref, sems.at[2 + rows // TILE]))
+    puts[-1].start()
+    for copy in puts:
+        copy.wait()
 
 
 def factor(full, rows):
     n = full.shape[0]
     f32, bf16 = jnp.float32, jnp.bfloat16
+    hbm = pl.BlockSpec(memory_space=pl.ANY)
     return pl.pallas_call(
         factor_kernel,
-        in_specs=[pl.BlockSpec(memory_space=pl.ANY)],
-        out_specs=[VMEM, VMEM],
+        in_specs=[hbm],
+        out_specs=[hbm, hbm],
         out_shape=[jax.ShapeDtypeStruct((3 * n, n), bf16), jax.ShapeDtypeStruct((rows, 2 * n), bf16)],
         scratch_shapes=[
             pltpu.VMEM((n, n), f32),
             pltpu.VMEM((n, n), f32),
             pltpu.VMEM((n, rows), f32),
-            pltpu.SemaphoreType.DMA((2,)),
+            pltpu.VMEM((3 * n, n), bf16),
+            pltpu.VMEM((rows, 2 * n), bf16),
+            pltpu.SemaphoreType.DMA((3 + rows // TILE,)),
         ],
         compiler_params=pltpu.CompilerParams(vmem_limit_bytes=56 * 1024 * 1024),
+        cost_estimate=pl.CostEstimate(flops=200_000_000_000, bytes_accessed=0, transcendentals=0),
         name="factor",
     )(full)
 
@@ -318,45 +335,51 @@
     local = pivots % rows_here
     ks = jnp.arange(block, dtype=jnp.int32)
     before = (owner[None, :] == owner[:, None]) & (ks[None, :] < ks[:, None])
-    place = (owner % NX) * NY + owner // NX
+    place = place_of(owner // NX, owner % NX)
     slot = place * CAP + jnp.sum(before.astype(jnp.int32), axis=1)
     y, x = lax.axis_index("y"), lax.axis_index("x")
-    mine = slot[None, :] == ((x * NY + y) * CAP + jnp.arange(CAP, dtype=jnp.int32))[:, None]
+    here = place_of(y, x)
+    mine = slot[None, :] == (here * CAP + jnp.arange(CAP, dtype=jnp.int32))[:, None]
     rows = jnp.sum(jnp.where(mine, local[None, :] + 1, 0), axis=1) - 1
-    slots = jnp.arange(NPROW * CAP, dtype=jnp.int32)
-    onehot = (slot[None, :] == slots[:, None]).astype(jnp.bfloat16)
-    lanes = pick(rows, (y % SHARE)[None], trailing)
+    lanes = pick(rows, (here % SHARE)[None], trailing)
 
     lt = l_panel.T
     slab = lt[:, :block]
     got = [lax.ppermute(slab, PROW, to_x(k)) for k in range(1, NX)]
     slab = jnp.where(p == 0, slab, sum(got))
-
     slab, lanes = lax.optimization_barrier((slab, lanes))
-
     got = [lax.ppermute(slab, PROW, to_y(k)) for k in range(1, NY)]
-    lanes = after(lanes, got[0])
     slab = jnp.where(p < NX, slab, sum(got))
 
     full = lax.all_gather(jnp.concatenate([lt, slab], axis=1), PCOL, axis=0, tiled=True)
 
+    tops = to_owners(first, slot[None, :], after(trailing, slab))
+    near = [lax.ppermute(tops[k], PROW, to_x(k)) for k in range(1, NX)]
+    far = [lax.ppermute(tops[NX + i], PROW, [(0, NX * (NEAR + i))]) for i in range(NY - NEAR)]
+
+    lanes = after(lanes, tops[1])
     share = lanes.reshape(NPROW, cols_here // NPROW, LANES)
     share = lax.all_to_all(share, PROW, 0, 0, tiled=True)
 
-    tops = to_owners(first, onehot, after(trailing, slab))
-    tops_x = [lax.ppermute(tops[k], PROW, to_x(k)) for k in range(1, NX)]
-
-    ct = to_order(share, onehot)
-    ct, tops_x = lax.optimization_barrier((ct, tops_x))
+    ct = to_order(share, slot[None, :])
+    near, far = lax.optimization_barrier((near, far, ct))[:2]
     ct = lax.all_to_all(ct, PROW, 0, 0, tiled=True).reshape(cols_here, block)
 
-    tops = jnp.where(p == 0, tops[0], sum(tops_x)).reshape(NY, CAP, cols_here)
-    early, late = range(1, NY - 2), range(NY - 2, NY)
-    got = [lax.ppermute(tops[k], PROW, to_y(k)) for k in early]
+    near = jnp.where(p == 0, tops[0], sum(near)).reshape(NEAR, CAP, cols_here)
+    far = sum(far).reshape(NX, CAP, cols_here)
+    got = []
+    for k in range(1, NEAR):
+        pairs = to_y(k)
+        sent = near[k]
+        if k < NX:
+            pairs = pairs + [(NX * i, NX * i + k) for i in range(NEAR, NY)]
+            sent = jnp.where(y == 0, near[k], far[k])
+        got.append(lax.ppermute(sent, PROW, pairs))
     m3, l2 = factor(full, rows_here)
-    tops, m3, got = lax.optimization_barrier((tops, m3, got))
-    got += [lax.ppermute(tops[k], PROW, to_y(k)) for k in late]
-    top = jnp.where(p < NX, tops[0], sum(got))
+    got, m3 = lax.optimization_barrier((got, m3))
+    own = jnp.where(y == 0, near[0], far[0])
+    top = jnp.where((y == 0) | ((y >= NEAR) & (x == 0)), own, sum(got))
+
     return update(rows, first, top, m3, l2, ct, trailing)
 
 

time: 119 us -> 105 us (0.88)
  the two profiles are of different devices: /device:TPU:256 before, /device:TPU:474 now
where the time goes in v3:
time: 105 us; the launch traced here: 104 us
  starting transfers between devices  33.3 us (32%)
  waiting for transfers between devices  27 us (26%)
  Pallas kernels  20.4 us (19%)
  between operations  13.9 us (13%)
  other arithmetic  5.11 us (5%)
  local copies, waits for them, and re-layouts  4.63 us (4%)
    ppermute x5, waiting for transfers between devices, on_device(): got.append(lax.ppermute(sent, PROW, pairs))  10.5 us
    ppermute x7, waiting for transfers between devices, on_device(): got = [lax.ppermute(slab, PROW, to_y(k)) for k in range(1, NY)]  9.05 us
    all_to_all x1, starting transfers between devices, on_device(): share = lax.all_to_all(share, PROW, 0, 0, tiled=True)  8.37 us
    all_to_all x1, starting transfers between devices, on_device(): ct = lax.all_to_all(ct, PROW, 0, 0, tiled=True).reshape(cols_here, block)  7.91 us
    pallas_call x1, Pallas kernels, factor(): pl.pallas_call(factor_kernel, in_specs=[hbm], out_specs=[hbm, hbm], out_s...  7.58 us
    pallas_call x1, Pallas kernels, update(): pl.pallas_call(update_kernel, in_specs=[SMEM, SMEM, VMEM, hbm, hbm, hbm,...  7.44 us
    ppermute x5, starting transfers between devices, on_device(): got.append(lax.ppermute(sent, PROW, pairs))  6.36 us
    all_to_all x1, waiting for transfers between devices, on_device(): share = lax.all_to_all(share, PROW, 0, 0, tiled=True)  6 us
  transfers between devices with their start and end apart: 23, of which 4 were waited for; matrix products, arithmetic and copies ran while one was open for 4% of the time, Pallas kernels for 12%

profile of v3, /device:TPU:474, one launch (start us, length us, event | category | flops | bytes accessed | tf_op | source)
XLA Modules:
  0.0 104.3 jit_solution(15104618241916497307)
XLA Ops:
  6.5 1.0 slice.54
  8.2 0.7 collective-permute-start.1
  9.6 0.7 add_select_fusion.6
  11.3 3.0 %pick_rows.1 = f32[512,128]{1,0:T(8,128)} custom-call(s32[32]{0:T(128)} %broadcast_add_fusion.rows_ref, s32[1]{0:T(128)} %bitcast.3.group_ref, f32[1280,512]{1,0:T(8,128)} %trail_ref.4), custom_call_target="tpu_custom_call" | custom-call | tf_op jit(solution)/shard_map/pick_rows/pallas_call | solution.py:48
  17.0 1.3 %collective-permute-start.5 = (f32[32,512]{1,0:T(8,128)S(1)}, f32[32,512]{1,0:T(8,128)S(1)}, u32[]{:S(2)}, u32[]{:S(2)}) collective-permute-start(f32[32,512]{1,0:T(8,128)S(1)} %add_select_fusion.2), channel_id=1, source_target_pairs={{0,192},{16,208},{32,224},{48,240},{1,193},{17,209},{33,225},{49,2... | collective-permute-start | bytes 196616 | tf_op jit(solution)/shard_map/ppermute | solution.py:351
  19.7 9.0 %collective-permute-done.5 = f32[32,512]{1,0:T(8,128)S(1)} collective-permute-done((f32[32,512]{1,0:T(8,128)S(1)}, f32[32,512]{1,0:T(8,128)S(1)}, u32[]{:S(2)}, u32[]{:S(2)}) %collective-permute-start.5) | collective-permute-done | bytes 65568 | tf_op jit(solution)/shard_map/ppermute | solution.py:351
  28.8 0.7 pad_maximum_fusion
  29.6 0.7 copy-done.2
  30.3 0.7 copy-done.3
  31.1 0.7 copy-done.4
  31.8 0.7 copy-done.5
  32.5 8.4 %all-to-all-start = ((f32[32,16,128]{2,1,0:T(8,128)}), f32[32,16,128]{2,1,0:T(8,128)S(1)}, u32[]{:S(2)}, u32[]{:S(2)}) async-start(f32[32,16,128]{2,1,0:T(8,128)} %bitcast.8), calls=%async_computation | async-start | bytes 524288 | tf_op jit(solution)/shard_map/all_to_all | solution.py:362
  40.9 0.7 collective-permute-start.11
  41.6 0.7 collective-permute-start.12
  42.3 0.7 collective-permute-start.10
  42.9 0.7 collective-permute-start.13
  43.6 0.7 collective-permute-start.14
  44.3 6.0 %all-to-all-done.slots_ref = f32[32,16,128]{2,1,0:T(8,128)S(1)} async-done(((f32[32,16,128]{2,1,0:T(8,128)}), f32[32,16,128]{2,1,0:T(8,128)S(1)}, u32[]{:S(2)}, u32[]{:S(2)}) %all-to-all-start) | async-done | bytes 262176 | tf_op jit(solution)/shard_map/all_to_all | solution.py:362
  50.3 0.7 copy-done.7
  51.1 2.4 %slots_to_order.1 = f32[32,16,512]{2,1,0:T(8,128)} custom-call(s32[1,512]{1,0:T(1,128)} %bitcast.7, f32[32,16,128]{2,1,0:T(8,128)} %copy-done.7), custom_call_target="tpu_custom_call" | custom-call | tf_op jit(solution)/shard_map/slots_to_order/pallas_call | solution.py:102
  53.4 7.9 %all-to-all-start.1 = ((f32[32,16,512]{2,1,0:T(8,128)}), f32[32,16,512]{2,1,0:T(8,128)}, u32[]{:S(2)}, u32[]{:S(2)}) async-start(f32[32,16,512]{2,1,0:T(8,128)} %slots_to_order.1), calls=%async_computation.1 | async-start | bytes 2097152 | tf_op jit(solution)/shard_map/all_to_all | solution.py:366
  61.6 0.8 fusion.5
  62.4 1.3 %collective-permute-start.19 = (f32[32,512]{1,0:T(8,128)}, f32[32,512]{1,0:T(8,128)}, u32[]{:S(2)}, u32[]{:S(2)}) collective-permute-start(f32[32,512]{1,0:T(8,128)} %get-tuple-element.54), channel_id=1, source_target_pairs={{0,320},{16,336},{32,352},{48,368},{1,321},{17,337},{33,353},{49,3... | collective-permute-start | bytes 196616 | tf_op jit(solution)/shard_map/ppermute | solution.py:377
  63.7 1.3 %collective-permute-start.18 = (f32[32,512]{1,0:T(8,128)}, f32[32,512]{1,0:T(8,128)}, u32[]{:S(2)}, u32[]{:S(2)}) collective-permute-start(f32[32,512]{1,0:T(8,128)} %get-tuple-element.55), channel_id=1, source_target_pairs={{0,256},{16,272},{32,288},{48,304},{1,257},{17,273},{33,289},{49,3... | collective-permute-start | bytes 196616 | tf_op jit(solution)/shard_map/ppermute | solution.py:377
  64.9 1.3 %collective-permute-start.15 = (f32[32,512]{1,0:T(8,128)}, f32[32,512]{1,0:T(8,128)}, u32[]{:S(2)}, u32[]{:S(2)}) collective-permute-start(f32[32,512]{1,0:T(8,128)} %get-tuple-element.56), channel_id=1, source_target_pairs={{0,64},{16,80},{32,96},{48,112},{384,400},{448,464},{1,65},{17,81}... | collective-permute-start | bytes 196616 | tf_op jit(solution)/shard_map/ppermute | solution.py:377
  66.2 1.3 %collective-permute-start.16 = (f32[32,512]{1,0:T(8,128)}, f32[32,512]{1,0:T(8,128)}, u32[]{:S(2)}, u32[]{:S(2)}) collective-permute-start(f32[32,512]{1,0:T(8,128)} %get-tuple-element.57), channel_id=1, source_target_pairs={{0,128},{16,144},{32,160},{48,176},{384,416},{448,480},{1,129},{17... | collective-permute-start | bytes 196616 | tf_op jit(solution)/shard_map/ppermute | solution.py:377
  67.5 1.3 %collective-permute-start.17 = (f32[32,512]{1,0:T(8,128)}, f32[32,512]{1,0:T(8,128)}, u32[]{:S(2)}, u32[]{:S(2)}) collective-permute-start(f32[32,512]{1,0:T(8,128)} %get-tuple-element.58), channel_id=1, source_target_pairs={{0,192},{16,208},{32,224},{48,240},{384,432},{448,496},{1,193},{17... | collective-permute-start | bytes 196616 | tf_op jit(solution)/shard_map/ppermute | solution.py:377
  68.8 1.5 %all-gather.2.cloned.1.call-done.full_ref = f32[512,1792]{1,0:T(8,128)} async-done(((f32[32,1792]{1,0:T(8,128)}), f32[512,1792]{1,0:T(8,128)}) %all-gather.2.cloned.1.call-update) | async-done | bytes 3670032 | tf_op jit(solution)/shard_map/all_gather | solution.py:354
  70.2 7.6 %factor.1 = (bf16[1536,512]{1,0:T(8,128)(2,1)}, bf16[1280,1024]{1,0:T(8,128)(2,1)}) custom-call(f32[512,1792]{1,0:T(8,128)} %all-gather.2.cloned.1.call-done.full_ref), custom_call_target="tpu_custom_call" | custom-call | flops 199999995904 | tf_op jit(solution)/shard_map/factor/pallas_call | solution.py:221
  77.9 10.5 %collective-permute-done.17 = f32[32,512]{1,0:T(8,128)} collective-permute-done((f32[32,512]{1,0:T(8,128)}, f32[32,512]{1,0:T(8,128)}, u32[]{:S(2)}, u32[]{:S(2)}) %collective-permute-start.17) | collective-permute-done | bytes 65568 | tf_op jit(solution)/shard_map/ppermute | solution.py:377
  88.3 1.7 %fusion.1.top_ref = f32[32,512]{1,0:T(8,128)} fusion(f32[128,512]{1,0:T(8,128)} %copy-done.8, f32[192,512]{1,0:T(8,128)} %copy-done.6, f32[32,512]{1,0:T(8,128)} %collective-permute-done.19, f32[32,512]{1,0:T(8,128)} %collective-permute-done.18, f32[32,512]{1,0:T(8,128)} %collective-permute-done.17, f32[32,512]{1,0:T(8,128)} %collective-permute-done.15, ...), kind=kLoop, calls=%fused_computation.9 | loop fusion | flops 98304 | bytes 524290 | tf_op jit(solution)/shard_map/jit(_where)/select_n | solution.py:381
  90.0 7.4 %solve_update.1 = f32[1280,512]{1,0:T(8,128)} custom-call(s32[32]{0:T(128)} %broadcast_add_fusion.rows_ref, s32[1]{0:T(128)} %bitcast.first_ref, f32[32,512]{1,0:T(8,128)} %fusion.1.top_ref, bf16[1536,512]{1,0:T(8,128)(2,1)} %get-tuple-element.49.m3_ref, bf16[1280,1024]{1,0:T(8,128)(2,1)} %get-tuple-element.50.l2_ref, f32[512,512]{1,0:T(8,128)} %bitcast.5.ct_ref, ...), custom_call_target="tpu_custom_call" | custom-call | tf_op jit(solution)/shard_map/solve_update/pallas_call | solution.py:298
  (54 shorter events, 6.7 us)
Async XLA Ops:
  6.5 7.8 %copy-start.9 = (f32[1280,32]{0,1:T(8,128)S(1)}, f32[1280,32]{0,1:T(8,128)}, u32[]{:S(2)}) copy-start(f32[1280,32]{0,1:T(8,128)} %param.4) | copy-start | bytes 491524
  6.5 23.0 %copy-start = (f32[1280,512]{1,0:T(8,128)S(1)}, f32[1280,512]{1,0:T(8,128)}, u32[]{:S(2)}) copy-start(f32[1280,512]{1,0:T(8,128)} %trail_ref.4) | copy-start | bytes 7864324
  6.5 63.7 %all-gather.2.cloned.1.call-start = ((), (), s32[]{:S(2)}) async-start(), calls=%async_computation.2 | async-start | bytes 3899392 | tf_op jit(solution)/shard_map/all_gather | solution.py:354
  7.5 6.7 %collective-permute-start.2 = (f32[32,512]{1,0:T(8,128)S(1)}, f32[32,512]{1,0:T(8,128)S(1)}, u32[]{:S(2)}, u32[]{:S(2)}) collective-permute-start(f32[32,512]{1,0:T(8,128)S(1)} %slice.54), channel_id=1, source_target_pairs={{0,48},{1,49},{2,50},{3,51},{4,52},{5,53},{6,54},{7,55},{8,56},{9,... | collective-permute-start | bytes 196616 | tf_op jit(solution)/shard_map/ppermute | solution.py:348
  8.2 6.1 %collective-permute-start.1 = (f32[32,512]{1,0:T(8,128)S(1)}, f32[32,512]{1,0:T(8,128)S(1)}, u32[]{:S(2)}, u32[]{:S(2)}) collective-permute-start(f32[32,512]{1,0:T(8,128)S(1)} %slice.54), channel_id=1, source_target_pairs={{0,32},{1,33},{2,34},{3,35},{4,36},{5,37},{6,38},{7,39},{8,40},{9,... | collective-permute-start | bytes 196616 | tf_op jit(solution)/shard_map/ppermute | solution.py:348
  8.9 5.4 %collective-permute-start = (f32[32,512]{1,0:T(8,128)S(1)}, f32[32,512]{1,0:T(8,128)S(1)}, u32[]{:S(2)}, u32[]{:S(2)}) collective-permute-start(f32[32,512]{1,0:T(8,128)S(1)} %slice.54), channel_id=1, source_target_pairs={{0,16},{1,17},{2,18},{3,19},{4,20},{5,21},{6,22},{7,23},{8,24},{9,... | collective-permute-start | bytes 196616 | tf_op jit(solution)/shard_map/ppermute | solution.py:348
  10.5 19.0 %copy-start.1 = (s32[512]{0:T(512)}, s32[512]{0:T(512)S(1)}, u32[]{:S(2)}) copy-start(s32[512]{0:T(512)S(1)} %multiply_add_fusion) | copy-start | bytes 6148
  14.3 4.0 %collective-permute-start.9 = (f32[32,512]{1,0:T(8,128)S(1)}, f32[32,512]{1,0:T(8,128)S(1)}, u32[]{:S(2)}, u32[]{:S(2)}) collective-permute-start(f32[32,512]{1,0:T(8,128)S(1)} %add_select_fusion.2), channel_id=1, source_target_pairs={{0,448},{16,464},{32,480},{48,496},{1,449},{17,465},{33,481},{49,4... | collective-permute-start | bytes 196616 | tf_op jit(solution)/shard_map/ppermute | solution.py:351
  15.0 4.0 %collective-permute-start.8 = (f32[32,512]{1,0:T(8,128)S(1)}, f32[32,512]{1,0:T(8,128)S(1)}, u32[]{:S(2)}, u32[]{:S(2)}) collective-permute-start(f32[32,512]{1,0:T(8,128)S(1)} %add_select_fusion.2), channel_id=1, source_target_pairs={{0,384},{16,400},{32,416},{48,432},{1,385},{17,401},{33,417},{49,4... | collective-permute-start | bytes 196616 | tf_op jit(solution)/shard_map/ppermute | solution.py:351
  15.7 4.0 %collective-permute-start.7 = (f32[32,512]{1,0:T(8,128)S(1)}, f32[32,512]{1,0:T(8,128)S(1)}, u32[]{:S(2)}, u32[]{:S(2)}) collective-permute-start(f32[32,512]{1,0:T(8,128)S(1)} %add_select_fusion.2), channel_id=1, source_target_pairs={{0,320},{16,336},{32,352},{48,368},{1,321},{17,337},{33,353},{49,3... | collective-permute-start | bytes 196616 | tf_op jit(solution)/shard_map/ppermute | solution.py:351
  16.3 3.4 %collective-permute-start.6 = (f32[32,512]{1,0:T(8,128)S(1)}, f32[32,512]{1,0:T(8,128)S(1)}, u32[]{:S(2)}, u32[]{:S(2)}) collective-permute-start(f32[32,512]{1,0:T(8,128)S(1)} %add_select_fusion.2), channel_id=1, source_target_pairs={{0,256},{16,272},{32,288},{48,304},{1,257},{17,273},{33,289},{49,3... | collective-permute-start | bytes 196616 | tf_op jit(solution)/shard_map/ppermute | solution.py:351
  17.0 11.7 %collective-permute-start.5 = (f32[32,512]{1,0:T(8,128)S(1)}, f32[32,512]{1,0:T(8,128)S(1)}, u32[]{:S(2)}, u32[]{:S(2)}) collective-permute-start(f32[32,512]{1,0:T(8,128)S(1)} %add_select_fusion.2), channel_id=1, source_target_pairs={{0,192},{16,208},{32,224},{48,240},{1,193},{17,209},{33,225},{49,2... | collective-permute-start | bytes 196616 | tf_op jit(solution)/shard_map/ppermute | solution.py:351
  18.3 10.4 %collective-permute-start.4 = (f32[32,512]{1,0:T(8,128)S(1)}, f32[32,512]{1,0:T(8,128)S(1)}, u32[]{:S(2)}, u32[]{:S(2)}) collective-permute-start(f32[32,512]{1,0:T(8,128)S(1)} %add_select_fusion.2), channel_id=1, source_target_pairs={{0,128},{16,144},{32,160},{48,176},{1,129},{17,145},{33,161},{49,1... | collective-permute-start | bytes 196616 | tf_op jit(solution)/shard_map/ppermute | solution.py:351
  19.0 9.7 %collective-permute-start.3 = (f32[32,512]{1,0:T(8,128)S(1)}, f32[32,512]{1,0:T(8,128)S(1)}, u32[]{:S(2)}, u32[]{:S(2)}) collective-permute-start(f32[32,512]{1,0:T(8,128)S(1)} %add_select_fusion.2), channel_id=1, source_target_pairs={{0,64},{16,80},{32,96},{48,112},{1,65},{17,81},{33,97},{49,113},{2... | collective-permute-start | bytes 196616 | tf_op jit(solution)/shard_map/ppermute | solution.py:351
  29.6 0.8 copy-start.2
  30.3 0.7 copy-start.3
  31.1 0.7 copy-start.4
  32.5 17.8 %all-to-all-start = ((f32[32,16,128]{2,1,0:T(8,128)}), f32[32,16,128]{2,1,0:T(8,128)S(1)}, u32[]{:S(2)}, u32[]{:S(2)}) async-start(f32[32,16,128]{2,1,0:T(8,128)} %bitcast.8), calls=%async_computation | async-start | bytes 524288 | tf_op jit(solution)/shard_map/all_to_all | solution.py:362
  40.9 20.5 %collective-permute-start.11 = (f32[192,512]{1,0:T(8,128)}, f32[192,512]{1,0:T(8,128)S(1)}, u32[]{:S(2)}, u32[]{:S(2)}) collective-permute-start(f32[192,512]{1,0:T(8,128)} %copy-done.3), channel_id=1, source_target_pairs={{0,32},{1,33},{2,34},{3,35},{4,36},{5,37},{6,38},{7,39},{8,40},{9,... | collective-permute-start | bytes 1179656 | tf_op jit(solution)/shard_map/ppermute | solution.py:357
  41.6 19.8 %collective-permute-start.12 = (f32[192,512]{1,0:T(8,128)}, f32[192,512]{1,0:T(8,128)S(1)}, u32[]{:S(2)}, u32[]{:S(2)}) collective-permute-start(f32[192,512]{1,0:T(8,128)} %copy-done.2), channel_id=1, source_target_pairs={{0,48},{1,49},{2,50},{3,51},{4,52},{5,53},{6,54},{7,55},{8,56},{9,... | collective-permute-start | bytes 1179656 | tf_op jit(solution)/shard_map/ppermute | solution.py:357
  42.3 19.1 %collective-permute-start.10 = (f32[192,512]{1,0:T(8,128)S(1)}, f32[192,512]{1,0:T(8,128)S(1)}, u32[]{:S(2)}, u32[]{:S(2)}) collective-permute-start(f32[192,512]{1,0:T(8,128)S(1)} %get-tuple-element.31), channel_id=1, source_target_pairs={{0,16},{1,17},{2,18},{3,19},{4,20},{5,21},{6,22},{7,23},{8,24},{9,... | collective-permute-start | bytes 1179656 | tf_op jit(solution)/shard_map/ppermute | solution.py:357
  42.9 18.4 %collective-permute-start.13 = (f32[128,512]{1,0:T(8,128)}, f32[128,512]{1,0:T(8,128)S(1)}, u32[]{:S(2)}, u32[]{:S(2)}) collective-permute-start(f32[128,512]{1,0:T(8,128)} %copy-done.5), channel_id=1, source_target_pairs={{0,384},{1,385},{2,386},{3,387},{4,388},{5,389},{6,390},{7,391},{8... | collective-permute-start | bytes 786440 | tf_op jit(solution)/shard_map/ppermute | solution.py:358
  43.6 17.7 %collective-permute-start.14 = (f32[128,512]{1,0:T(8,128)}, f32[128,512]{1,0:T(8,128)S(1)}, u32[]{:S(2)}, u32[]{:S(2)}) collective-permute-start(f32[128,512]{1,0:T(8,128)} %copy-done.4), channel_id=1, source_target_pairs={{0,448},{1,449},{2,450},{3,451},{4,452},{5,453},{6,454},{7,455},{8... | collective-permute-start | bytes 786440 | tf_op jit(solution)/shard_map/ppermute | solution.py:358
  50.3 0.7 copy-start.7
  53.4 36.6 %all-to-all-start.1 = ((f32[32,16,512]{2,1,0:T(8,128)}), f32[32,16,512]{2,1,0:T(8,128)}, u32[]{:S(2)}, u32[]{:S(2)}) async-start(f32[32,16,512]{2,1,0:T(8,128)} %slots_to_order.1), calls=%async_computation.1 | async-start | bytes 2097152 | tf_op jit(solution)/shard_map/all_to_all | solution.py:366
  61.4 16.4 %copy-start.8 = (f32[128,512]{1,0:T(8,128)}, f32[128,512]{1,0:T(8,128)S(1)}, u32[]{:S(2)}) copy-start(f32[128,512]{1,0:T(8,128)S(1)} %add.114) | copy-start | bytes 786436
  61.6 16.2 %copy-start.6 = (f32[192,512]{1,0:T(8,128)}, f32[192,512]{1,0:T(8,128)S(1)}, u32[]{:S(2)}) copy-start(f32[192,512]{1,0:T(8,128)S(1)} %add_select_fusion) | copy-start | bytes 1179652
  62.4 15.5 %collective-permute-start.19 = (f32[32,512]{1,0:T(8,128)}, f32[32,512]{1,0:T(8,128)}, u32[]{:S(2)}, u32[]{:S(2)}) collective-permute-start(f32[32,512]{1,0:T(8,128)} %get-tuple-element.54), channel_id=1, source_target_pairs={{0,320},{16,336},{32,352},{48,368},{1,321},{17,337},{33,353},{49,3... | collective-permute-start | bytes 196616 | tf_op jit(solution)/shard_map/ppermute | solution.py:377
  63.7 14.2 %collective-permute-start.18 = (f32[32,512]{1,0:T(8,128)}, f32[32,512]{1,0:T(8,128)}, u32[]{:S(2)}, u32[]{:S(2)}) collective-permute-start(f32[32,512]{1,0:T(8,128)} %get-tuple-element.55), channel_id=1, source_target_pairs={{0,256},{16,272},{32,288},{48,304},{1,257},{17,273},{33,289},{49,3... | collective-permute-start | bytes 196616 | tf_op jit(solution)/shard_map/ppermute | solution.py:377
  64.9 12.9 %collective-permute-start.15 = (f32[32,512]{1,0:T(8,128)}, f32[32,512]{1,0:T(8,128)}, u32[]{:S(2)}, u32[]{:S(2)}) collective-permute-start(f32[32,512]{1,0:T(8,128)} %get-tuple-element.56), channel_id=1, source_target_pairs={{0,64},{16,80},{32,96},{48,112},{384,400},{448,464},{1,65},{17,81}... | collective-permute-start | bytes 196616 | tf_op jit(solution)/shard_map/ppermute | solution.py:377
  66.2 11.7 %collective-permute-start.16 = (f32[32,512]{1,0:T(8,128)}, f32[32,512]{1,0:T(8,128)}, u32[]{:S(2)}, u32[]{:S(2)}) collective-permute-start(f32[32,512]{1,0:T(8,128)} %get-tuple-element.57), channel_id=1, source_target_pairs={{0,128},{16,144},{32,160},{48,176},{384,416},{448,480},{1,129},{17... | collective-permute-start | bytes 196616 | tf_op jit(solution)/shard_map/ppermute | solution.py:377
  67.5 20.9 %collective-permute-start.17 = (f32[32,512]{1,0:T(8,128)}, f32[32,512]{1,0:T(8,128)}, u32[]{:S(2)}, u32[]{:S(2)}) collective-permute-start(f32[32,512]{1,0:T(8,128)} %get-tuple-element.58), channel_id=1, source_target_pairs={{0,192},{16,208},{32,224},{48,240},{384,432},{448,496},{1,193},{17... | collective-permute-start | bytes 196616 | tf_op jit(solution)/shard_map/ppermute | solution.py:377
  (1 other events, 0.7 us)
Sparse Core Ops, SparseCore 0:
  29.7 40.5 all-gather.1

commit v4 on v3

--- a/solution.py
+++ b/solution.py
@@ -110,35 +110,49 @@
 
 
 def tops_kernel(first_ref, slot_ref, trail_ref, *refs):
-    outs, sem = refs[:-1], refs[-1]
-
-    def run(top):
-        read = pltpu.make_async_copy(trail_ref.at[pl.ds(0, top.shape[0]), :], top, sem)
+    blocks = NX + NY - NEAR
+    outs, sems = refs[:blocks], refs[blocks]
+
+    def run(top, rows):
+        read = pltpu.make_async_copy(trail_ref.at[pl.ds(0, top.shape[0]), :], top, sems.at[blocks])
         read.start()
         read.wait()
         parts = pieces(top[...])
+        writes = []
         start = 0
-        for out in outs:
-            pick = onehot(slot_ref[...], start, out.shape[0])
+        for b, out in enumerate(outs):
+            count = out.shape[0]
+            pick = onehot(slot_ref[...], start, count)
             hi, mid, lo = (dot(pick, part, precision=None) for part in parts)
-            out[...] = hi + mid + lo
-            start += out.shape[0]
+            rows[pl.ds(start, count), :] = hi + mid + lo
+            writes.append(pltpu.make_async_copy(rows.at[pl.ds(start, count), :], out, sems.at[b]))
+            writes[-1].start()
+            start += count
+        for copy in writes:
+            copy.wait()
 
     @pl.when(first_ref[0] == 1)
     def _():
-        pl.run_scoped(run, pltpu.VMEM((slot_ref.shape[1], trail_ref.shape[1]), jnp.float32))
+        n, cols = slot_ref.shape[1], trail_ref.shape[1]
+        pl.run_scoped(
+            run,
+            pltpu.VMEM((n, cols), jnp.float32),
+            pltpu.VMEM((NPROW * CAP, cols), jnp.float32),
+        )
 
 
 def to_owners(first, slot, trailing):
     cols = trailing.shape[1]
+    hbm = pl.BlockSpec(memory_space=pltpu.HBM)
     counts = [NEAR * CAP] * NX + [NX * CAP] * (NY - NEAR)
     return pl.pallas_call(
         tops_kernel,
         in_specs=[SMEM, VMEM, pl.BlockSpec(memory_space=pl.ANY)],
-        out_specs=[VMEM] * len(counts),
-        out_shape=[jax.ShapeDtypeStruct((count, cols), jnp.float32) for count in counts],
-        scratch_shapes=[pltpu.SemaphoreType.DMA],
-        compiler_params=pltpu.CompilerParams(vmem_limit_bytes=16 * 1024 * 1024),
+        out_specs=[hbm] * len(counts),
+        out_shape=[pltpu.HBM((count, cols), jnp.float32) for count in counts],
+        scratch_shapes=[pltpu.SemaphoreType.DMA((len(counts) + 1,))],
+        compiler_params=pltpu.CompilerParams(vmem_limit_bytes=24 * 1024 * 1024),
+        cost_estimate=pl.CostEstimate(flops=20_000_000_000, bytes_accessed=0, transcendentals=0),
         name="tops_to_owners",
     )(first, slot, trailing)
 
@@ -237,15 +251,19 @@
     )(full)
 
 
-def update_kernel(
-    rows_ref, first_ref, top_ref, m3_ref, l2_ref, ct_ref, trail_ref, out_ref, m3, l2, ct, x3, here, sems
-):
+def update_kernel(rows_ref, flags_ref, *refs):
+    parts, refs = refs[:NEAR], refs[NEAR:]
+    m3_ref, l2_ref, ct_ref, trail_ref, out_ref, m3, l2, ct, x3, here, top, sems = refs
     rows, n = l2.shape[0], ct.shape[1]
     tiles, late = rows // TILE, n // TILE
     sources = ((ct_ref, ct), (m3_ref, m3), (trail_ref, here), (l2_ref, l2))
     gets = [pltpu.make_async_copy(a, b, sems.at[tiles + i]) for i, (a, b) in enumerate(sources)]
     for copy in gets:
         copy.start()
+    received = parts[1][...]
+    for part in parts[2:]:
+        received = received + part[...]
+    top[...] = jnp.where(flags_ref[1] == 1, parts[0][...], received)
     gets[0].wait()
     gets[1].wait()
     hi, lo = split(ct[...])
@@ -261,7 +279,7 @@
 
         @pl.when(row >= 0)
         def _(r=r, row=row):
-            here[pl.ds(row, 1), :] = top_ref[pl.ds(r, 1), :]
+            here[pl.ds(row, 1), :] = top[pl.ds(r, 1), :]
 
     gets[3].wait()
     puts = []
@@ -280,7 +298,7 @@
         if i >= late:
             put(i)
 
-    @pl.when(first_ref[0] == 1)
+    @pl.when(flags_ref[0] == 1)
     def _():
         here[pl.ds(0, n), :] = xt.T
 
@@ -290,14 +308,14 @@
         copy.wait()
 
 
-def update(rows, first, top, m3, l2, ct, trailing):
+def update(rows, flags, parts, m3, l2, ct, trailing):
     height, cols = trailing.shape
     n = ct.shape[1]
     hbm = pl.BlockSpec(memory_space=pl.ANY)
     f32, bf16 = jnp.float32, jnp.bfloat16
     return pl.pallas_call(
         update_kernel,
-        in_specs=[SMEM, SMEM, VMEM, hbm, hbm, hbm, hbm],
+        in_specs=[SMEM, SMEM] + [VMEM] * len(parts) + [hbm] * 4,
         out_specs=hbm,
         out_shape=jax.ShapeDtypeStruct(trailing.shape, f32),
         scratch_shapes=[
@@ -306,19 +324,19 @@
             pltpu.VMEM(ct.shape, f32),
             pltpu.VMEM((cols, 3 * n), bf16),
             pltpu.VMEM((height, cols), f32),
+            pltpu.VMEM((CAP, cols), f32),
             pltpu.SemaphoreType.DMA((height // TILE + 4,)),
         ],
         compiler_params=pltpu.CompilerParams(vmem_limit_bytes=56 * 1024 * 1024),
         name="solve_update",
-    )(rows, first, top, m3, l2, ct, trailing)
-
-
-def to_x(k):
-    return [(0, k)]
-
-
-def to_y(k):
-    return [(x, NX * k + x) for x in range(NX)]
+    )(rows, flags, *parts, m3, l2, ct, trailing)
+
+
+def from_hubs(k):
+    pairs = [(x, NX * k + x) for x in range(NX)]
+    if k < NX:
+        pairs += [(NX * y, NX * y + k) for y in range(NEAR, NY)]
+    return pairs
 
 
 def after(value, *others):
@@ -341,20 +359,23 @@
     here = place_of(y, x)
     mine = slot[None, :] == (here * CAP + jnp.arange(CAP, dtype=jnp.int32))[:, None]
     rows = jnp.sum(jnp.where(mine, local[None, :] + 1, 0), axis=1) - 1
-    lanes = pick(rows, (here % SHARE)[None], trailing)
+    hub = (y == 0) | ((y >= NEAR) & (x == 0))
 
     lt = l_panel.T
     slab = lt[:, :block]
-    got = [lax.ppermute(slab, PROW, to_x(k)) for k in range(1, NX)]
+    got = [lax.ppermute(slab, PROW, [(0, k)]) for k in range(1, NX)]
     slab = jnp.where(p == 0, slab, sum(got))
+    lanes = pick(rows, (here % SHARE)[None], trailing)
     slab, lanes = lax.optimization_barrier((slab, lanes))
-    got = [lax.ppermute(slab, PROW, to_y(k)) for k in range(1, NY)]
-    slab = jnp.where(p < NX, slab, sum(got))
+    got = [lax.ppermute(slab, PROW, [(x0, NX * k + x0) for x0 in range(NX)]) for k in range(1, NY)]
+    slab = jnp.where(y == 0, slab, sum(got))
+
+    tops = to_owners(first, slot[None, :], after(trailing, lanes))
+    slab = after(slab, tops[1])
 
     full = lax.all_gather(jnp.concatenate([lt, slab], axis=1), PCOL, axis=0, tiled=True)
 
-    tops = to_owners(first, slot[None, :], after(trailing, slab))
-    near = [lax.ppermute(tops[k], PROW, to_x(k)) for k in range(1, NX)]
+    near = [lax.ppermute(tops[k], PROW, [(0, k)]) for k in range(1, NX)]
     far = [lax.ppermute(tops[NX + i], PROW, [(0, NX * (NEAR + i))]) for i in range(NY - NEAR)]
 
     lanes = after(lanes, tops[1])
@@ -369,18 +390,14 @@
     far = sum(far).reshape(NX, CAP, cols_here)
     got = []
     for k in range(1, NEAR):
-        pairs = to_y(k)
-        sent = near[k]
-        if k < NX:
-            pairs = pairs + [(NX * i, NX * i + k) for i in range(NEAR, NY)]
-            sent = jnp.where(y == 0, near[k], far[k])
-        got.append(lax.ppermute(sent, PROW, pairs))
+        sent = jnp.where(y == 0, near[k], far[k]) if k < NX else near[k]
+        got.append(lax.ppermute(sent, PROW, from_hubs(k)))
+
     m3, l2 = factor(full, rows_here)
     got, m3 = lax.optimization_barrier((got, m3))
     own = jnp.where(y == 0, near[0], far[0])
-    top = jnp.where((y == 0) | ((y >= NEAR) & (x == 0)), own, sum(got))
-
-    return update(rows, first, top, m3, l2, ct, trailing)
+    flags = jnp.stack([first[0], hub.astype(jnp.int32)])
+    return update(rows, flags, [own] + got, m3, l2, ct, trailing)
 
 
 def solution(mesh):

time: 105 us -> 103 us (0.981)
  the two profiles are of different devices: /device:TPU:474 before, /device:TPU:1 now
where the time goes in v4:
time: 103 us; the launch traced here: 102 us
  starting transfers between devices  46.4 us (45%)
  Pallas kernels  23.7 us (23%)
  between operations  13.9 us (13%)
  waiting for transfers between devices  12.1 us (12%)
  other arithmetic  4.05 us (4%)
  local copies, waits for them, and re-layouts  1.72 us (2%)
    ppermute x5, starting transfers between devices, on_device(): got.append(lax.ppermute(sent, PROW, from_hubs(k)))  10.3 us
    ppermute x7, starting transfers between devices, on_device(): lax.ppermute(slab, PROW, [(x0, NX * k + x0) for x0 in range(NX)])  9.05 us
    all_gather x1, waiting for transfers between devices, on_device(): lax.all_gather(jnp.concatenate([lt, slab], axis=1), PCOL, axis=0, tiled=T...  8.49 us
    pallas_call x1, Pallas kernels, update(): pl.pallas_call(update_kernel, in_specs=[SMEM, SMEM] + [VMEM] * len(parts)...  7.94 us
    ppermute x3, starting transfers between devices, on_device(): got = [lax.ppermute(slab, PROW, [(0, k)]) for k in range(1, NX)]  7.79 us
    pallas_call x1, Pallas kernels, factor(): pl.pallas_call(factor_kernel, in_specs=[hbm], out_specs=[hbm, hbm], out_s...  7.59 us
    ppermute x3, starting transfers between devices, on_device(): near = [lax.ppermute(tops[k], PROW, [(0, k)]) for k in range(1, NX)]  6.66 us
    all_to_all x1, starting transfers between devices, on_device(): share = lax.all_to_all(share, PROW, 0, 0, tiled=True)  5.37 us
  transfers between devices with their start and end apart: 23, of which 3 were waited for; matrix products, arithmetic and copies ran while one was open for 3% of the time, Pallas kernels for 16%

profile of v4, /device:TPU:1, one launch (start us, length us, event | category | flops | bytes accessed | tf_op | source)
XLA Modules:
  0.0 101.9 jit_solution(9606486458364454732)
XLA Ops:
  6.5 1.0 slice.54
  7.5 5.2 %collective-permute-start.2 = (f32[32,512]{1,0:T(8,128)S(1)}, f32[32,512]{1,0:T(8,128)S(1)}, u32[]{:S(2)}, u32[]{:S(2)}) collective-permute-start(f32[32,512]{1,0:T(8,128)S(1)} %slice.54), channel_id=1, source_target_pairs={{0,48},{1,49},{2,50},{3,51},{4,52},{5,53},{6,54},{7,55},{8,56},{9,... | collective-permute-start | bytes 196616 | tf_op jit(solution)/shard_map/ppermute | solution.py:366
  12.7 1.3 %collective-permute-start = (f32[32,512]{1,0:T(8,128)S(1)}, f32[32,512]{1,0:T(8,128)S(1)}, u32[]{:S(2)}, u32[]{:S(2)}) collective-permute-start(f32[32,512]{1,0:T(8,128)S(1)} %slice.54), channel_id=1, source_target_pairs={{0,16},{1,17},{2,18},{3,19},{4,20},{5,21},{6,22},{7,23},{8,24},{9,... | collective-permute-start | bytes 196616 | tf_op jit(solution)/shard_map/ppermute | solution.py:366
  14.0 1.3 %collective-permute-start.1 = (f32[32,512]{1,0:T(8,128)S(1)}, f32[32,512]{1,0:T(8,128)S(1)}, u32[]{:S(2)}, u32[]{:S(2)}) collective-permute-start(f32[32,512]{1,0:T(8,128)S(1)} %slice.54), channel_id=1, source_target_pairs={{0,32},{1,33},{2,34},{3,35},{4,36},{5,37},{6,38},{7,39},{8,40},{9,... | collective-permute-start | bytes 196616 | tf_op jit(solution)/shard_map/ppermute | solution.py:366
  17.1 3.1 %pick_rows.1 = f32[512,128]{1,0:T(8,128)} custom-call(s32[32]{0:T(128)} %broadcast_add_fusion.rows_ref, s32[1]{0:T(128)} %bitcast.4.group_ref, f32[1280,512]{1,0:T(8,128)} %refs_9_.1), custom_call_target="tpu_custom_call" | custom-call | tf_op jit(solution)/shard_map/pick_rows/pallas_call | solution.py:48
  20.3 1.3 %collective-permute-start.19 = (f32[32,512]{1,0:T(8,128)S(1)}, f32[32,512]{1,0:T(8,128)S(1)}, u32[]{:S(2)}, u32[]{:S(2)}) collective-permute-start(f32[32,512]{1,0:T(8,128)S(1)} %add_select_fusion.2), channel_id=1, source_target_pairs={{0,448},{16,464},{32,480},{48,496},{1,449},{17,465},{33,481},{49,4... | collective-permute-start | bytes 196616 | tf_op jit(solution)/shard_map/ppermute | solution.py:370
  21.6 1.3 %collective-permute-start.18 = (f32[32,512]{1,0:T(8,128)S(1)}, f32[32,512]{1,0:T(8,128)S(1)}, u32[]{:S(2)}, u32[]{:S(2)}) collective-permute-start(f32[32,512]{1,0:T(8,128)S(1)} %add_select_fusion.2), channel_id=1, source_target_pairs={{0,384},{16,400},{32,416},{48,432},{1,385},{17,401},{33,417},{49,4... | collective-permute-start | bytes 196616 | tf_op jit(solution)/shard_map/ppermute | solution.py:370
  22.9 1.3 %collective-permute-start.17 = (f32[32,512]{1,0:T(8,128)S(1)}, f32[32,512]{1,0:T(8,128)S(1)}, u32[]{:S(2)}, u32[]{:S(2)}) collective-permute-start(f32[32,512]{1,0:T(8,128)S(1)} %add_select_fusion.2), channel_id=1, source_target_pairs={{0,320},{16,336},{32,352},{48,368},{1,321},{17,337},{33,353},{49,3... | collective-permute-start | bytes 196616 | tf_op jit(solution)/shard_map/ppermute | solution.py:370
  24.2 1.3 %collective-permute-start.16 = (f32[32,512]{1,0:T(8,128)S(1)}, f32[32,512]{1,0:T(8,128)S(1)}, u32[]{:S(2)}, u32[]{:S(2)}) collective-permute-start(f32[32,512]{1,0:T(8,128)S(1)} %add_select_fusion.2), channel_id=1, source_target_pairs={{0,256},{16,272},{32,288},{48,304},{1,257},{17,273},{33,289},{49,3... | collective-permute-start | bytes 196616 | tf_op jit(solution)/shard_map/ppermute | solution.py:370
  25.5 1.3 %collective-permute-start.15 = (f32[32,512]{1,0:T(8,128)S(1)}, f32[32,512]{1,0:T(8,128)S(1)}, u32[]{:S(2)}, u32[]{:S(2)}) collective-permute-start(f32[32,512]{1,0:T(8,128)S(1)} %add_select_fusion.2), channel_id=1, source_target_pairs={{0,192},{16,208},{32,224},{48,240},{1,193},{17,209},{33,225},{49,2... | collective-permute-start | bytes 196616 | tf_op jit(solution)/shard_map/ppermute | solution.py:370
  26.8 1.3 %collective-permute-start.13 = (f32[32,512]{1,0:T(8,128)S(1)}, f32[32,512]{1,0:T(8,128)S(1)}, u32[]{:S(2)}, u32[]{:S(2)}) collective-permute-start(f32[32,512]{1,0:T(8,128)S(1)} %add_select_fusion.2), channel_id=1, source_target_pairs={{0,64},{16,80},{32,96},{48,112},{1,65},{17,81},{33,97},{49,113},{2... | collective-permute-start | bytes 196616 | tf_op jit(solution)/shard_map/ppermute | solution.py:370
  28.1 1.3 %collective-permute-start.14 = (f32[32,512]{1,0:T(8,128)S(1)}, f32[32,512]{1,0:T(8,128)S(1)}, u32[]{:S(2)}, u32[]{:S(2)}) collective-permute-start(f32[32,512]{1,0:T(8,128)S(1)} %add_select_fusion.2), channel_id=1, source_target_pairs={{0,128},{16,144},{32,160},{48,176},{1,129},{17,145},{33,161},{49,1... | collective-permute-start | bytes 196616 | tf_op jit(solution)/shard_map/ppermute | solution.py:370
  29.4 2.7 %tops_to_owners.1 = (f32[192,512]{1,0:T(8,128)}, f32[192,512]{1,0:T(8,128)}, f32[192,512]{1,0:T(8,128)}, f32[192,512]{1,0:T(8,128)}, f32[128,512]{1,0:T(8,128)}, /*index=5*/f32[128,512]{1,0:T(8,128)}) custom-call(s32[1]{0:T(128)} %bitcast.first_ref, s32[1,512]{1,0:T(1,128)S(1)} %bitcast.7, f32[1280,512]{1,0:T(8,128)S(1)} %copy-done), custom_call_target="tpu_custom_call" | custom-call | flops 20000000000 | tf_op jit(solution)/shard_map/tops_to_owners/pallas_call | solution.py:148
  32.3 0.7 pad_maximum_fusion
  33.0 5.4 %all-to-all-start = ((f32[32,16,128]{2,1,0:T(8,128)}), f32[32,16,128]{2,1,0:T(8,128)S(1)}, u32[]{:S(2)}, u32[]{:S(2)}) async-start(f32[32,16,128]{2,1,0:T(8,128)} %bitcast.5), calls=%async_computation | async-start | bytes 524288 | tf_op jit(solution)/shard_map/all_to_all | solution.py:383
  38.4 3.2 %collective-permute-start.3 = (f32[192,512]{1,0:T(8,128)}, f32[192,512]{1,0:T(8,128)S(1)}, u32[]{:S(2)}, u32[]{:S(2)}) collective-permute-start(f32[192,512]{1,0:T(8,128)} %get-tuple-element.32), channel_id=1, source_target_pairs={{0,16},{1,17},{2,18},{3,19},{4,20},{5,21},{6,22},{7,23},{8,24},{9,... | collective-permute-start | bytes 1179656 | tf_op jit(solution)/shard_map/ppermute | solution.py:378
  41.6 2.2 %collective-permute-start.4 = (f32[192,512]{1,0:T(8,128)}, f32[192,512]{1,0:T(8,128)S(1)}, u32[]{:S(2)}, u32[]{:S(2)}) collective-permute-start(f32[192,512]{1,0:T(8,128)} %get-tuple-element.33), channel_id=1, source_target_pairs={{0,32},{1,33},{2,34},{3,35},{4,36},{5,37},{6,38},{7,39},{8,40},{9,... | collective-permute-start | bytes 1179656 | tf_op jit(solution)/shard_map/ppermute | solution.py:378
  43.8 1.3 %collective-permute-start.5 = (f32[192,512]{1,0:T(8,128)}, f32[192,512]{1,0:T(8,128)S(1)}, u32[]{:S(2)}, u32[]{:S(2)}) collective-permute-start(f32[192,512]{1,0:T(8,128)} %get-tuple-element.34), channel_id=1, source_target_pairs={{0,48},{1,49},{2,50},{3,51},{4,52},{5,53},{6,54},{7,55},{8,56},{9,... | collective-permute-start | bytes 1179656 | tf_op jit(solution)/shard_map/ppermute | solution.py:378
  45.1 1.3 %collective-permute-start.6 = (f32[128,512]{1,0:T(8,128)}, f32[128,512]{1,0:T(8,128)S(1)}, u32[]{:S(2)}, u32[]{:S(2)}) collective-permute-start(f32[128,512]{1,0:T(8,128)} %get-tuple-element.35), channel_id=1, source_target_pairs={{0,384},{1,385},{2,386},{3,387},{4,388},{5,389},{6,390},{7,391},{8... | collective-permute-start | bytes 786440 | tf_op jit(solution)/shard_map/ppermute | solution.py:379
  46.4 1.3 %collective-permute-start.7 = (f32[128,512]{1,0:T(8,128)}, f32[128,512]{1,0:T(8,128)S(1)}, u32[]{:S(2)}, u32[]{:S(2)}) collective-permute-start(f32[128,512]{1,0:T(8,128)} %get-tuple-element.36), channel_id=1, source_target_pairs={{0,448},{1,449},{2,450},{3,451},{4,452},{5,453},{6,454},{7,455},{8... | collective-permute-start | bytes 786440 | tf_op jit(solution)/shard_map/ppermute | solution.py:379
  49.5 2.4 %slots_to_order.1 = f32[32,16,512]{2,1,0:T(8,128)} custom-call(s32[1,512]{1,0:T(1,128)} %bitcast.8, f32[32,16,128]{2,1,0:T(8,128)} %copy-done.2), custom_call_target="tpu_custom_call" | custom-call | tf_op jit(solution)/shard_map/slots_to_order/pallas_call | solution.py:102
  51.9 4.7 %all-to-all-start.1 = ((f32[32,16,512]{2,1,0:T(8,128)}), f32[32,16,512]{2,1,0:T(8,128)}, u32[]{:S(2)}, u32[]{:S(2)}) async-start(f32[32,16,512]{2,1,0:T(8,128)} %slots_to_order.1), calls=%async_computation.1 | async-start | bytes 2097152 | tf_op jit(solution)/shard_map/all_to_all | solution.py:387
  56.6 3.1 %collective-permute-done.4 = f32[192,512]{1,0:T(8,128)S(1)} collective-permute-done((f32[192,512]{1,0:T(8,128)}, f32[192,512]{1,0:T(8,128)S(1)}, u32[]{:S(2)}, u32[]{:S(2)}) %collective-permute-start.4) | collective-permute-done | bytes 393248 | tf_op jit(solution)/shard_map/ppermute | solution.py:378
  59.9 0.8 fusion.4
  60.7 1.9 %collective-permute-start.8 = (f32[32,512]{1,0:T(8,128)}, f32[32,512]{1,0:T(8,128)}, u32[]{:S(2)}, u32[]{:S(2)}) collective-permute-start(f32[32,512]{1,0:T(8,128)} %get-tuple-element.60), channel_id=1, source_target_pairs={{0,64},{16,80},{32,96},{48,112},{384,400},{448,464},{1,65},{17,81}... | collective-permute-start | bytes 196616 | tf_op jit(solution)/shard_map/ppermute | solution.py:394
  62.6 1.9 %collective-permute-start.9 = (f32[32,512]{1,0:T(8,128)}, f32[32,512]{1,0:T(8,128)}, u32[]{:S(2)}, u32[]{:S(2)}) collective-permute-start(f32[32,512]{1,0:T(8,128)} %get-tuple-element.61), channel_id=1, source_target_pairs={{0,128},{16,144},{32,160},{48,176},{384,416},{448,480},{1,129},{17... | collective-permute-start | bytes 196616 | tf_op jit(solution)/shard_map/ppermute | solution.py:394
  64.5 1.9 %collective-permute-start.10 = (f32[32,512]{1,0:T(8,128)}, f32[32,512]{1,0:T(8,128)}, u32[]{:S(2)}, u32[]{:S(2)}) collective-permute-start(f32[32,512]{1,0:T(8,128)} %get-tuple-element.62), channel_id=1, source_target_pairs={{0,192},{16,208},{32,224},{48,240},{384,432},{448,496},{1,193},{17... | collective-permute-start | bytes 196616 | tf_op jit(solution)/shard_map/ppermute | solution.py:394
  66.4 2.6 %collective-permute-start.11 = (f32[32,512]{1,0:T(8,128)}, f32[32,512]{1,0:T(8,128)}, u32[]{:S(2)}, u32[]{:S(2)}) collective-permute-start(f32[32,512]{1,0:T(8,128)} %get-tuple-element.58), channel_id=1, source_target_pairs={{0,256},{16,272},{32,288},{48,304},{1,257},{17,273},{33,289},{49,3... | collective-permute-start | bytes 196616 | tf_op jit(solution)/shard_map/ppermute | solution.py:394
  69.0 1.9 %collective-permute-start.12 = (f32[32,512]{1,0:T(8,128)}, f32[32,512]{1,0:T(8,128)}, u32[]{:S(2)}, u32[]{:S(2)}) collective-permute-start(f32[32,512]{1,0:T(8,128)} %get-tuple-element.57), channel_id=1, source_target_pairs={{0,320},{16,336},{32,352},{48,368},{1,321},{17,337},{33,353},{49,3... | collective-permute-start | bytes 196616 | tf_op jit(solution)/shard_map/ppermute | solution.py:394
  70.9 8.5 %all-gather.2.cloned.1.call-done.full_ref = f32[512,1792]{1,0:T(8,128)} async-done(((f32[32,1792]{1,0:T(8,128)}), f32[512,1792]{1,0:T(8,128)}) %all-gather.2.cloned.1.call-update) | async-done | bytes 3670032 | tf_op jit(solution)/shard_map/all_gather | solution.py:376
  79.4 7.6 %factor.1 = (bf16[1536,512]{1,0:T(8,128)(2,1)}, bf16[1280,1024]{1,0:T(8,128)(2,1)}) custom-call(f32[512,1792]{1,0:T(8,128)} %all-gather.2.cloned.1.call-done.full_ref), custom_call_target="tpu_custom_call" | custom-call | flops 199999995904 | tf_op jit(solution)/shard_map/factor/pallas_call | solution.py:235
  87.1 7.9 %solve_update.1 = f32[1280,512]{1,0:T(8,128)} custom-call(s32[32]{0:T(128)} %broadcast_add_fusion.rows_ref, s32[2]{0:T(128)} %pad_add_fusion.flags_ref, f32[32,512]{1,0:T(8,128)} %get-tuple-element.59.refs_0_, f32[32,512]{1,0:T(8,128)} %collective-permute-done.8.refs_1_, f32[32,512]{1,0:T(8,128)} %collective-permute-done.9.refs_2_, ...), custom_call_target="tpu_custom_call" | custom-call | tf_op jit(solution)/shard_map/solve_update/pallas_call | solution.py:316
  (44 shorter events, 3.8 us)
Async XLA Ops:
  6.5 13.7 %copy-start.3 = (f32[1280,32]{0,1:T(8,128)S(1)}, f32[1280,32]{0,1:T(8,128)}, u32[]{:S(2)}) copy-start(f32[1280,32]{0,1:T(8,128)} %param.4) | copy-start | bytes 491524
  6.5 22.9 %copy-start = (f32[1280,512]{1,0:T(8,128)S(1)}, f32[1280,512]{1,0:T(8,128)}, u32[]{:S(2)}) copy-start(f32[1280,512]{1,0:T(8,128)} %refs_9_.1) | copy-start | bytes 7864324
  6.5 72.9 %all-gather.2.cloned.1.call-start = ((), (), s32[]{:S(2)}) async-start(), calls=%async_computation.2 | async-start | bytes 3899392 | tf_op jit(solution)/shard_map/all_gather | solution.py:376
  7.5 12.7 %collective-permute-start.2 = (f32[32,512]{1,0:T(8,128)S(1)}, f32[32,512]{1,0:T(8,128)S(1)}, u32[]{:S(2)}, u32[]{:S(2)}) collective-permute-start(f32[32,512]{1,0:T(8,128)S(1)} %slice.54), channel_id=1, source_target_pairs={{0,48},{1,49},{2,50},{3,51},{4,52},{5,53},{6,54},{7,55},{8,56},{9,... | collective-permute-start | bytes 196616 | tf_op jit(solution)/shard_map/ppermute | solution.py:366
  12.7 7.5 %collective-permute-start = (f32[32,512]{1,0:T(8,128)S(1)}, f32[32,512]{1,0:T(8,128)S(1)}, u32[]{:S(2)}, u32[]{:S(2)}) collective-permute-start(f32[32,512]{1,0:T(8,128)S(1)} %slice.54), channel_id=1, source_target_pairs={{0,16},{1,17},{2,18},{3,19},{4,20},{5,21},{6,22},{7,23},{8,24},{9,... | collective-permute-start | bytes 196616 | tf_op jit(solution)/shard_map/ppermute | solution.py:366
  14.0 6.2 %collective-permute-start.1 = (f32[32,512]{1,0:T(8,128)S(1)}, f32[32,512]{1,0:T(8,128)S(1)}, u32[]{:S(2)}, u32[]{:S(2)}) collective-permute-start(f32[32,512]{1,0:T(8,128)S(1)} %slice.54), channel_id=1, source_target_pairs={{0,32},{1,33},{2,34},{3,35},{4,36},{5,37},{6,38},{7,39},{8,40},{9,... | collective-permute-start | bytes 196616 | tf_op jit(solution)/shard_map/ppermute | solution.py:366
  16.3 15.9 %copy-start.1 = (s32[512]{0:T(512)}, s32[512]{0:T(512)S(1)}, u32[]{:S(2)}) copy-start(s32[512]{0:T(512)S(1)} %multiply_add_fusion) | copy-start | bytes 6148
  20.3 6.5 %collective-permute-start.19 = (f32[32,512]{1,0:T(8,128)S(1)}, f32[32,512]{1,0:T(8,128)S(1)}, u32[]{:S(2)}, u32[]{:S(2)}) collective-permute-start(f32[32,512]{1,0:T(8,128)S(1)} %add_select_fusion.2), channel_id=1, source_target_pairs={{0,448},{16,464},{32,480},{48,496},{1,449},{17,465},{33,481},{49,4... | collective-permute-start | bytes 196616 | tf_op jit(solution)/shard_map/ppermute | solution.py:370
  21.6 6.5 %collective-permute-start.18 = (f32[32,512]{1,0:T(8,128)S(1)}, f32[32,512]{1,0:T(8,128)S(1)}, u32[]{:S(2)}, u32[]{:S(2)}) collective-permute-start(f32[32,512]{1,0:T(8,128)S(1)} %add_select_fusion.2), channel_id=1, source_target_pairs={{0,384},{16,400},{32,416},{48,432},{1,385},{17,401},{33,417},{49,4... | collective-permute-start | bytes 196616 | tf_op jit(solution)/shard_map/ppermute | solution.py:370
  22.9 9.3 %collective-permute-start.17 = (f32[32,512]{1,0:T(8,128)S(1)}, f32[32,512]{1,0:T(8,128)S(1)}, u32[]{:S(2)}, u32[]{:S(2)}) collective-permute-start(f32[32,512]{1,0:T(8,128)S(1)} %add_select_fusion.2), channel_id=1, source_target_pairs={{0,320},{16,336},{32,352},{48,368},{1,321},{17,337},{33,353},{49,3... | collective-permute-start | bytes 196616 | tf_op jit(solution)/shard_map/ppermute | solution.py:370
  24.2 8.0 %collective-permute-start.16 = (f32[32,512]{1,0:T(8,128)S(1)}, f32[32,512]{1,0:T(8,128)S(1)}, u32[]{:S(2)}, u32[]{:S(2)}) collective-permute-start(f32[32,512]{1,0:T(8,128)S(1)} %add_select_fusion.2), channel_id=1, source_target_pairs={{0,256},{16,272},{32,288},{48,304},{1,257},{17,273},{33,289},{49,3... | collective-permute-start | bytes 196616 | tf_op jit(solution)/shard_map/ppermute | solution.py:370
  25.5 6.7 %collective-permute-start.15 = (f32[32,512]{1,0:T(8,128)S(1)}, f32[32,512]{1,0:T(8,128)S(1)}, u32[]{:S(2)}, u32[]{:S(2)}) collective-permute-start(f32[32,512]{1,0:T(8,128)S(1)} %add_select_fusion.2), channel_id=1, source_target_pairs={{0,192},{16,208},{32,224},{48,240},{1,193},{17,209},{33,225},{49,2... | collective-permute-start | bytes 196616 | tf_op jit(solution)/shard_map/ppermute | solution.py:370
  26.8 5.4 %collective-permute-start.13 = (f32[32,512]{1,0:T(8,128)S(1)}, f32[32,512]{1,0:T(8,128)S(1)}, u32[]{:S(2)}, u32[]{:S(2)}) collective-permute-start(f32[32,512]{1,0:T(8,128)S(1)} %add_select_fusion.2), channel_id=1, source_target_pairs={{0,64},{16,80},{32,96},{48,112},{1,65},{17,81},{33,97},{49,113},{2... | collective-permute-start | bytes 196616 | tf_op jit(solution)/shard_map/ppermute | solution.py:370
  28.1 4.1 %collective-permute-start.14 = (f32[32,512]{1,0:T(8,128)S(1)}, f32[32,512]{1,0:T(8,128)S(1)}, u32[]{:S(2)}, u32[]{:S(2)}) collective-permute-start(f32[32,512]{1,0:T(8,128)S(1)} %add_select_fusion.2), channel_id=1, source_target_pairs={{0,128},{16,144},{32,160},{48,176},{1,129},{17,145},{33,161},{49,1... | collective-permute-start | bytes 196616 | tf_op jit(solution)/shard_map/ppermute | solution.py:370
  32.3 27.5 %copy-start.4 = (f32[192,512]{1,0:T(8,128)S(1)}, f32[192,512]{1,0:T(8,128)}, u32[]{:S(2)}) copy-start(f32[192,512]{1,0:T(8,128)} %get-tuple-element.31) | copy-start | bytes 1179652
  33.0 15.8 %all-to-all-start = ((f32[32,16,128]{2,1,0:T(8,128)}), f32[32,16,128]{2,1,0:T(8,128)S(1)}, u32[]{:S(2)}, u32[]{:S(2)}) async-start(f32[32,16,128]{2,1,0:T(8,128)} %bitcast.5), calls=%async_computation | async-start | bytes 524288 | tf_op jit(solution)/shard_map/all_to_all | solution.py:383
  38.4 18.2 %collective-permute-start.3 = (f32[192,512]{1,0:T(8,128)}, f32[192,512]{1,0:T(8,128)S(1)}, u32[]{:S(2)}, u32[]{:S(2)}) collective-permute-start(f32[192,512]{1,0:T(8,128)} %get-tuple-element.32), channel_id=1, source_target_pairs={{0,16},{1,17},{2,18},{3,19},{4,20},{5,21},{6,22},{7,23},{8,24},{9,... | collective-permute-start | bytes 1179656 | tf_op jit(solution)/shard_map/ppermute | solution.py:378
  41.6 18.1 %collective-permute-start.4 = (f32[192,512]{1,0:T(8,128)}, f32[192,512]{1,0:T(8,128)S(1)}, u32[]{:S(2)}, u32[]{:S(2)}) collective-permute-start(f32[192,512]{1,0:T(8,128)} %get-tuple-element.33), channel_id=1, source_target_pairs={{0,32},{1,33},{2,34},{3,35},{4,36},{5,37},{6,38},{7,39},{8,40},{9,... | collective-permute-start | bytes 1179656 | tf_op jit(solution)/shard_map/ppermute | solution.py:378
  43.8 15.9 %collective-permute-start.5 = (f32[192,512]{1,0:T(8,128)}, f32[192,512]{1,0:T(8,128)S(1)}, u32[]{:S(2)}, u32[]{:S(2)}) collective-permute-start(f32[192,512]{1,0:T(8,128)} %get-tuple-element.34), channel_id=1, source_target_pairs={{0,48},{1,49},{2,50},{3,51},{4,52},{5,53},{6,54},{7,55},{8,56},{9,... | collective-permute-start | bytes 1179656 | tf_op jit(solution)/shard_map/ppermute | solution.py:378
  45.1 11.5 %collective-permute-start.6 = (f32[128,512]{1,0:T(8,128)}, f32[128,512]{1,0:T(8,128)S(1)}, u32[]{:S(2)}, u32[]{:S(2)}) collective-permute-start(f32[128,512]{1,0:T(8,128)} %get-tuple-element.35), channel_id=1, source_target_pairs={{0,384},{1,385},{2,386},{3,387},{4,388},{5,389},{6,390},{7,391},{8... | collective-permute-start | bytes 786440 | tf_op jit(solution)/shard_map/ppermute | solution.py:379
  46.4 10.2 %collective-permute-start.7 = (f32[128,512]{1,0:T(8,128)}, f32[128,512]{1,0:T(8,128)S(1)}, u32[]{:S(2)}, u32[]{:S(2)}) collective-permute-start(f32[128,512]{1,0:T(8,128)} %get-tuple-element.36), channel_id=1, source_target_pairs={{0,448},{1,449},{2,450},{3,451},{4,452},{5,453},{6,454},{7,455},{8... | collective-permute-start | bytes 786440 | tf_op jit(solution)/shard_map/ppermute | solution.py:379
  48.8 0.7 copy-start.2
  51.9 35.2 %all-to-all-start.1 = ((f32[32,16,512]{2,1,0:T(8,128)}), f32[32,16,512]{2,1,0:T(8,128)}, u32[]{:S(2)}, u32[]{:S(2)}) async-start(f32[32,16,512]{2,1,0:T(8,128)} %slots_to_order.1), calls=%async_computation.1 | async-start | bytes 2097152 | tf_op jit(solution)/shard_map/all_to_all | solution.py:387
  60.7 26.3 %collective-permute-start.8 = (f32[32,512]{1,0:T(8,128)}, f32[32,512]{1,0:T(8,128)}, u32[]{:S(2)}, u32[]{:S(2)}) collective-permute-start(f32[32,512]{1,0:T(8,128)} %get-tuple-element.60), channel_id=1, source_target_pairs={{0,64},{16,80},{32,96},{48,112},{384,400},{448,464},{1,65},{17,81}... | collective-permute-start | bytes 196616 | tf_op jit(solution)/shard_map/ppermute | solution.py:394
  62.6 24.5 %collective-permute-start.9 = (f32[32,512]{1,0:T(8,128)}, f32[32,512]{1,0:T(8,128)}, u32[]{:S(2)}, u32[]{:S(2)}) collective-permute-start(f32[32,512]{1,0:T(8,128)} %get-tuple-element.61), channel_id=1, source_target_pairs={{0,128},{16,144},{32,160},{48,176},{384,416},{448,480},{1,129},{17... | collective-permute-start | bytes 196616 | tf_op jit(solution)/shard_map/ppermute | solution.py:394
  64.5 22.6 %collective-permute-start.10 = (f32[32,512]{1,0:T(8,128)}, f32[32,512]{1,0:T(8,128)}, u32[]{:S(2)}, u32[]{:S(2)}) collective-permute-start(f32[32,512]{1,0:T(8,128)} %get-tuple-element.62), channel_id=1, source_target_pairs={{0,192},{16,208},{32,224},{48,240},{384,432},{448,496},{1,193},{17... | collective-permute-start | bytes 196616 | tf_op jit(solution)/shard_map/ppermute | solution.py:394
  66.4 20.7 %collective-permute-start.11 = (f32[32,512]{1,0:T(8,128)}, f32[32,512]{1,0:T(8,128)}, u32[]{:S(2)}, u32[]{:S(2)}) collective-permute-start(f32[32,512]{1,0:T(8,128)} %get-tuple-element.58), channel_id=1, source_target_pairs={{0,256},{16,272},{32,288},{48,304},{1,257},{17,273},{33,289},{49,3... | collective-permute-start | bytes 196616 | tf_op jit(solution)/shard_map/ppermute | solution.py:394
  69.0 18.0 %collective-permute-start.12 = (f32[32,512]{1,0:T(8,128)}, f32[32,512]{1,0:T(8,128)}, u32[]{:S(2)}, u32[]{:S(2)}) collective-permute-start(f32[32,512]{1,0:T(8,128)} %get-tuple-element.57), channel_id=1, source_target_pairs={{0,320},{16,336},{32,352},{48,368},{1,321},{17,337},{33,353},{49,3... | collective-permute-start | bytes 196616 | tf_op jit(solution)/shard_map/ppermute | solution.py:394
Sparse Core Ops, SparseCore 0:
  33.2 46.2 all-gather.1

commit v5 on v4

--- a/solution.py
+++ b/solution.py
@@ -236,7 +236,7 @@
         factor_kernel,
         in_specs=[hbm],
         out_specs=[hbm, hbm],
-        out_shape=[jax.ShapeDtypeStruct((3 * n, n), bf16), jax.ShapeDtypeStruct((rows, 2 * n), bf16)],
+        out_shape=[pltpu.HBM((3 * n, n), bf16), pltpu.HBM((rows, 2 * n), bf16)],
         scratch_shapes=[
             pltpu.VMEM((n, n), f32),
             pltpu.VMEM((n, n), f32),
@@ -245,10 +245,10 @@
             pltpu.VMEM((rows, 2 * n), bf16),
             pltpu.SemaphoreType.DMA((3 + rows // TILE,)),
         ],
-        compiler_params=pltpu.CompilerParams(vmem_limit_bytes=56 * 1024 * 1024),
+        compiler_params=pltpu.CompilerParams(vmem_limit_bytes=20 * 1024 * 1024),
         cost_estimate=pl.CostEstimate(flops=200_000_000_000, bytes_accessed=0, transcendentals=0),
         name="factor",
-    )(full)
+    )(pltpu.with_memory_space_constraint(full, pltpu.HBM))
 
 
 def update_kernel(rows_ref, flags_ref, *refs):
@@ -256,7 +256,7 @@
     m3_ref, l2_ref, ct_ref, trail_ref, out_ref, m3, l2, ct, x3, here, top, sems = refs
     rows, n = l2.shape[0], ct.shape[1]
     tiles, late = rows // TILE, n // TILE
-    sources = ((ct_ref, ct), (m3_ref, m3), (trail_ref, here), (l2_ref, l2))
+    sources = ((ct_ref, ct), (m3_ref, m3), (l2_ref, l2))
     gets = [pltpu.make_async_copy(a, b, sems.at[tiles + i]) for i, (a, b) in enumerate(sources)]
     for copy in gets:
         copy.start()
@@ -264,6 +264,14 @@
     for part in parts[2:]:
         received = received + part[...]
     top[...] = jnp.where(flags_ref[1] == 1, parts[0][...], received)
+    here[...] = trail_ref[...]
+    for r in range(CAP):
+        row = rows_ref[r]
+
+        @pl.when(row >= 0)
+        def _(r=r, row=row):
+            here[pl.ds(row, 1), :] = top[pl.ds(r, 1), :]
+
     gets[0].wait()
     gets[1].wait()
     hi, lo = split(ct[...])
@@ -274,14 +282,6 @@
     x3[:, pl.ds(2 * n, n)] = lo
 
     gets[2].wait()
-    for r in range(CAP):
-        row = rows_ref[r]
-
-        @pl.when(row >= 0)
-        def _(r=r, row=row):
-            here[pl.ds(row, 1), :] = top[pl.ds(r, 1), :]
-
-    gets[3].wait()
     puts = []
 
     def put(i):
@@ -315,7 +315,7 @@
     f32, bf16 = jnp.float32, jnp.bfloat16
     return pl.pallas_call(
         update_kernel,
-        in_specs=[SMEM, SMEM] + [VMEM] * len(parts) + [hbm] * 4,
+        in_specs=[SMEM, SMEM] + [VMEM] * len(parts) + [hbm] * 3 + [VMEM],
         out_specs=hbm,
         out_shape=jax.ShapeDtypeStruct(trailing.shape, f32),
         scratch_shapes=[
@@ -327,9 +327,9 @@
             pltpu.VMEM((CAP, cols), f32),
             pltpu.SemaphoreType.DMA((height // TILE + 4,)),
         ],
-        compiler_params=pltpu.CompilerParams(vmem_limit_bytes=56 * 1024 * 1024),
+        compiler_params=pltpu.CompilerParams(vmem_limit_bytes=24 * 1024 * 1024),
         name="solve_update",
-    )(rows, flags, *parts, m3, l2, ct, trailing)
+    )(rows, flags, *parts, *(pltpu.with_memory_space_constraint(a, pltpu.HBM) for a in (m3, l2)), ct, trailing)
 
 
 def from_hubs(k):

time: 103 us -> 102 us (level)
  waiting for transfers between devices: 12.1 us -> 5.71 us
  starting transfers between devices: 46.4 us -> 51.6 us
  other arithmetic: 4.05 us -> 5.67 us
    all_gather x1, waiting for transfers between devices: 8.49 us -> 4.63 us  [on_device(): lax.all_gather(jnp.concatenate([lt, slab], axis=1), PCOL, axis=0, tiled=T...]
    ppermute x3, starting transfers between devices: 6.66 us -> 8.85 us  [on_device(): near = [lax.ppermute(tops[k], PROW, [(0, k)]) for k in range(1, NX)]]
    ppermute x3, waiting for transfers between devices: 3.09 us -> 1.01 us  [on_device(): near = [lax.ppermute(tops[k], PROW, [(0, k)]) for k in range(1, NX)]]
    ppermute x5, starting transfers between devices: 10.3 us -> 12.3 us  [on_device(): got.append(lax.ppermute(sent, PROW, from_hubs(k)))]
    select_n x1, other arithmetic: 0.15 us -> 1.44 us  [on_device(): near = jnp.where(p == 0, tops[0], sum(near)).reshape(NEAR, CAP, cols_here)]
  transfers between devices with their start and end apart: 23 -> 23, of which waited for: 3 -> 2; matrix products, arithmetic and copies ran while one was open for 3% -> 5% of each run, Pallas kernels for 16% -> 15%
where the time goes in v5:
time: 102 us; the launch traced here: 101 us
  starting transfers between devices  51.6 us (51%)
  Pallas kernels  23 us (23%)
  between operations  13.8 us (14%)
  waiting for transfers between devices  5.71 us (6%)
  other arithmetic  5.67 us (6%)
  local copies, waits for them, and re-layouts  1.7 us (2%)
    ppermute x5, starting transfers between devices, on_device(): got.append(lax.ppermute(sent, PROW, from_hubs(k)))  12.3 us
    ppermute x7, starting transfers between devices, on_device(): lax.ppermute(slab, PROW, [(x0, NX * k + x0) for x0 in range(NX)])  9.05 us
    ppermute x3, starting transfers between devices, on_device(): near = [lax.ppermute(tops[k], PROW, [(0, k)]) for k in range(1, NX)]  8.85 us
    ppermute x3, starting transfers between devices, on_device(): got = [lax.ppermute(slab, PROW, [(0, k)]) for k in range(1, NX)]  7.79 us
    pallas_call x1, Pallas kernels, factor(): pl.pallas_call(factor_kernel, in_specs=[hbm], out_specs=[hbm, hbm], out_s...  7.58 us
    pallas_call x1, Pallas kernels, update(): pl.pallas_call(update_kernel, in_specs=[SMEM, SMEM] + [VMEM] * len(parts)...  7.32 us
    all_to_all x1, starting transfers between devices, on_device(): share = lax.all_to_all(share, PROW, 0, 0, tiled=True)  5.61 us
    all_to_all x1, starting transfers between devices, on_device(): ct = lax.all_to_all(ct, PROW, 0, 0, tiled=True).reshape(cols_here, block)  4.66 us
  transfers between devices with their start and end apart: 23, of which 2 were waited for; matrix products, arithmetic and copies ran while one was open for 5% of the time, Pallas kernels for 15%

profile of v5, /device:TPU:1, one launch (start us, length us, event | category | flops | bytes accessed | tf_op | source)
XLA Modules:
  0.0 101.4 jit_solution(10982663616870254366)
XLA Ops:
  6.5 1.0 slice.54
  7.5 5.2 %collective-permute-start.2 = (f32[32,512]{1,0:T(8,128)S(1)}, f32[32,512]{1,0:T(8,128)S(1)}, u32[]{:S(2)}, u32[]{:S(2)}) collective-permute-start(f32[32,512]{1,0:T(8,128)S(1)} %slice.54), channel_id=1, source_target_pairs={{0,48},{1,49},{2,50},{3,51},{4,52},{5,53},{6,54},{7,55},{8,56},{9,... | collective-permute-start | bytes 196616 | tf_op jit(solution)/shard_map/ppermute | solution.py:366
  12.7 1.3 %collective-permute-start = (f32[32,512]{1,0:T(8,128)S(1)}, f32[32,512]{1,0:T(8,128)S(1)}, u32[]{:S(2)}, u32[]{:S(2)}) collective-permute-start(f32[32,512]{1,0:T(8,128)S(1)} %slice.54), channel_id=1, source_target_pairs={{0,16},{1,17},{2,18},{3,19},{4,20},{5,21},{6,22},{7,23},{8,24},{9,... | collective-permute-start | bytes 196616 | tf_op jit(solution)/shard_map/ppermute | solution.py:366
  14.0 1.3 %collective-permute-start.1 = (f32[32,512]{1,0:T(8,128)S(1)}, f32[32,512]{1,0:T(8,128)S(1)}, u32[]{:S(2)}, u32[]{:S(2)}) collective-permute-start(f32[32,512]{1,0:T(8,128)S(1)} %slice.54), channel_id=1, source_target_pairs={{0,32},{1,33},{2,34},{3,35},{4,36},{5,37},{6,38},{7,39},{8,40},{9,... | collective-permute-start | bytes 196616 | tf_op jit(solution)/shard_map/ppermute | solution.py:366
  17.0 3.0 %pick_rows.1 = f32[512,128]{1,0:T(8,128)} custom-call(s32[32]{0:T(128)} %broadcast_add_fusion.rows_ref, s32[1]{0:T(128)} %bitcast.4.group_ref, f32[1280,512]{1,0:T(8,128)} %refs_9_.1), custom_call_target="tpu_custom_call" | custom-call | tf_op jit(solution)/shard_map/pick_rows/pallas_call | solution.py:48
  20.1 1.3 %collective-permute-start.19 = (f32[32,512]{1,0:T(8,128)S(1)}, f32[32,512]{1,0:T(8,128)S(1)}, u32[]{:S(2)}, u32[]{:S(2)}) collective-permute-start(f32[32,512]{1,0:T(8,128)S(1)} %add_select_fusion.2), channel_id=1, source_target_pairs={{0,448},{16,464},{32,480},{48,496},{1,449},{17,465},{33,481},{49,4... | collective-permute-start | bytes 196616 | tf_op jit(solution)/shard_map/ppermute | solution.py:370
  21.4 1.3 %collective-permute-start.18 = (f32[32,512]{1,0:T(8,128)S(1)}, f32[32,512]{1,0:T(8,128)S(1)}, u32[]{:S(2)}, u32[]{:S(2)}) collective-permute-start(f32[32,512]{1,0:T(8,128)S(1)} %add_select_fusion.2), channel_id=1, source_target_pairs={{0,384},{16,400},{32,416},{48,432},{1,385},{17,401},{33,417},{49,4... | collective-permute-start | bytes 196616 | tf_op jit(solution)/shard_map/ppermute | solution.py:370
  22.7 1.3 %collective-permute-start.17 = (f32[32,512]{1,0:T(8,128)S(1)}, f32[32,512]{1,0:T(8,128)S(1)}, u32[]{:S(2)}, u32[]{:S(2)}) collective-permute-start(f32[32,512]{1,0:T(8,128)S(1)} %add_select_fusion.2), channel_id=1, source_target_pairs={{0,320},{16,336},{32,352},{48,368},{1,321},{17,337},{33,353},{49,3... | collective-permute-start | bytes 196616 | tf_op jit(solution)/shard_map/ppermute | solution.py:370
  24.0 1.3 %collective-permute-start.16 = (f32[32,512]{1,0:T(8,128)S(1)}, f32[32,512]{1,0:T(8,128)S(1)}, u32[]{:S(2)}, u32[]{:S(2)}) collective-permute-start(f32[32,512]{1,0:T(8,128)S(1)} %add_select_fusion.2), channel_id=1, source_target_pairs={{0,256},{16,272},{32,288},{48,304},{1,257},{17,273},{33,289},{49,3... | collective-permute-start | bytes 196616 | tf_op jit(solution)/shard_map/ppermute | solution.py:370
  25.3 1.3 %collective-permute-start.15 = (f32[32,512]{1,0:T(8,128)S(1)}, f32[32,512]{1,0:T(8,128)S(1)}, u32[]{:S(2)}, u32[]{:S(2)}) collective-permute-start(f32[32,512]{1,0:T(8,128)S(1)} %add_select_fusion.2), channel_id=1, source_target_pairs={{0,192},{16,208},{32,224},{48,240},{1,193},{17,209},{33,225},{49,2... | collective-permute-start | bytes 196616 | tf_op jit(solution)/shard_map/ppermute | solution.py:370
  26.7 1.3 %collective-permute-start.13 = (f32[32,512]{1,0:T(8,128)S(1)}, f32[32,512]{1,0:T(8,128)S(1)}, u32[]{:S(2)}, u32[]{:S(2)}) collective-permute-start(f32[32,512]{1,0:T(8,128)S(1)} %add_select_fusion.2), channel_id=1, source_target_pairs={{0,64},{16,80},{32,96},{48,112},{1,65},{17,81},{33,97},{49,113},{2... | collective-permute-start | bytes 196616 | tf_op jit(solution)/shard_map/ppermute | solution.py:370
  28.0 1.3 %collective-permute-start.14 = (f32[32,512]{1,0:T(8,128)S(1)}, f32[32,512]{1,0:T(8,128)S(1)}, u32[]{:S(2)}, u32[]{:S(2)}) collective-permute-start(f32[32,512]{1,0:T(8,128)S(1)} %add_select_fusion.2), channel_id=1, source_target_pairs={{0,128},{16,144},{32,160},{48,176},{1,129},{17,145},{33,161},{49,1... | collective-permute-start | bytes 196616 | tf_op jit(solution)/shard_map/ppermute | solution.py:370
  29.3 2.7 %tops_to_owners.1 = (f32[192,512]{1,0:T(8,128)}, f32[192,512]{1,0:T(8,128)}, f32[192,512]{1,0:T(8,128)}, f32[192,512]{1,0:T(8,128)}, f32[128,512]{1,0:T(8,128)}, /*index=5*/f32[128,512]{1,0:T(8,128)}) custom-call(s32[1]{0:T(128)} %bitcast.first_ref, s32[1,512]{1,0:T(1,128)S(1)} %bitcast.7, f32[1280,512]{1,0:T(8,128)S(1)} %copy-done), custom_call_target="tpu_custom_call" | custom-call | flops 20000000000 | tf_op jit(solution)/shard_map/tops_to_owners/pallas_call | solution.py:148
  32.9 5.6 %all-to-all-start = ((f32[32,16,128]{2,1,0:T(8,128)}), f32[32,16,128]{2,1,0:T(8,128)S(1)}, u32[]{:S(2)}, u32[]{:S(2)}) async-start(f32[32,16,128]{2,1,0:T(8,128)} %bitcast.5), calls=%async_computation | async-start | bytes 524288 | tf_op jit(solution)/shard_map/all_to_all | solution.py:383
  38.5 3.9 %collective-permute-start.3 = (f32[192,512]{1,0:T(8,128)}, f32[192,512]{1,0:T(8,128)}, u32[]{:S(2)}, u32[]{:S(2)}) collective-permute-start(f32[192,512]{1,0:T(8,128)} %get-tuple-element.32), channel_id=1, source_target_pairs={{0,16},{1,17},{2,18},{3,19},{4,20},{5,21},{6,22},{7,23},{8,24},{9,... | collective-permute-start | bytes 1179656 | tf_op jit(solution)/shard_map/ppermute | solution.py:378
  42.4 2.9 %collective-permute-start.4 = (f32[192,512]{1,0:T(8,128)}, f32[192,512]{1,0:T(8,128)}, u32[]{:S(2)}, u32[]{:S(2)}) collective-permute-start(f32[192,512]{1,0:T(8,128)} %get-tuple-element.33), channel_id=1, source_target_pairs={{0,32},{1,33},{2,34},{3,35},{4,36},{5,37},{6,38},{7,39},{8,40},{9,... | collective-permute-start | bytes 1179656 | tf_op jit(solution)/shard_map/ppermute | solution.py:378
  45.3 2.0 %collective-permute-start.5 = (f32[192,512]{1,0:T(8,128)}, f32[192,512]{1,0:T(8,128)}, u32[]{:S(2)}, u32[]{:S(2)}) collective-permute-start(f32[192,512]{1,0:T(8,128)} %get-tuple-element.34), channel_id=1, source_target_pairs={{0,48},{1,49},{2,50},{3,51},{4,52},{5,53},{6,54},{7,55},{8,56},{9,... | collective-permute-start | bytes 1179656 | tf_op jit(solution)/shard_map/ppermute | solution.py:378
  47.3 1.3 %collective-permute-start.6 = (f32[128,512]{1,0:T(8,128)}, f32[128,512]{1,0:T(8,128)S(1)}, u32[]{:S(2)}, u32[]{:S(2)}) collective-permute-start(f32[128,512]{1,0:T(8,128)} %get-tuple-element.35), channel_id=1, source_target_pairs={{0,384},{1,385},{2,386},{3,387},{4,388},{5,389},{6,390},{7,391},{8... | collective-permute-start | bytes 786440 | tf_op jit(solution)/shard_map/ppermute | solution.py:379
  48.6 2.0 %collective-permute-start.7 = (f32[128,512]{1,0:T(8,128)}, f32[128,512]{1,0:T(8,128)}, u32[]{:S(2)}, u32[]{:S(2)}) collective-permute-start(f32[128,512]{1,0:T(8,128)} %get-tuple-element.36), channel_id=1, source_target_pairs={{0,448},{1,449},{2,450},{3,451},{4,452},{5,453},{6,454},{7,455},{8... | collective-permute-start | bytes 786440 | tf_op jit(solution)/shard_map/ppermute | solution.py:379
  51.4 2.4 %slots_to_order.1 = f32[32,16,512]{2,1,0:T(8,128)} custom-call(s32[1,512]{1,0:T(1,128)} %bitcast.8, f32[32,16,128]{2,1,0:T(8,128)} %copy-done.3), custom_call_target="tpu_custom_call" | custom-call | tf_op jit(solution)/shard_map/slots_to_order/pallas_call | solution.py:102
  53.7 4.7 %all-to-all-start.1 = ((f32[32,16,512]{2,1,0:T(8,128)}), f32[32,16,512]{2,1,0:T(8,128)}, u32[]{:S(2)}, u32[]{:S(2)}) async-start(f32[32,16,512]{2,1,0:T(8,128)} %slots_to_order.1), calls=%async_computation.1 | async-start | bytes 2097152 | tf_op jit(solution)/shard_map/all_to_all | solution.py:387
  58.4 1.0 collective-permute-done.4
  59.4 1.0 add.96
  60.5 1.4 %add_select_fusion = f32[192,512]{1,0:T(8,128)S(1)} fusion(f32[192,512]{1,0:T(8,128)S(1)} %copy-done.5, f32[192,512]{1,0:T(8,128)} %collective-permute-done.5, f32[192,512]{1,0:T(8,128)} %collective-permute-done.3, f32[192,512]{1,0:T(8,128)} %collective-permute-done.4, pred[]{:T(512)S(6)} %eq.53), kind=kLoop, calls=%fused_computation.3 | loop fusion | flops 294912 | bytes 1966081 | tf_op jit(solution)/shard_map/jit(_where)/select_n | solution.py:389
  62.6 2.6 %collective-permute-start.8 = (f32[32,512]{1,0:T(8,128)}, f32[32,512]{1,0:T(8,128)}, u32[]{:S(2)}, u32[]{:S(2)}) collective-permute-start(f32[32,512]{1,0:T(8,128)} %get-tuple-element.60), channel_id=1, source_target_pairs={{0,64},{16,80},{32,96},{48,112},{384,400},{448,464},{1,65},{17,81}... | collective-permute-start | bytes 196616 | tf_op jit(solution)/shard_map/ppermute | solution.py:394
  65.2 2.2 %collective-permute-start.9 = (f32[32,512]{1,0:T(8,128)}, f32[32,512]{1,0:T(8,128)}, u32[]{:S(2)}, u32[]{:S(2)}) collective-permute-start(f32[32,512]{1,0:T(8,128)} %get-tuple-element.61), channel_id=1, source_target_pairs={{0,128},{16,144},{32,160},{48,176},{384,416},{448,480},{1,129},{17... | collective-permute-start | bytes 196616 | tf_op jit(solution)/shard_map/ppermute | solution.py:394
  67.4 2.2 %collective-permute-start.10 = (f32[32,512]{1,0:T(8,128)}, f32[32,512]{1,0:T(8,128)}, u32[]{:S(2)}, u32[]{:S(2)}) collective-permute-start(f32[32,512]{1,0:T(8,128)} %get-tuple-element.62), channel_id=1, source_target_pairs={{0,192},{16,208},{32,224},{48,240},{384,432},{448,496},{1,193},{17... | collective-permute-start | bytes 196616 | tf_op jit(solution)/shard_map/ppermute | solution.py:394
  69.6 3.4 %collective-permute-start.11 = (f32[32,512]{1,0:T(8,128)}, f32[32,512]{1,0:T(8,128)}, u32[]{:S(2)}, u32[]{:S(2)}) collective-permute-start(f32[32,512]{1,0:T(8,128)} %get-tuple-element.58), channel_id=1, source_target_pairs={{0,256},{16,272},{32,288},{48,304},{1,257},{17,273},{33,289},{49,3... | collective-permute-start | bytes 196616 | tf_op jit(solution)/shard_map/ppermute | solution.py:394
  73.0 1.9 %collective-permute-start.12 = (f32[32,512]{1,0:T(8,128)}, f32[32,512]{1,0:T(8,128)}, u32[]{:S(2)}, u32[]{:S(2)}) collective-permute-start(f32[32,512]{1,0:T(8,128)} %get-tuple-element.57), channel_id=1, source_target_pairs={{0,320},{16,336},{32,352},{48,368},{1,321},{17,337},{33,353},{49,3... | collective-permute-start | bytes 196616 | tf_op jit(solution)/shard_map/ppermute | solution.py:394
  75.0 4.6 %all-gather.2.cloned.1.call-done.full_ref = f32[512,1792]{1,0:T(8,128)} async-done(((f32[32,1792]{1,0:T(8,128)}), f32[512,1792]{1,0:T(8,128)}) %all-gather.2.cloned.1.call-update) | async-done | bytes 3670032 | tf_op jit(solution)/shard_map/all_gather | solution.py:376
  79.6 7.6 %factor.1 = (bf16[1536,512]{1,0:T(8,128)(2,1)}, bf16[1280,1024]{1,0:T(8,128)(2,1)}) custom-call(f32[512,1792]{1,0:T(8,128)} %all-gather.2.cloned.1.call-done.full_ref), custom_call_target="tpu_custom_call" | custom-call | flops 199999995904 | tf_op jit(solution)/shard_map/factor/pallas_call | solution.py:235
  87.2 7.3 %solve_update.1 = f32[1280,512]{1,0:T(8,128)} custom-call(s32[32]{0:T(128)S(1)} %copy-done.2, s32[2]{0:T(128)S(1)} %pad_add_fusion.flags_ref, f32[32,512]{1,0:T(8,128)S(1)} %get-tuple-element.59.refs_0_, f32[32,512]{1,0:T(8,128)} %collective-permute-done.8.refs_1_, f32[32,512]{1,0:T(8,128)} %collective-permute-done.9.refs_2_, ...), custom_call_target="tpu_custom_call" | custom-call | tf_op jit(solution)/shard_map/solve_update/pallas_call | solution.py:316
  (46 shorter events, 4.0 us)
Async XLA Ops:
  6.5 13.6 %copy-start.4 = (f32[1280,32]{0,1:T(8,128)S(1)}, f32[1280,32]{0,1:T(8,128)}, u32[]{:S(2)}) copy-start(f32[1280,32]{0,1:T(8,128)} %param.4) | copy-start | bytes 491524
  6.5 22.7 %copy-start = (f32[1280,512]{1,0:T(8,128)S(1)}, f32[1280,512]{1,0:T(8,128)}, u32[]{:S(2)}) copy-start(f32[1280,512]{1,0:T(8,128)} %refs_9_.1) | copy-start | bytes 7864324
  6.5 73.0 %all-gather.2.cloned.1.call-start = ((), (), s32[]{:S(2)}) async-start(), calls=%async_computation.2 | async-start | bytes 3899392 | tf_op jit(solution)/shard_map/all_gather | solution.py:376
  7.5 12.5 %collective-permute-start.2 = (f32[32,512]{1,0:T(8,128)S(1)}, f32[32,512]{1,0:T(8,128)S(1)}, u32[]{:S(2)}, u32[]{:S(2)}) collective-permute-start(f32[32,512]{1,0:T(8,128)S(1)} %slice.54), channel_id=1, source_target_pairs={{0,48},{1,49},{2,50},{3,51},{4,52},{5,53},{6,54},{7,55},{8,56},{9,... | collective-permute-start | bytes 196616 | tf_op jit(solution)/shard_map/ppermute | solution.py:366
  12.7 7.3 %collective-permute-start = (f32[32,512]{1,0:T(8,128)S(1)}, f32[32,512]{1,0:T(8,128)S(1)}, u32[]{:S(2)}, u32[]{:S(2)}) collective-permute-start(f32[32,512]{1,0:T(8,128)S(1)} %slice.54), channel_id=1, source_target_pairs={{0,16},{1,17},{2,18},{3,19},{4,20},{5,21},{6,22},{7,23},{8,24},{9,... | collective-permute-start | bytes 196616 | tf_op jit(solution)/shard_map/ppermute | solution.py:366
  14.0 6.0 %collective-permute-start.1 = (f32[32,512]{1,0:T(8,128)S(1)}, f32[32,512]{1,0:T(8,128)S(1)}, u32[]{:S(2)}, u32[]{:S(2)}) collective-permute-start(f32[32,512]{1,0:T(8,128)S(1)} %slice.54), channel_id=1, source_target_pairs={{0,32},{1,33},{2,34},{3,35},{4,36},{5,37},{6,38},{7,39},{8,40},{9,... | collective-permute-start | bytes 196616 | tf_op jit(solution)/shard_map/ppermute | solution.py:366
  16.3 15.7 %copy-start.1 = (s32[512]{0:T(512)}, s32[512]{0:T(512)S(1)}, u32[]{:S(2)}) copy-start(s32[512]{0:T(512)S(1)} %multiply_add_fusion) | copy-start | bytes 6148
  20.1 6.5 %collective-permute-start.19 = (f32[32,512]{1,0:T(8,128)S(1)}, f32[32,512]{1,0:T(8,128)S(1)}, u32[]{:S(2)}, u32[]{:S(2)}) collective-permute-start(f32[32,512]{1,0:T(8,128)S(1)} %add_select_fusion.2), channel_id=1, source_target_pairs={{0,448},{16,464},{32,480},{48,496},{1,449},{17,465},{33,481},{49,4... | collective-permute-start | bytes 196616 | tf_op jit(solution)/shard_map/ppermute | solution.py:370
  21.4 6.5 %collective-permute-start.18 = (f32[32,512]{1,0:T(8,128)S(1)}, f32[32,512]{1,0:T(8,128)S(1)}, u32[]{:S(2)}, u32[]{:S(2)}) collective-permute-start(f32[32,512]{1,0:T(8,128)S(1)} %add_select_fusion.2), channel_id=1, source_target_pairs={{0,384},{16,400},{32,416},{48,432},{1,385},{17,401},{33,417},{49,4... | collective-permute-start | bytes 196616 | tf_op jit(solution)/shard_map/ppermute | solution.py:370
  22.7 9.3 %collective-permute-start.17 = (f32[32,512]{1,0:T(8,128)S(1)}, f32[32,512]{1,0:T(8,128)S(1)}, u32[]{:S(2)}, u32[]{:S(2)}) collective-permute-start(f32[32,512]{1,0:T(8,128)S(1)} %add_select_fusion.2), channel_id=1, source_target_pairs={{0,320},{16,336},{32,352},{48,368},{1,321},{17,337},{33,353},{49,3... | collective-permute-start | bytes 196616 | tf_op jit(solution)/shard_map/ppermute | solution.py:370
  24.0 8.0 %collective-permute-start.16 = (f32[32,512]{1,0:T(8,128)S(1)}, f32[32,512]{1,0:T(8,128)S(1)}, u32[]{:S(2)}, u32[]{:S(2)}) collective-permute-start(f32[32,512]{1,0:T(8,128)S(1)} %add_select_fusion.2), channel_id=1, source_target_pairs={{0,256},{16,272},{32,288},{48,304},{1,257},{17,273},{33,289},{49,3... | collective-permute-start | bytes 196616 | tf_op jit(solution)/shard_map/ppermute | solution.py:370
  25.3 6.7 %collective-permute-start.15 = (f32[32,512]{1,0:T(8,128)S(1)}, f32[32,512]{1,0:T(8,128)S(1)}, u32[]{:S(2)}, u32[]{:S(2)}) collective-permute-start(f32[32,512]{1,0:T(8,128)S(1)} %add_select_fusion.2), channel_id=1, source_target_pairs={{0,192},{16,208},{32,224},{48,240},{1,193},{17,209},{33,225},{49,2... | collective-permute-start | bytes 196616 | tf_op jit(solution)/shard_map/ppermute | solution.py:370
  26.7 5.4 %collective-permute-start.13 = (f32[32,512]{1,0:T(8,128)S(1)}, f32[32,512]{1,0:T(8,128)S(1)}, u32[]{:S(2)}, u32[]{:S(2)}) collective-permute-start(f32[32,512]{1,0:T(8,128)S(1)} %add_select_fusion.2), channel_id=1, source_target_pairs={{0,64},{16,80},{32,96},{48,112},{1,65},{17,81},{33,97},{49,113},{2... | collective-permute-start | bytes 196616 | tf_op jit(solution)/shard_map/ppermute | solution.py:370
  28.0 4.1 %collective-permute-start.14 = (f32[32,512]{1,0:T(8,128)S(1)}, f32[32,512]{1,0:T(8,128)S(1)}, u32[]{:S(2)}, u32[]{:S(2)}) collective-permute-start(f32[32,512]{1,0:T(8,128)S(1)} %add_select_fusion.2), channel_id=1, source_target_pairs={{0,128},{16,144},{32,160},{48,176},{1,129},{17,145},{33,161},{49,1... | collective-permute-start | bytes 196616 | tf_op jit(solution)/shard_map/ppermute | solution.py:370
  32.1 28.3 %copy-start.5 = (f32[192,512]{1,0:T(8,128)S(1)}, f32[192,512]{1,0:T(8,128)}, u32[]{:S(2)}) copy-start(f32[192,512]{1,0:T(8,128)} %get-tuple-element.31) | copy-start | bytes 1179652
  32.9 17.8 %all-to-all-start = ((f32[32,16,128]{2,1,0:T(8,128)}), f32[32,16,128]{2,1,0:T(8,128)S(1)}, u32[]{:S(2)}, u32[]{:S(2)}) async-start(f32[32,16,128]{2,1,0:T(8,128)} %bitcast.5), calls=%async_computation | async-start | bytes 524288 | tf_op jit(solution)/shard_map/all_to_all | solution.py:383
  38.5 20.0 %collective-permute-start.3 = (f32[192,512]{1,0:T(8,128)}, f32[192,512]{1,0:T(8,128)}, u32[]{:S(2)}, u32[]{:S(2)}) collective-permute-start(f32[192,512]{1,0:T(8,128)} %get-tuple-element.32), channel_id=1, source_target_pairs={{0,16},{1,17},{2,18},{3,19},{4,20},{5,21},{6,22},{7,23},{8,24},{9,... | collective-permute-start | bytes 1179656 | tf_op jit(solution)/shard_map/ppermute | solution.py:378
  42.4 17.1 %collective-permute-start.4 = (f32[192,512]{1,0:T(8,128)}, f32[192,512]{1,0:T(8,128)}, u32[]{:S(2)}, u32[]{:S(2)}) collective-permute-start(f32[192,512]{1,0:T(8,128)} %get-tuple-element.33), channel_id=1, source_target_pairs={{0,32},{1,33},{2,34},{3,35},{4,36},{5,37},{6,38},{7,39},{8,40},{9,... | collective-permute-start | bytes 1179656 | tf_op jit(solution)/shard_map/ppermute | solution.py:378
  45.3 14.1 %collective-permute-start.5 = (f32[192,512]{1,0:T(8,128)}, f32[192,512]{1,0:T(8,128)}, u32[]{:S(2)}, u32[]{:S(2)}) collective-permute-start(f32[192,512]{1,0:T(8,128)} %get-tuple-element.34), channel_id=1, source_target_pairs={{0,48},{1,49},{2,50},{3,51},{4,52},{5,53},{6,54},{7,55},{8,56},{9,... | collective-permute-start | bytes 1179656 | tf_op jit(solution)/shard_map/ppermute | solution.py:378
  47.3 11.1 %collective-permute-start.6 = (f32[128,512]{1,0:T(8,128)}, f32[128,512]{1,0:T(8,128)S(1)}, u32[]{:S(2)}, u32[]{:S(2)}) collective-permute-start(f32[128,512]{1,0:T(8,128)} %get-tuple-element.35), channel_id=1, source_target_pairs={{0,384},{1,385},{2,386},{3,387},{4,388},{5,389},{6,390},{7,391},{8... | collective-permute-start | bytes 786440 | tf_op jit(solution)/shard_map/ppermute | solution.py:379
  48.6 9.8 %collective-permute-start.7 = (f32[128,512]{1,0:T(8,128)}, f32[128,512]{1,0:T(8,128)}, u32[]{:S(2)}, u32[]{:S(2)}) collective-permute-start(f32[128,512]{1,0:T(8,128)} %get-tuple-element.36), channel_id=1, source_target_pairs={{0,448},{1,449},{2,450},{3,451},{4,452},{5,453},{6,454},{7,455},{8... | collective-permute-start | bytes 786440 | tf_op jit(solution)/shard_map/ppermute | solution.py:379
  50.7 0.7 copy-start.3
  53.7 33.5 %all-to-all-start.1 = ((f32[32,16,512]{2,1,0:T(8,128)}), f32[32,16,512]{2,1,0:T(8,128)}, u32[]{:S(2)}, u32[]{:S(2)}) async-start(f32[32,16,512]{2,1,0:T(8,128)} %slots_to_order.1), calls=%async_computation.1 | async-start | bytes 2097152 | tf_op jit(solution)/shard_map/all_to_all | solution.py:387
  62.6 24.5 %collective-permute-start.8 = (f32[32,512]{1,0:T(8,128)}, f32[32,512]{1,0:T(8,128)}, u32[]{:S(2)}, u32[]{:S(2)}) collective-permute-start(f32[32,512]{1,0:T(8,128)} %get-tuple-element.60), channel_id=1, source_target_pairs={{0,64},{16,80},{32,96},{48,112},{384,400},{448,464},{1,65},{17,81}... | collective-permute-start | bytes 196616 | tf_op jit(solution)/shard_map/ppermute | solution.py:394
  65.2 22.0 %collective-permute-start.9 = (f32[32,512]{1,0:T(8,128)}, f32[32,512]{1,0:T(8,128)}, u32[]{:S(2)}, u32[]{:S(2)}) collective-permute-start(f32[32,512]{1,0:T(8,128)} %get-tuple-element.61), channel_id=1, source_target_pairs={{0,128},{16,144},{32,160},{48,176},{384,416},{448,480},{1,129},{17... | collective-permute-start | bytes 196616 | tf_op jit(solution)/shard_map/ppermute | solution.py:394
  67.4 19.8 %collective-permute-start.10 = (f32[32,512]{1,0:T(8,128)}, f32[32,512]{1,0:T(8,128)}, u32[]{:S(2)}, u32[]{:S(2)}) collective-permute-start(f32[32,512]{1,0:T(8,128)} %get-tuple-element.62), channel_id=1, source_target_pairs={{0,192},{16,208},{32,224},{48,240},{384,432},{448,496},{1,193},{17... | collective-permute-start | bytes 196616 | tf_op jit(solution)/shard_map/ppermute | solution.py:394
  69.6 17.6 %collective-permute-start.11 = (f32[32,512]{1,0:T(8,128)}, f32[32,512]{1,0:T(8,128)}, u32[]{:S(2)}, u32[]{:S(2)}) collective-permute-start(f32[32,512]{1,0:T(8,128)} %get-tuple-element.58), channel_id=1, source_target_pairs={{0,256},{16,272},{32,288},{48,304},{1,257},{17,273},{33,289},{49,3... | collective-permute-start | bytes 196616 | tf_op jit(solution)/shard_map/ppermute | solution.py:394
  73.0 14.2 %collective-permute-start.12 = (f32[32,512]{1,0:T(8,128)}, f32[32,512]{1,0:T(8,128)}, u32[]{:S(2)}, u32[]{:S(2)}) collective-permute-start(f32[32,512]{1,0:T(8,128)} %get-tuple-element.57), channel_id=1, source_target_pairs={{0,320},{16,336},{32,352},{48,368},{1,321},{17,337},{33,353},{49,3... | collective-permute-start | bytes 196616 | tf_op jit(solution)/shard_map/ppermute | solution.py:394
  79.6 7.7 %copy-start.2 = (s32[32]{0:T(128)S(1)}, s32[32]{0:T(128)}, u32[]{:S(2)}) copy-start(s32[32]{0:T(128)} %broadcast_add_fusion.rows_ref) | copy-start | bytes 388
Sparse Core Ops, SparseCore 0:
  33.0 46.5 all-gather.1

commit v6 on v5

--- a/solution.py
+++ b/solution.py
@@ -9,7 +9,11 @@
 NPROW = NX * NY
 CAP = 32
 LANES = 128
-NEAR = 6
+ORDER1 = (1, 2, 3, 4, 5, 6, 7)
+ORDER2 = (4, 3, 2, 1, 5)
+FARS = (6, 7)
+NEARS = (0, 1, 2, 3, 4, 5)
+NEAR = len(NEARS)
 SHARE = LANES // CAP
 PROW, PCOL = ("y", "x"), ("z", "c")
 HI = lax.Precision.HIGHEST
@@ -27,20 +31,16 @@
     return hi, lo
 
 
-def pick_kernel(rows_ref, group_ref, trail_ref, out_ref, near, lanes, sems):
-    def copy(r):
-        tile = pl.multiple_of((jnp.maximum(rows_ref[r], 0) // 8) * 8, 8)
-        return pltpu.make_async_copy(trail_ref.at[pl.ds(tile, 8), :], near.at[r], sems.at[r])
-
+def pick_kernel(rows_ref, group_ref, trail_ref, out_ref, near, picked, sem):
+    here = [jnp.maximum(rows_ref[r], 0) for r in range(CAP)]
     for r in range(CAP):
-        copy(r).start()
-    lanes[...] = jnp.zeros_like(lanes)
-    base = group_ref[0] * CAP
+        tile = pl.multiple_of((here[r] // 8) * 8, 8)
+        pltpu.make_async_copy(trail_ref.at[pl.ds(tile, 8), :], near.at[r], sem).start()
+    pltpu.make_async_copy(near, near, sem).wait()
     for r in range(CAP):
-        copy(r).wait()
-        row = jnp.maximum(rows_ref[r], 0) % 8
-        lanes[pl.ds(base + r, 1), :] = near[r, pl.ds(row, 1), :]
-    out_ref[...] = lanes[...].T
+        picked[pl.ds(r, 1), :] = near[r, pl.ds(here[r] % 8, 1), :]
+    parts = [jnp.where(group_ref[0] == g, picked[...], 0.0) for g in range(SHARE)]
+    out_ref[...] = jnp.concatenate(parts, axis=0).T
 
 
 def pick(rows, group, trailing):
@@ -52,8 +52,8 @@
         out_shape=jax.ShapeDtypeStruct((cols, LANES), jnp.float32),
         scratch_shapes=[
             pltpu.VMEM((CAP, 8, cols), jnp.float32),
-            pltpu.VMEM((LANES, cols), jnp.float32),
-            pltpu.SemaphoreType.DMA((CAP,)),
+            pltpu.VMEM((CAP, cols), jnp.float32),
+            pltpu.SemaphoreType.DMA,
         ],
         cost_estimate=pl.CostEstimate(flops=0, bytes_accessed=0, transcendentals=0),
         name="pick_rows",
@@ -73,14 +73,21 @@
 
 def owner_at(place):
     if place < NX * NEAR:
-        x, y = divmod(place, NEAR)
+        x, i = divmod(place, NEAR)
+        y = NEARS[i]
     else:
-        y, x = divmod(place, NX)
+        i, x = divmod(place - NX * NEAR, NX)
+        y = FARS[i]
     return NX * y + x
 
 
+def is_far(y):
+    return (y >= FARS[0]) & (y <= FARS[-1])
+
+
 def place_of(y, x):
-    return jnp.where(y < NEAR, x * NEAR + y, NX * y + x)
+    near = x * NEAR + jnp.where(y < FARS[0], y, y - len(FARS))
+    return jnp.where(is_far(y), NX * NEAR + NX * (y - FARS[0]) + x, near)
 
 
 def order_kernel(slot_ref, slots_ref, out_ref):
@@ -191,7 +198,7 @@
 TILE = 256
 
 
-def factor_kernel(full_ref, m3_ref, l2_ref, u, m, lt, m3, l2, sems):
+def factor_kernel(full_ref, m2_ref, l2_ref, u, m, lt, m2, l2, sems):
     n, rows = lt.shape
     get_u = pltpu.make_async_copy(full_ref.at[:, pl.ds(rows, n)], u, sems.at[0])
     get_l = pltpu.make_async_copy(full_ref.at[:, pl.ds(0, rows)], lt, sems.at[1])
@@ -219,10 +226,9 @@
     while todo:
         between(n)
     hi, lo = split(m[...])
-    m3[pl.ds(0, n), :] = hi
-    m3[pl.ds(n, n), :] = hi
-    m3[pl.ds(2 * n, n), :] = lo
-    puts.append(pltpu.make_async_copy(m3, m3_ref, sems.at[2 + rows // TILE]))
+    m2[pl.ds(0, n), :] = hi
+    m2[pl.ds(n, n), :] = lo
+    puts.append(pltpu.make_async_copy(m2, m2_ref, sems.at[2 + rows // TILE]))
     puts[-1].start()
     for copy in puts:
         copy.wait()
@@ -236,12 +242,12 @@
         factor_kernel,
         in_specs=[hbm],
         out_specs=[hbm, hbm],
-        out_shape=[pltpu.HBM((3 * n, n), bf16), pltpu.HBM((rows, 2 * n), bf16)],
+        out_shape=[pltpu.HBM((2 * n, n), bf16), pltpu.HBM((rows, 2 * n), bf16)],
         scratch_shapes=[
             pltpu.VMEM((n, n), f32),
             pltpu.VMEM((n, n), f32),
             pltpu.VMEM((n, rows), f32),
-            pltpu.VMEM((3 * n, n), bf16),
+            pltpu.VMEM((2 * n, n), bf16),
             pltpu.VMEM((rows, 2 * n), bf16),
             pltpu.SemaphoreType.DMA((3 + rows // TILE,)),
         ],
@@ -253,10 +259,10 @@
 
 def update_kernel(rows_ref, flags_ref, *refs):
     parts, refs = refs[:NEAR], refs[NEAR:]
-    m3_ref, l2_ref, ct_ref, trail_ref, out_ref, m3, l2, ct, x3, here, top, sems = refs
+    m2_ref, l2_ref, ct, trail_ref, out_ref, m2, l2, x3, here, top, sems = refs
     rows, n = l2.shape[0], ct.shape[1]
     tiles, late = rows // TILE, n // TILE
-    sources = ((ct_ref, ct), (m3_ref, m3), (l2_ref, l2))
+    sources = ((m2_ref, m2), (l2_ref, l2))
     gets = [pltpu.make_async_copy(a, b, sems.at[tiles + i]) for i, (a, b) in enumerate(sources)]
     for copy in gets:
         copy.start()
@@ -272,16 +278,16 @@
         def _(r=r, row=row):
             here[pl.ds(row, 1), :] = top[pl.ds(r, 1), :]
 
+    hi, lo = split(ct[...])
     gets[0].wait()
-    gets[1].wait()
-    hi, lo = split(ct[...])
-    xt = dot(jnp.concatenate([hi, lo, hi], axis=1), m3[...], precision=None)
+    both = dot(jnp.concatenate([hi, lo], axis=0), m2[pl.ds(0, n), :], precision=None)
+    xt = both[: ct.shape[0]] + (both[ct.shape[0] :] + dot(hi, m2[pl.ds(n, n), :], precision=None))
     hi, lo = split(xt)
     x3[:, pl.ds(0, n)] = hi
     x3[:, pl.ds(n, n)] = hi
     x3[:, pl.ds(2 * n, n)] = lo
 
-    gets[2].wait()
+    gets[1].wait()
     puts = []
 
     def put(i):
@@ -308,20 +314,19 @@
         copy.wait()
 
 
-def update(rows, flags, parts, m3, l2, ct, trailing):
+def update(rows, flags, parts, m2, l2, ct, trailing):
     height, cols = trailing.shape
     n = ct.shape[1]
     hbm = pl.BlockSpec(memory_space=pl.ANY)
     f32, bf16 = jnp.float32, jnp.bfloat16
     return pl.pallas_call(
         update_kernel,
-        in_specs=[SMEM, SMEM] + [VMEM] * len(parts) + [hbm] * 3 + [VMEM],
+        in_specs=[SMEM, SMEM] + [VMEM] * len(parts) + [hbm, hbm, VMEM, VMEM],
         out_specs=hbm,
         out_shape=jax.ShapeDtypeStruct(trailing.shape, f32),
         scratch_shapes=[
-            pltpu.VMEM(m3.shape, bf16),
+            pltpu.VMEM(m2.shape, bf16),
             pltpu.VMEM(l2.shape, bf16),
-            pltpu.VMEM(ct.shape, f32),
             pltpu.VMEM((cols, 3 * n), bf16),
             pltpu.VMEM((height, cols), f32),
             pltpu.VMEM((CAP, cols), f32),
@@ -329,13 +334,13 @@
         ],
         compiler_params=pltpu.CompilerParams(vmem_limit_bytes=24 * 1024 * 1024),
         name="solve_update",
-    )(rows, flags, *parts, *(pltpu.with_memory_space_constraint(a, pltpu.HBM) for a in (m3, l2)), ct, trailing)
+    )(rows, flags, *parts, *(pltpu.with_memory_space_constraint(a, pltpu.HBM) for a in (m2, l2)), ct, trailing)
 
 
 def from_hubs(k):
-    pairs = [(x, NX * k + x) for x in range(NX)]
+    pairs = [(x, NX * NEARS[k] + x) for x in range(NX)]
     if k < NX:
-        pairs += [(NX * y, NX * y + k) for y in range(NEAR, NY)]
+        pairs += [(NX * y, NX * y + k) for y in FARS]
     return pairs
 
 
@@ -359,7 +364,7 @@
     here = place_of(y, x)
     mine = slot[None, :] == (here * CAP + jnp.arange(CAP, dtype=jnp.int32))[:, None]
     rows = jnp.sum(jnp.where(mine, local[None, :] + 1, 0), axis=1) - 1
-    hub = (y == 0) | ((y >= NEAR) & (x == 0))
+    hub = (y == 0) | (is_far(y) & (x == 0))
 
     lt = l_panel.T
     slab = lt[:, :block]
@@ -367,7 +372,7 @@
     slab = jnp.where(p == 0, slab, sum(got))
     lanes = pick(rows, (here % SHARE)[None], trailing)
     slab, lanes = lax.optimization_barrier((slab, lanes))
-    got = [lax.ppermute(slab, PROW, [(x0, NX * k + x0) for x0 in range(NX)]) for k in range(1, NY)]
+    got = [lax.ppermute(slab, PROW, [(x0, NX * k + x0) for x0 in range(NX)]) for k in ORDER1]
     slab = jnp.where(y == 0, slab, sum(got))
 
     tops = to_owners(first, slot[None, :], after(trailing, lanes))
@@ -376,7 +381,7 @@
     full = lax.all_gather(jnp.concatenate([lt, slab], axis=1), PCOL, axis=0, tiled=True)
 
     near = [lax.ppermute(tops[k], PROW, [(0, k)]) for k in range(1, NX)]
-    far = [lax.ppermute(tops[NX + i], PROW, [(0, NX * (NEAR + i))]) for i in range(NY - NEAR)]
+    far = [lax.ppermute(tops[NX + i], PROW, [(0, NX * f)]) for i, f in enumerate(FARS)]
 
     lanes = after(lanes, tops[1])
     share = lanes.reshape(NPROW, cols_here // NPROW, LANES)
@@ -389,15 +394,15 @@
     near = jnp.where(p == 0, tops[0], sum(near)).reshape(NEAR, CAP, cols_here)
     far = sum(far).reshape(NX, CAP, cols_here)
     got = []
-    for k in range(1, NEAR):
+    for k in ORDER2:
         sent = jnp.where(y == 0, near[k], far[k]) if k < NX else near[k]
         got.append(lax.ppermute(sent, PROW, from_hubs(k)))
 
-    m3, l2 = factor(full, rows_here)
-    got, m3 = lax.optimization_barrier((got, m3))
+    m2, l2 = factor(full, rows_here)
+    got, m2 = lax.optimization_barrier((got, m2))
     own = jnp.where(y == 0, near[0], far[0])
     flags = jnp.stack([first[0], hub.astype(jnp.int32)])
-    return update(rows, flags, [own] + got, m3, l2, ct, trailing)
+    return update(rows, flags, [own] + got, m2, l2, ct, trailing)
 
 
 def solution(mesh):

time: 102 us -> 102 us (level)
  waiting for transfers between devices: 5.71 us -> 3.69 us
  starting transfers between devices: 51.6 us -> 53.3 us
    ppermute x5, starting transfers between devices: 12.3 us -> 14.4 us  [on_device(): got.append(lax.ppermute(sent, PROW, from_hubs(k)))]
    all_gather x1, waiting for transfers between devices: 4.63 us -> 2.75 us  [on_device(): lax.all_gather(jnp.concatenate([lt, slab], axis=1), PCOL, axis=0, tiled=T...]
where the time goes in v6:
time: 102 us; the launch traced here: 101 us
  starting transfers between devices  53.3 us (52%)
  Pallas kernels  22.9 us (22%)
  between operations  13.8 us (14%)
  other arithmetic  5.74 us (6%)
  waiting for transfers between devices  3.69 us (4%)
  local copies, waits for them, and re-layouts  1.73 us (2%)
    ppermute x5, starting transfers between devices, on_device(): got.append(lax.ppermute(sent, PROW, from_hubs(k)))  14.4 us
    ppermute x7, starting transfers between devices, on_device(): lax.ppermute(slab, PROW, [(x0, NX * k + x0) for x0 in range(NX)])  9.05 us
    ppermute x3, starting transfers between devices, on_device(): near = [lax.ppermute(tops[k], PROW, [(0, k)]) for k in range(1, NX)]  8.83 us
    ppermute x3, starting transfers between devices, on_device(): got = [lax.ppermute(slab, PROW, [(0, k)]) for k in range(1, NX)]  7.79 us
    pallas_call x1, Pallas kernels, factor(): pl.pallas_call(factor_kernel, in_specs=[hbm], out_specs=[hbm, hbm], out_s...  7.51 us
    pallas_call x1, Pallas kernels, update(): pl.pallas_call(update_kernel, in_specs=[SMEM, SMEM] + [VMEM] * len(parts)...  7.24 us
    all_to_all x1, starting transfers between devices, on_device(): share = lax.all_to_all(share, PROW, 0, 0, tiled=True)  5.28 us
    all_to_all x1, starting transfers between devices, on_device(): ct = lax.all_to_all(ct, PROW, 0, 0, tiled=True).reshape(cols_here, block)  4.66 us
  transfers between devices with their start and end apart: 23, of which 2 were waited for; matrix products, arithmetic and copies ran while one was open for 5% of the time, Pallas kernels for 15%

profile of v6, /device:TPU:1, one launch (start us, length us, event | category | flops | bytes accessed | tf_op | source)
XLA Modules:
  0.0 101.2 jit_solution(13991476723847779666)
XLA Ops:
  6.5 1.0 slice.54
  7.5 5.2 %collective-permute-start.2 = (f32[32,512]{1,0:T(8,128)S(1)}, f32[32,512]{1,0:T(8,128)S(1)}, u32[]{:S(2)}, u32[]{:S(2)}) collective-permute-start(f32[32,512]{1,0:T(8,128)S(1)} %slice.54), channel_id=1, source_target_pairs={{0,48},{1,49},{2,50},{3,51},{4,52},{5,53},{6,54},{7,55},{8,56},{9,... | collective-permute-start | bytes 196616 | tf_op jit(solution)/shard_map/ppermute | solution.py:371
  12.7 1.3 %collective-permute-start = (f32[32,512]{1,0:T(8,128)S(1)}, f32[32,512]{1,0:T(8,128)S(1)}, u32[]{:S(2)}, u32[]{:S(2)}) collective-permute-start(f32[32,512]{1,0:T(8,128)S(1)} %slice.54), channel_id=1, source_target_pairs={{0,16},{1,17},{2,18},{3,19},{4,20},{5,21},{6,22},{7,23},{8,24},{9,... | collective-permute-start | bytes 196616 | tf_op jit(solution)/shard_map/ppermute | solution.py:371
  14.0 1.3 %collective-permute-start.1 = (f32[32,512]{1,0:T(8,128)S(1)}, f32[32,512]{1,0:T(8,128)S(1)}, u32[]{:S(2)}, u32[]{:S(2)}) collective-permute-start(f32[32,512]{1,0:T(8,128)S(1)} %slice.54), channel_id=1, source_target_pairs={{0,32},{1,33},{2,34},{3,35},{4,36},{5,37},{6,38},{7,39},{8,40},{9,... | collective-permute-start | bytes 196616 | tf_op jit(solution)/shard_map/ppermute | solution.py:371
  17.1 3.1 %pick_rows.1 = f32[512,128]{1,0:T(8,128)} custom-call(s32[32]{0:T(128)} %broadcast_add_fusion.rows_ref, s32[1]{0:T(128)} %bitcast.4.group_ref, f32[1280,512]{1,0:T(8,128)} %refs_9_.1), custom_call_target="tpu_custom_call" | custom-call | tf_op jit(solution)/shard_map/pick_rows/pallas_call | solution.py:48
  20.3 1.3 %collective-permute-start.19 = (f32[32,512]{1,0:T(8,128)S(1)}, f32[32,512]{1,0:T(8,128)S(1)}, u32[]{:S(2)}, u32[]{:S(2)}) collective-permute-start(f32[32,512]{1,0:T(8,128)S(1)} %add_select_fusion.2), channel_id=1, source_target_pairs={{0,448},{16,464},{32,480},{48,496},{1,449},{17,465},{33,481},{49,4... | collective-permute-start | bytes 196616 | tf_op jit(solution)/shard_map/ppermute | solution.py:375
  21.6 1.3 %collective-permute-start.18 = (f32[32,512]{1,0:T(8,128)S(1)}, f32[32,512]{1,0:T(8,128)S(1)}, u32[]{:S(2)}, u32[]{:S(2)}) collective-permute-start(f32[32,512]{1,0:T(8,128)S(1)} %add_select_fusion.2), channel_id=1, source_target_pairs={{0,384},{16,400},{32,416},{48,432},{1,385},{17,401},{33,417},{49,4... | collective-permute-start | bytes 196616 | tf_op jit(solution)/shard_map/ppermute | solution.py:375
  22.9 1.3 %collective-permute-start.17 = (f32[32,512]{1,0:T(8,128)S(1)}, f32[32,512]{1,0:T(8,128)S(1)}, u32[]{:S(2)}, u32[]{:S(2)}) collective-permute-start(f32[32,512]{1,0:T(8,128)S(1)} %add_select_fusion.2), channel_id=1, source_target_pairs={{0,320},{16,336},{32,352},{48,368},{1,321},{17,337},{33,353},{49,3... | collective-permute-start | bytes 196616 | tf_op jit(solution)/shard_map/ppermute | solution.py:375
  24.2 1.3 %collective-permute-start.16 = (f32[32,512]{1,0:T(8,128)S(1)}, f32[32,512]{1,0:T(8,128)S(1)}, u32[]{:S(2)}, u32[]{:S(2)}) collective-permute-start(f32[32,512]{1,0:T(8,128)S(1)} %add_select_fusion.2), channel_id=1, source_target_pairs={{0,256},{16,272},{32,288},{48,304},{1,257},{17,273},{33,289},{49,3... | collective-permute-start | bytes 196616 | tf_op jit(solution)/shard_map/ppermute | solution.py:375
  25.5 1.3 %collective-permute-start.15 = (f32[32,512]{1,0:T(8,128)S(1)}, f32[32,512]{1,0:T(8,128)S(1)}, u32[]{:S(2)}, u32[]{:S(2)}) collective-permute-start(f32[32,512]{1,0:T(8,128)S(1)} %add_select_fusion.2), channel_id=1, source_target_pairs={{0,192},{16,208},{32,224},{48,240},{1,193},{17,209},{33,225},{49,2... | collective-permute-start | bytes 196616 | tf_op jit(solution)/shard_map/ppermute | solution.py:375
  26.8 1.3 %collective-permute-start.13 = (f32[32,512]{1,0:T(8,128)S(1)}, f32[32,512]{1,0:T(8,128)S(1)}, u32[]{:S(2)}, u32[]{:S(2)}) collective-permute-start(f32[32,512]{1,0:T(8,128)S(1)} %add_select_fusion.2), channel_id=1, source_target_pairs={{0,64},{16,80},{32,96},{48,112},{1,65},{17,81},{33,97},{49,113},{2... | collective-permute-start | bytes 196616 | tf_op jit(solution)/shard_map/ppermute | solution.py:375
  28.1 1.3 %collective-permute-start.14 = (f32[32,512]{1,0:T(8,128)S(1)}, f32[32,512]{1,0:T(8,128)S(1)}, u32[]{:S(2)}, u32[]{:S(2)}) collective-permute-start(f32[32,512]{1,0:T(8,128)S(1)} %add_select_fusion.2), channel_id=1, source_target_pairs={{0,128},{16,144},{32,160},{48,176},{1,129},{17,145},{33,161},{49,1... | collective-permute-start | bytes 196616 | tf_op jit(solution)/shard_map/ppermute | solution.py:375
  29.4 2.8 %tops_to_owners.1 = (f32[192,512]{1,0:T(8,128)}, f32[192,512]{1,0:T(8,128)}, f32[192,512]{1,0:T(8,128)}, f32[192,512]{1,0:T(8,128)}, f32[128,512]{1,0:T(8,128)}, /*index=5*/f32[128,512]{1,0:T(8,128)}) custom-call(s32[1]{0:T(128)} %bitcast.first_ref, s32[1,512]{1,0:T(1,128)S(1)} %bitcast.7, f32[1280,512]{1,0:T(8,128)S(1)} %copy-done), custom_call_target="tpu_custom_call" | custom-call | flops 20000000000 | tf_op jit(solution)/shard_map/tops_to_owners/pallas_call | solution.py:155
  33.0 5.3 %all-to-all-start = ((f32[32,16,128]{2,1,0:T(8,128)}), f32[32,16,128]{2,1,0:T(8,128)S(1)}, u32[]{:S(2)}, u32[]{:S(2)}) async-start(f32[32,16,128]{2,1,0:T(8,128)} %bitcast.5), calls=%async_computation | async-start | bytes 524288 | tf_op jit(solution)/shard_map/all_to_all | solution.py:388
  38.3 3.9 %collective-permute-start.3 = (f32[192,512]{1,0:T(8,128)}, f32[192,512]{1,0:T(8,128)}, u32[]{:S(2)}, u32[]{:S(2)}) collective-permute-start(f32[192,512]{1,0:T(8,128)} %get-tuple-element.32), channel_id=1, source_target_pairs={{0,16},{1,17},{2,18},{3,19},{4,20},{5,21},{6,22},{7,23},{8,24},{9,... | collective-permute-start | bytes 1179656 | tf_op jit(solution)/shard_map/ppermute | solution.py:383
  42.2 2.9 %collective-permute-start.4 = (f32[192,512]{1,0:T(8,128)}, f32[192,512]{1,0:T(8,128)}, u32[]{:S(2)}, u32[]{:S(2)}) collective-permute-start(f32[192,512]{1,0:T(8,128)} %get-tuple-element.33), channel_id=1, source_target_pairs={{0,32},{1,33},{2,34},{3,35},{4,36},{5,37},{6,38},{7,39},{8,40},{9,... | collective-permute-start | bytes 1179656 | tf_op jit(solution)/shard_map/ppermute | solution.py:383
  45.1 2.0 %collective-permute-start.5 = (f32[192,512]{1,0:T(8,128)}, f32[192,512]{1,0:T(8,128)}, u32[]{:S(2)}, u32[]{:S(2)}) collective-permute-start(f32[192,512]{1,0:T(8,128)} %get-tuple-element.34), channel_id=1, source_target_pairs={{0,48},{1,49},{2,50},{3,51},{4,52},{5,53},{6,54},{7,55},{8,56},{9,... | collective-permute-start | bytes 1179656 | tf_op jit(solution)/shard_map/ppermute | solution.py:383
  47.1 1.3 %collective-permute-start.6 = (f32[128,512]{1,0:T(8,128)}, f32[128,512]{1,0:T(8,128)S(1)}, u32[]{:S(2)}, u32[]{:S(2)}) collective-permute-start(f32[128,512]{1,0:T(8,128)} %get-tuple-element.35), channel_id=1, source_target_pairs={{0,384},{1,385},{2,386},{3,387},{4,388},{5,389},{6,390},{7,391},{8... | collective-permute-start | bytes 786440 | tf_op jit(solution)/shard_map/ppermute | solution.py:384
  48.4 2.0 %collective-permute-start.7 = (f32[128,512]{1,0:T(8,128)}, f32[128,512]{1,0:T(8,128)}, u32[]{:S(2)}, u32[]{:S(2)}) collective-permute-start(f32[128,512]{1,0:T(8,128)} %get-tuple-element.36), channel_id=1, source_target_pairs={{0,448},{1,449},{2,450},{3,451},{4,452},{5,453},{6,454},{7,455},{8... | collective-permute-start | bytes 786440 | tf_op jit(solution)/shard_map/ppermute | solution.py:384
  51.3 2.4 %slots_to_order.1 = f32[32,16,512]{2,1,0:T(8,128)} custom-call(s32[1,512]{1,0:T(1,128)} %bitcast.8, f32[32,16,128]{2,1,0:T(8,128)} %copy-done.3), custom_call_target="tpu_custom_call" | custom-call | tf_op jit(solution)/shard_map/slots_to_order/pallas_call | solution.py:109
  53.6 4.7 %all-to-all-start.1 = ((f32[32,16,512]{2,1,0:T(8,128)}), f32[32,16,512]{2,1,0:T(8,128)}, u32[]{:S(2)}, u32[]{:S(2)}) async-start(f32[32,16,512]{2,1,0:T(8,128)} %slots_to_order.1), calls=%async_computation.1 | async-start | bytes 2097152 | tf_op jit(solution)/shard_map/all_to_all | solution.py:392
  58.3 0.9 collective-permute-done.4
  59.2 1.0 add.115
  60.2 1.4 %add_select_fusion = f32[192,512]{1,0:T(8,128)S(1)} fusion(f32[192,512]{1,0:T(8,128)S(1)} %copy-done.5, f32[192,512]{1,0:T(8,128)} %collective-permute-done.5, f32[192,512]{1,0:T(8,128)} %collective-permute-done.3, f32[192,512]{1,0:T(8,128)} %collective-permute-done.4, pred[]{:T(512)S(6)} %eq.53), kind=kLoop, calls=%fused_computation.3 | loop fusion | flops 294912 | bytes 1966081 | tf_op jit(solution)/shard_map/jit(_where)/select_n | solution.py:394
  62.4 6.8 %collective-permute-start.8 = (f32[32,512]{1,0:T(8,128)}, f32[32,512]{1,0:T(8,128)}, u32[]{:S(2)}, u32[]{:S(2)}) collective-permute-start(f32[32,512]{1,0:T(8,128)} %get-tuple-element.58), channel_id=1, source_target_pairs={{0,256},{16,272},{32,288},{48,304},{1,257},{17,273},{33,289},{49,3... | collective-permute-start | bytes 196616 | tf_op jit(solution)/shard_map/ppermute | solution.py:399
  69.1 1.9 %collective-permute-start.9 = (f32[32,512]{1,0:T(8,128)}, f32[32,512]{1,0:T(8,128)}, u32[]{:S(2)}, u32[]{:S(2)}) collective-permute-start(f32[32,512]{1,0:T(8,128)} %get-tuple-element.55), channel_id=1, source_target_pairs={{0,192},{16,208},{32,224},{48,240},{384,432},{448,496},{1,193},{17... | collective-permute-start | bytes 196616 | tf_op jit(solution)/shard_map/ppermute | solution.py:399
  71.0 1.9 %collective-permute-start.10 = (f32[32,512]{1,0:T(8,128)}, f32[32,512]{1,0:T(8,128)}, u32[]{:S(2)}, u32[]{:S(2)}) collective-permute-start(f32[32,512]{1,0:T(8,128)} %get-tuple-element.54), channel_id=1, source_target_pairs={{0,128},{16,144},{32,160},{48,176},{384,416},{448,480},{1,129},{17... | collective-permute-start | bytes 196616 | tf_op jit(solution)/shard_map/ppermute | solution.py:399
  73.0 1.9 %collective-permute-start.11 = (f32[32,512]{1,0:T(8,128)}, f32[32,512]{1,0:T(8,128)}, u32[]{:S(2)}, u32[]{:S(2)}) collective-permute-start(f32[32,512]{1,0:T(8,128)} %get-tuple-element.53), channel_id=1, source_target_pairs={{0,64},{16,80},{32,96},{48,112},{384,400},{448,464},{1,65},{17,81}... | collective-permute-start | bytes 196616 | tf_op jit(solution)/shard_map/ppermute | solution.py:399
  74.8 1.9 %collective-permute-start.12 = (f32[32,512]{1,0:T(8,128)}, f32[32,512]{1,0:T(8,128)}, u32[]{:S(2)}, u32[]{:S(2)}) collective-permute-start(f32[32,512]{1,0:T(8,128)} %get-tuple-element.57), channel_id=1, source_target_pairs={{0,320},{16,336},{32,352},{48,368},{1,321},{17,337},{33,353},{49,3... | collective-permute-start | bytes 196616 | tf_op jit(solution)/shard_map/ppermute | solution.py:399
  76.8 2.8 %all-gather.2.cloned.1.call-done.full_ref = f32[512,1792]{1,0:T(8,128)} async-done(((f32[32,1792]{1,0:T(8,128)}), f32[512,1792]{1,0:T(8,128)}) %all-gather.2.cloned.1.call-update) | async-done | bytes 3670032 | tf_op jit(solution)/shard_map/all_gather | solution.py:381
  79.5 7.5 %factor.1 = (bf16[1024,512]{1,0:T(8,128)(2,1)}, bf16[1280,1024]{1,0:T(8,128)(2,1)}) custom-call(f32[512,1792]{1,0:T(8,128)} %all-gather.2.cloned.1.call-done.full_ref), custom_call_target="tpu_custom_call" | custom-call | flops 199999995904 | tf_op jit(solution)/shard_map/factor/pallas_call | solution.py:241
  87.1 7.2 %solve_update.1 = f32[1280,512]{1,0:T(8,128)} custom-call(s32[32]{0:T(128)S(1)} %copy-done.2, s32[2]{0:T(128)S(1)} %pad_add_fusion.flags_ref, f32[32,512]{1,0:T(8,128)S(1)} %get-tuple-element.56.refs_0_, f32[32,512]{1,0:T(8,128)} %collective-permute-done.8.refs_1_, f32[32,512]{1,0:T(8,128)} %collective-permute-done.9.refs_2_, ...), custom_call_target="tpu_custom_call" | custom-call | tf_op jit(solution)/shard_map/solve_update/pallas_call | solution.py:322
  (46 shorter events, 4.1 us)
Async XLA Ops:
  6.5 13.7 %copy-start.4 = (f32[1280,32]{0,1:T(8,128)S(1)}, f32[1280,32]{0,1:T(8,128)}, u32[]{:S(2)}) copy-start(f32[1280,32]{0,1:T(8,128)} %param.4) | copy-start | bytes 491524
  6.5 22.9 %copy-start = (f32[1280,512]{1,0:T(8,128)S(1)}, f32[1280,512]{1,0:T(8,128)}, u32[]{:S(2)}) copy-start(f32[1280,512]{1,0:T(8,128)} %refs_9_.1) | copy-start | bytes 7864324
  6.5 73.0 %all-gather.2.cloned.1.call-start = ((), (), s32[]{:S(2)}) async-start(), calls=%async_computation.2 | async-start | bytes 3899392 | tf_op jit(solution)/shard_map/all_gather | solution.py:381
  7.5 12.7 %collective-permute-start.2 = (f32[32,512]{1,0:T(8,128)S(1)}, f32[32,512]{1,0:T(8,128)S(1)}, u32[]{:S(2)}, u32[]{:S(2)}) collective-permute-start(f32[32,512]{1,0:T(8,128)S(1)} %slice.54), channel_id=1, source_target_pairs={{0,48},{1,49},{2,50},{3,51},{4,52},{5,53},{6,54},{7,55},{8,56},{9,... | collective-permute-start | bytes 196616 | tf_op jit(solution)/shard_map/ppermute | solution.py:371
  12.7 7.5 %collective-permute-start = (f32[32,512]{1,0:T(8,128)S(1)}, f32[32,512]{1,0:T(8,128)S(1)}, u32[]{:S(2)}, u32[]{:S(2)}) collective-permute-start(f32[32,512]{1,0:T(8,128)S(1)} %slice.54), channel_id=1, source_target_pairs={{0,16},{1,17},{2,18},{3,19},{4,20},{5,21},{6,22},{7,23},{8,24},{9,... | collective-permute-start | bytes 196616 | tf_op jit(solution)/shard_map/ppermute | solution.py:371
  14.0 6.2 %collective-permute-start.1 = (f32[32,512]{1,0:T(8,128)S(1)}, f32[32,512]{1,0:T(8,128)S(1)}, u32[]{:S(2)}, u32[]{:S(2)}) collective-permute-start(f32[32,512]{1,0:T(8,128)S(1)} %slice.54), channel_id=1, source_target_pairs={{0,32},{1,33},{2,34},{3,35},{4,36},{5,37},{6,38},{7,39},{8,40},{9,... | collective-permute-start | bytes 196616 | tf_op jit(solution)/shard_map/ppermute | solution.py:371
  16.3 15.8 %copy-start.1 = (s32[512]{0:T(512)}, s32[512]{0:T(512)S(1)}, u32[]{:S(2)}) copy-start(s32[512]{0:T(512)S(1)} %fusion.5) | copy-start | bytes 6148
  20.3 6.5 %collective-permute-start.19 = (f32[32,512]{1,0:T(8,128)S(1)}, f32[32,512]{1,0:T(8,128)S(1)}, u32[]{:S(2)}, u32[]{:S(2)}) collective-permute-start(f32[32,512]{1,0:T(8,128)S(1)} %add_select_fusion.2), channel_id=1, source_target_pairs={{0,448},{16,464},{32,480},{48,496},{1,449},{17,465},{33,481},{49,4... | collective-permute-start | bytes 196616 | tf_op jit(solution)/shard_map/ppermute | solution.py:375
  21.6 6.5 %collective-permute-start.18 = (f32[32,512]{1,0:T(8,128)S(1)}, f32[32,512]{1,0:T(8,128)S(1)}, u32[]{:S(2)}, u32[]{:S(2)}) collective-permute-start(f32[32,512]{1,0:T(8,128)S(1)} %add_select_fusion.2), channel_id=1, source_target_pairs={{0,384},{16,400},{32,416},{48,432},{1,385},{17,401},{33,417},{49,4... | collective-permute-start | bytes 196616 | tf_op jit(solution)/shard_map/ppermute | solution.py:375
  22.9 9.3 %collective-permute-start.17 = (f32[32,512]{1,0:T(8,128)S(1)}, f32[32,512]{1,0:T(8,128)S(1)}, u32[]{:S(2)}, u32[]{:S(2)}) collective-permute-start(f32[32,512]{1,0:T(8,128)S(1)} %add_select_fusion.2), channel_id=1, source_target_pairs={{0,320},{16,336},{32,352},{48,368},{1,321},{17,337},{33,353},{49,3... | collective-permute-start | bytes 196616 | tf_op jit(solution)/shard_map/ppermute | solution.py:375
  24.2 8.0 %collective-permute-start.16 = (f32[32,512]{1,0:T(8,128)S(1)}, f32[32,512]{1,0:T(8,128)S(1)}, u32[]{:S(2)}, u32[]{:S(2)}) collective-permute-start(f32[32,512]{1,0:T(8,128)S(1)} %add_select_fusion.2), channel_id=1, source_target_pairs={{0,256},{16,272},{32,288},{48,304},{1,257},{17,273},{33,289},{49,3... | collective-permute-start | bytes 196616 | tf_op jit(solution)/shard_map/ppermute | solution.py:375
  25.5 6.7 %collective-permute-start.15 = (f32[32,512]{1,0:T(8,128)S(1)}, f32[32,512]{1,0:T(8,128)S(1)}, u32[]{:S(2)}, u32[]{:S(2)}) collective-permute-start(f32[32,512]{1,0:T(8,128)S(1)} %add_select_fusion.2), channel_id=1, source_target_pairs={{0,192},{16,208},{32,224},{48,240},{1,193},{17,209},{33,225},{49,2... | collective-permute-start | bytes 196616 | tf_op jit(solution)/shard_map/ppermute | solution.py:375
  26.8 5.4 %collective-permute-start.13 = (f32[32,512]{1,0:T(8,128)S(1)}, f32[32,512]{1,0:T(8,128)S(1)}, u32[]{:S(2)}, u32[]{:S(2)}) collective-permute-start(f32[32,512]{1,0:T(8,128)S(1)} %add_select_fusion.2), channel_id=1, source_target_pairs={{0,64},{16,80},{32,96},{48,112},{1,65},{17,81},{33,97},{49,113},{2... | collective-permute-start | bytes 196616 | tf_op jit(solution)/shard_map/ppermute | solution.py:375
  28.1 4.1 %collective-permute-start.14 = (f32[32,512]{1,0:T(8,128)S(1)}, f32[32,512]{1,0:T(8,128)S(1)}, u32[]{:S(2)}, u32[]{:S(2)}) collective-permute-start(f32[32,512]{1,0:T(8,128)S(1)} %add_select_fusion.2), channel_id=1, source_target_pairs={{0,128},{16,144},{32,160},{48,176},{1,129},{17,145},{33,161},{49,1... | collective-permute-start | bytes 196616 | tf_op jit(solution)/shard_map/ppermute | solution.py:375
  32.3 27.9 %copy-start.5 = (f32[192,512]{1,0:T(8,128)S(1)}, f32[192,512]{1,0:T(8,128)}, u32[]{:S(2)}) copy-start(f32[192,512]{1,0:T(8,128)} %get-tuple-element.31) | copy-start | bytes 1179652
  33.0 17.5 %all-to-all-start = ((f32[32,16,128]{2,1,0:T(8,128)}), f32[32,16,128]{2,1,0:T(8,128)S(1)}, u32[]{:S(2)}, u32[]{:S(2)}) async-start(f32[32,16,128]{2,1,0:T(8,128)} %bitcast.5), calls=%async_computation | async-start | bytes 524288 | tf_op jit(solution)/shard_map/all_to_all | solution.py:388
  38.3 20.0 %collective-permute-start.3 = (f32[192,512]{1,0:T(8,128)}, f32[192,512]{1,0:T(8,128)}, u32[]{:S(2)}, u32[]{:S(2)}) collective-permute-start(f32[192,512]{1,0:T(8,128)} %get-tuple-element.32), channel_id=1, source_target_pairs={{0,16},{1,17},{2,18},{3,19},{4,20},{5,21},{6,22},{7,23},{8,24},{9,... | collective-permute-start | bytes 1179656 | tf_op jit(solution)/shard_map/ppermute | solution.py:383
  42.2 17.0 %collective-permute-start.4 = (f32[192,512]{1,0:T(8,128)}, f32[192,512]{1,0:T(8,128)}, u32[]{:S(2)}, u32[]{:S(2)}) collective-permute-start(f32[192,512]{1,0:T(8,128)} %get-tuple-element.33), channel_id=1, source_target_pairs={{0,32},{1,33},{2,34},{3,35},{4,36},{5,37},{6,38},{7,39},{8,40},{9,... | collective-permute-start | bytes 1179656 | tf_op jit(solution)/shard_map/ppermute | solution.py:383
  45.1 14.1 %collective-permute-start.5 = (f32[192,512]{1,0:T(8,128)}, f32[192,512]{1,0:T(8,128)}, u32[]{:S(2)}, u32[]{:S(2)}) collective-permute-start(f32[192,512]{1,0:T(8,128)} %get-tuple-element.34), channel_id=1, source_target_pairs={{0,48},{1,49},{2,50},{3,51},{4,52},{5,53},{6,54},{7,55},{8,56},{9,... | collective-permute-start | bytes 1179656 | tf_op jit(solution)/shard_map/ppermute | solution.py:383
  47.1 11.2 %collective-permute-start.6 = (f32[128,512]{1,0:T(8,128)}, f32[128,512]{1,0:T(8,128)S(1)}, u32[]{:S(2)}, u32[]{:S(2)}) collective-permute-start(f32[128,512]{1,0:T(8,128)} %get-tuple-element.35), channel_id=1, source_target_pairs={{0,384},{1,385},{2,386},{3,387},{4,388},{5,389},{6,390},{7,391},{8... | collective-permute-start | bytes 786440 | tf_op jit(solution)/shard_map/ppermute | solution.py:384
  48.4 9.9 %collective-permute-start.7 = (f32[128,512]{1,0:T(8,128)}, f32[128,512]{1,0:T(8,128)}, u32[]{:S(2)}, u32[]{:S(2)}) collective-permute-start(f32[128,512]{1,0:T(8,128)} %get-tuple-element.36), channel_id=1, source_target_pairs={{0,448},{1,449},{2,450},{3,451},{4,452},{5,453},{6,454},{7,455},{8... | collective-permute-start | bytes 786440 | tf_op jit(solution)/shard_map/ppermute | solution.py:384
  50.5 0.7 copy-start.3
  53.6 33.5 %all-to-all-start.1 = ((f32[32,16,512]{2,1,0:T(8,128)}), f32[32,16,512]{2,1,0:T(8,128)}, u32[]{:S(2)}, u32[]{:S(2)}) async-start(f32[32,16,512]{2,1,0:T(8,128)} %slots_to_order.1), calls=%async_computation.1 | async-start | bytes 2097152 | tf_op jit(solution)/shard_map/all_to_all | solution.py:392
  62.4 24.7 %collective-permute-start.8 = (f32[32,512]{1,0:T(8,128)}, f32[32,512]{1,0:T(8,128)}, u32[]{:S(2)}, u32[]{:S(2)}) collective-permute-start(f32[32,512]{1,0:T(8,128)} %get-tuple-element.58), channel_id=1, source_target_pairs={{0,256},{16,272},{32,288},{48,304},{1,257},{17,273},{33,289},{49,3... | collective-permute-start | bytes 196616 | tf_op jit(solution)/shard_map/ppermute | solution.py:399
  69.1 17.9 %collective-permute-start.9 = (f32[32,512]{1,0:T(8,128)}, f32[32,512]{1,0:T(8,128)}, u32[]{:S(2)}, u32[]{:S(2)}) collective-permute-start(f32[32,512]{1,0:T(8,128)} %get-tuple-element.55), channel_id=1, source_target_pairs={{0,192},{16,208},{32,224},{48,240},{384,432},{448,496},{1,193},{17... | collective-permute-start | bytes 196616 | tf_op jit(solution)/shard_map/ppermute | solution.py:399
  71.0 16.0 %collective-permute-start.10 = (f32[32,512]{1,0:T(8,128)}, f32[32,512]{1,0:T(8,128)}, u32[]{:S(2)}, u32[]{:S(2)}) collective-permute-start(f32[32,512]{1,0:T(8,128)} %get-tuple-element.54), channel_id=1, source_target_pairs={{0,128},{16,144},{32,160},{48,176},{384,416},{448,480},{1,129},{17... | collective-permute-start | bytes 196616 | tf_op jit(solution)/shard_map/ppermute | solution.py:399
  73.0 14.1 %collective-permute-start.11 = (f32[32,512]{1,0:T(8,128)}, f32[32,512]{1,0:T(8,128)}, u32[]{:S(2)}, u32[]{:S(2)}) collective-permute-start(f32[32,512]{1,0:T(8,128)} %get-tuple-element.53), channel_id=1, source_target_pairs={{0,64},{16,80},{32,96},{48,112},{384,400},{448,464},{1,65},{17,81}... | collective-permute-start | bytes 196616 | tf_op jit(solution)/shard_map/ppermute | solution.py:399
  74.8 12.2 %collective-permute-start.12 = (f32[32,512]{1,0:T(8,128)}, f32[32,512]{1,0:T(8,128)}, u32[]{:S(2)}, u32[]{:S(2)}) collective-permute-start(f32[32,512]{1,0:T(8,128)} %get-tuple-element.57), channel_id=1, source_target_pairs={{0,320},{16,336},{32,352},{48,368},{1,321},{17,337},{33,353},{49,3... | collective-permute-start | bytes 196616 | tf_op jit(solution)/shard_map/ppermute | solution.py:399
  79.5 7.6 %copy-start.2 = (s32[32]{0:T(128)S(1)}, s32[32]{0:T(128)}, u32[]{:S(2)}) copy-start(s32[32]{0:T(128)} %broadcast_add_fusion.rows_ref) | copy-start | bytes 388
Sparse Core Ops, SparseCore 0:
  33.1 46.3 all-gather.1
